TPU v7x, 32 devices: a whole 2x2x4 slice. The times are simulated.
32 devices in a mesh: section: 2 (over core), dp: 4 (over z), seq: 4 (over y, x).
Axes of the slice: x: 2, y: 2, z: 4, core: 2. Of those that a mesh axis runs over, the one named last changes fastest.
Arguments:
- tokens: bfloat16 [2, 4, 1024, 1024], P(None, 'dp', 'seq'), may hold values from -6 to 6
- cotangent: bfloat16 [2, 4, 1024, 1024], P(None, 'dp', 'seq'), may hold values from -6 to 6
- lengths: int32 [2, 4], P(None, 'dp'), may hold values from 128 to 1024, as said below
- norm_gain: float32 [2, 2, 1024], P('section'), may hold values from 0.5 to 1.5
- norm_bias: float32 [2, 2, 1024], P('section'), may hold values from -1.75 to 1.75
- mixer_in: bfloat16 [2, 1024, 3072], P('section', ('dp', 'seq')), may hold values from -0.1875 to 0.1875
- short_kernel: float32 [2, 3, 3072], P('section'), may hold values from -3.5 to 3.5
- filter_first: float32 [2, 33, 64], P('section'), may hold values from -16 to 16
- filter_second: float32 [2, 64, 64], P('section'), may hold values from -6 to 6
- filter_last: float32 [2, 64, 1024], P('section'), may hold values from -0.0625 to 0.0625
- filter_bias: float32 [2, 1024], P('section'), may hold values from -1.75 to 1.75
- decay_rates: float32 [2, 1024], P('section'), may hold values from 0.00024414062 to 0.0234375
- mixer_out: bfloat16 [2, 1024, 1024], P('section', ('dp', 'seq')), may hold values from -0.1875 to 0.1875
- up_weight: bfloat16 [2, 1024, 4096], P('section', ('dp', 'seq')), may hold values from -0.1875 to 0.1875
- down_weight: bfloat16 [2, 4096, 1024], P('section', ('dp', 'seq')), may hold values from -0.09375 to 0.09375
Outputs:
- block_outputs: float32 [2, 2, 4, 1024, 1024], P('section', None, 'dp', 'seq')
- input_grads: float32 [2, 2, 4, 1024, 1024], P('section', None, 'dp', 'seq')
- grad_norm_gain: float32 [2, 2, 1024], P('section')
- grad_norm_bias: float32 [2, 2, 1024], P('section')
- grad_mixer_in: float32 [2, 1024, 3072], P('section', ('dp', 'seq'))
- grad_short_kernel: float32 [2, 3, 3072], P('section')
- grad_filter_first: float32 [2, 33, 64], P('section')
- grad_filter_second: float32 [2, 64, 64], P('section')
- grad_filter_last: float32 [2, 64, 1024], P('section')
- grad_filter_bias: float32 [2, 1024], P('section')
- grad_mixer_out: float32 [2, 1024, 1024], P('section', ('dp', 'seq'))
- grad_up_weight: float32 [2, 1024, 4096], P('section', ('dp', 'seq'))
- grad_down_weight: float32 [2, 4096, 1024], P('section', ('dp', 'seq'))
Inputs may be any that keep to these rules, and one draw needn't show every extreme that they name: `lengths`: each row's length is at least 128; for every dp index, one of the 2 micro-batches holds a row of full length 1024.
All inputs are finite; a program needn't handle non-finite values.
Results may differ from a plain program's by a relative error of at most 0.028.
Values may be sent and summed in bfloat16 or wider, within the bound.
A program may use at most 384 MiB of HBM per device.

v0:
```python
from functools import partial
import math

import jax
import jax.numpy as jnp
from jax import lax
from jax.sharding import PartitionSpec as P

precise = lax.Precision.HIGHEST


def passed_along(block, axis, distance):
    devices = range(lax.axis_size(axis))
    route = [(i - distance, i) for i in devices if i - distance in devices]
    return lax.ppermute(block, axis, route)


def norm_rows(values, gain, shift):
    average = jnp.mean(values, axis=-1, keepdims=True)
    centred = values - average
    variance = jnp.mean(centred * centred, axis=-1, keepdims=True)
    return centred * lax.rsqrt(variance + 1e-05) * gain + shift


def position_table(length):
    offsets = jnp.arange(length, dtype=jnp.float32)
    frequencies = jnp.linspace(0.0001, 15.0, 16, dtype=jnp.float32)
    angles = 2.0 * math.pi * offsets[:, None] * frequencies[None, :] / length
    return jnp.concatenate(
        [offsets[:, None] / (length - 1), jnp.cos(angles), -jnp.sin(angles)], axis=1
    )


def filter_taps(first_w, second_w, last_w, rates, length):
    embedding = position_table(length)
    hidden = jnp.sin(
        jnp.dot(embedding, first_w, preferred_element_type=jnp.float32, precision=precise)
    )
    hidden = jnp.sin(
        jnp.dot(hidden, second_w, preferred_element_type=jnp.float32, precision=precise)
    )
    offsets = jnp.arange(length, dtype=jnp.float32)
    return jnp.dot(hidden, last_w, preferred_element_type=jnp.float32, precision=precise) * jnp.exp(
        -offsets[:, None] * rates[None, :]
    )


def square_table(count):
    indices = jnp.arange(count, dtype=jnp.int32)
    angles = (indices[:, None] * indices[None, :] % count).astype(jnp.float32) * (
        2.0 * math.pi / count
    )
    return (jnp.cos(angles), jnp.sin(angles))


def dft_tables(full_size):
    lead_size = math.gcd(full_size, 64)
    tail_size = full_size // lead_size
    lead_cos, lead_sin = square_table(lead_size)
    tail_cos, tail_sin = square_table(tail_size)
    twist_turns = (
        jnp.arange(lead_size, dtype=jnp.int32)[:, None]
        * jnp.arange(tail_size, dtype=jnp.int32)[None, :]
        % full_size
    )
    twist_angles = twist_turns.astype(jnp.float32) * (2.0 * math.pi / full_size)
    return (
        lead_size,
        tail_size,
        lead_cos,
        lead_sin,
        tail_cos,
        tail_sin,
        jnp.cos(twist_angles),
        jnp.sin(twist_angles),
    )


def to_spectrum(signal, tables):
    lead_size, tail_size, lead_cos, lead_sin, tail_cos, tail_sin, twist_cos, twist_sin = tables
    signal_grid = signal.reshape(signal.shape[0], lead_size, tail_size)
    part_re = jnp.einsum("kn,cnm->ckm", lead_cos, signal_grid, precision=precise)
    part_im = -jnp.einsum("kn,cnm->ckm", lead_sin, signal_grid, precision=precise)
    turned_re = part_re * twist_cos + part_im * twist_sin
    turned_im = part_im * twist_cos - part_re * twist_sin
    spec_re = jnp.einsum("ckn,nm->ckm", turned_re, tail_cos, precision=precise) + jnp.einsum(
        "ckn,nm->ckm", turned_im, tail_sin, precision=precise
    )
    spec_im = jnp.einsum("ckn,nm->ckm", turned_im, tail_cos, precision=precise) - jnp.einsum(
        "ckn,nm->ckm", turned_re, tail_sin, precision=precise
    )
    return (spec_re, spec_im)


def from_spectrum(spec_re, spec_im, tables, full_size):
    lead_size, tail_size, lead_cos, lead_sin, tail_cos, tail_sin, twist_cos, twist_sin = tables
    back_re = jnp.einsum("ckm,mn->ckn", spec_re, tail_cos, precision=precise) - jnp.einsum(
        "ckm,mn->ckn", spec_im, tail_sin, precision=precise
    )
    back_im = jnp.einsum("ckm,mn->ckn", spec_im, tail_cos, precision=precise) + jnp.einsum(
        "ckm,mn->ckn", spec_re, tail_sin, precision=precise
    )
    turned_re = back_re * twist_cos - back_im * twist_sin
    turned_im = back_im * twist_cos + back_re * twist_sin
    signal_grid = jnp.einsum("nk,ckm->cnm", lead_cos, turned_re, precision=precise) - jnp.einsum(
        "nk,ckm->cnm", lead_sin, turned_im, precision=precise
    )
    return signal_grid.reshape(spec_re.shape[0], full_size) / full_size


def long_conv(filter_rows, signal):
    length = signal.shape[1]
    full_size = 2 * length
    tables = dft_tables(full_size)
    padding = ((0, 0), (0, length))
    filt_re, filt_im = to_spectrum(jnp.pad(filter_rows, padding), tables)
    sig_re, sig_im = to_spectrum(jnp.pad(signal, padding), tables)
    convolved = from_spectrum(
        filt_re * sig_re - filt_im * sig_im, filt_re * sig_im + filt_im * sig_re, tables, full_size
    )
    return convolved[:, :length]


def short_apply(extended, kernel):
    return kernel[0] * extended[2:] + kernel[1] * extended[1:-1] + kernel[2] * extended[:-2]


def contract_rows(left, right):
    return jnp.einsum("tf,td->fd", left, right, preferred_element_type=jnp.float32)


def times_transpose(left, right):
    return jnp.einsum("tf,df->td", left, right, preferred_element_type=jnp.float32)


def rounded(values):
    return values.astype(jnp.bfloat16).astype(jnp.float32)


def per_device(
    tokens,
    cotangent,
    lengths,
    norm_gain,
    norm_bias,
    mixer_in,
    short_kernel,
    filter_first,
    filter_second,
    filter_last,
    filter_bias,
    decay_rates,
    mixer_out,
    up_weight,
    down_weight,
):
    section_first = lax.axis_index("section") == 0
    seq_index = lax.axis_index("seq")
    seq_count = lax.axis_size("seq")
    micro_count = tokens.shape[0]
    local_len = tokens.shape[2]
    model_width = tokens.shape[3]
    row_len = local_len * seq_count
    chan_count = model_width // seq_count
    chan_start = seq_index * chan_count
    whole_in, whole_out, whole_up, whole_down = (
        lax.all_gather(mixer_in, ("dp", "seq"), axis=1, tiled=True),
        lax.all_gather(mixer_out, ("dp", "seq"), axis=1, tiled=True),
        lax.all_gather(up_weight, ("dp", "seq"), axis=1, tiled=True),
        lax.all_gather(down_weight, ("dp", "seq"), axis=1, tiled=True),
    )
    weight_in = whole_in[0]
    weight_out = whole_out[0]
    weight_up = whole_up[0]
    weight_down = whole_down[0]
    norm_gains = norm_gain[0]
    biases = norm_bias[0]
    kernel = short_kernel[0]
    first_layer = filter_first[0]
    second_layer = filter_second[0]
    last_mine = lax.dynamic_slice_in_dim(filter_last[0], chan_start, chan_count, 1)
    bias_mine = lax.dynamic_slice_in_dim(filter_bias[0], chan_start, chan_count, 0)
    rates_mine = lax.dynamic_slice_in_dim(decay_rates[0], chan_start, chan_count, 0)
    positions = seq_index * local_len + jnp.arange(local_len)

    def conv_apply(product_chan, first_w, second_w, last_w, bias_part):
        filter_rows = jnp.transpose(filter_taps(first_w, second_w, last_w, rates_mine, row_len))
        return long_conv(filter_rows, product_chan) + bias_part[:, None] * product_chan

    def channel_gate(streams):
        product_chan = rounded(streams[0] * streams[2])
        return streams[1] * conv_apply(
            product_chan, first_layer, second_layer, last_mine, bias_mine
        )

    def layer_forward(inputs, row_mask):
        normed_low = norm_rows(inputs, norm_gains[0], biases[0]).astype(jnp.bfloat16)
        projected = jnp.dot(normed_low, weight_in, preferred_element_type=jnp.float32)
        prev_rows = passed_along(projected[-2:], "seq", 1)
        mixed_low = short_apply(jnp.concatenate([prev_rows, projected], 0), kernel).astype(
            jnp.bfloat16
        )
        arranged = jnp.transpose(mixed_low.reshape(local_len, 3, model_width), (1, 2, 0))
        chan_data = lax.all_to_all(arranged, "seq", split_axis=1, concat_axis=2, tiled=True)
        gated_low = channel_gate(chan_data.astype(jnp.float32)).astype(jnp.bfloat16)
        tok_data = jnp.transpose(
            lax.all_to_all(gated_low, "seq", split_axis=1, concat_axis=0, tiled=True)
        )
        branch = jnp.dot(tok_data, weight_out, preferred_element_type=jnp.float32)
        middle = inputs + row_mask * branch
        second_low = norm_rows(middle, norm_gains[1], biases[1]).astype(jnp.bfloat16)
        hidden_pre = jnp.dot(second_low, weight_up, preferred_element_type=jnp.float32)
        hidden_low = jax.nn.gelu(hidden_pre, approximate=True).astype(jnp.bfloat16)
        result = middle + row_mask * jnp.dot(
            hidden_low, weight_down, preferred_element_type=jnp.float32
        )
        return (
            result,
            (
                normed_low,
                projected,
                prev_rows,
                chan_data,
                tok_data,
                mixed_low,
                middle,
                second_low,
                hidden_pre,
                hidden_low,
                tok_data,
            ),
        )

    received = jnp.zeros((local_len, model_width), jnp.float32)
    saved_inputs = []
    saved_masks = []
    kept_mixer = []
    results = []
    for position in range(micro_count + 1):
        own_input = tokens[min(position, micro_count - 1), 0].astype(jnp.float32)
        layer_input = jnp.where(section_first, own_input, received)
        length_now = jnp.where(
            section_first,
            lengths[min(position, micro_count - 1), 0],
            lengths[max(position - 1, 0), 0],
        )
        row_mask = (positions < length_now).astype(jnp.float32)[:, None]
        result, saved = layer_forward(layer_input, row_mask)
        saved_inputs.append(layer_input)
        saved_masks.append(row_mask)
        kept_mixer.append((saved[2], saved[3], saved[4]))
        results.append(result)
        if position < micro_count:
            received = passed_along(result.astype(jnp.bfloat16), "section", 1).astype(result.dtype)
    received_grad = jnp.zeros((local_len, model_width), jnp.float32)
    accum = None
    factor_list = []
    grad_list = []
    for position in range(micro_count + 1):
        index_late = min(position, micro_count - 1)
        index_early = max(position - 1, 0)
        layer_input = jnp.where(
            section_first, saved_inputs[index_early], saved_inputs[index_late + 1]
        )
        row_mask = jnp.where(section_first, saved_masks[index_early], saved_masks[index_late + 1])
        out_grad = jnp.where(
            section_first, received_grad, cotangent[index_late, 0].astype(jnp.float32)
        )
        valid_now = jnp.where(section_first, position >= 1, position < micro_count)
        out_grad = out_grad * valid_now.astype(jnp.float32)
        saved = layer_forward(layer_input, row_mask)[1]
        (
            layer_normed_low,
            layer_projected,
            layer_prev_rows,
            layer_chan_data,
            layer_tok_data,
            layer_mixed_low,
            layer_middle,
            layer_second_low,
            layer_hidden_pre,
            layer_hidden_low,
            layer_gated_tok,
        ) = saved
        out_low = (out_grad * row_mask).astype(jnp.bfloat16)
        hidden_grad = times_transpose(out_low, weight_down)
        gelu_back = jax.vjp(partial(jax.nn.gelu, approximate=True), layer_hidden_pre)[1]
        pre_low = gelu_back(hidden_grad)[0].astype(jnp.bfloat16)
        norm_late = jax.vjp(norm_rows, layer_middle, norm_gains[1], biases[1])[1]
        mid_part, gain_late, bias_late = norm_late(times_transpose(pre_low, weight_up))
        middle_grad = out_grad + mid_part
        branch_low = (middle_grad * row_mask).astype(jnp.bfloat16)
        gated_grad = times_transpose(branch_low, weight_out).astype(jnp.bfloat16)
        gated_chan = lax.all_to_all(
            jnp.transpose(gated_grad), "seq", split_axis=0, concat_axis=1, tiled=True
        ).astype(jnp.float32)
        layer_streams = layer_chan_data.astype(jnp.float32)
        layer_product_chan = rounded(layer_streams[0] * layer_streams[2])
        filtered_chan, conv_back = jax.vjp(
            conv_apply, layer_product_chan, first_layer, second_layer, last_mine, bias_mine
        )
        filtered_grad = rounded(gated_chan * layer_streams[1])
        product_grad, grad_first, grad_second, grad_last, grad_bias = conv_back(filtered_grad)
        product_grad = rounded(product_grad)
        stream_grads = jnp.stack(
            [
                product_grad * layer_streams[2],
                gated_chan * filtered_chan,
                product_grad * layer_streams[0],
            ]
        ).astype(jnp.bfloat16)
        token_grads = lax.all_to_all(stream_grads, "seq", split_axis=2, concat_axis=1, tiled=True)
        mixed_grad_low = jnp.transpose(token_grads, (2, 0, 1)).reshape(local_len, 3 * model_width)
        next_rows = passed_along(mixed_grad_low[:2], "seq", -1)
        mixed_grad = mixed_grad_low.astype(jnp.float32)
        extended = jnp.concatenate([mixed_grad, next_rows.astype(jnp.float32)], 0)
        proj_low = (
            kernel[0] * extended[:-2] + kernel[1] * extended[1:-1] + kernel[2] * extended[2:]
        ).astype(jnp.bfloat16)
        earlier = jnp.concatenate([layer_prev_rows, layer_projected], 0)
        grad_kernel = jnp.stack(
            [
                jnp.sum(mixed_grad * earlier[2:], 0),
                jnp.sum(mixed_grad * earlier[1:-1], 0),
                jnp.sum(mixed_grad * earlier[:-2], 0),
            ]
        )
        norm_early = jax.vjp(norm_rows, layer_input, norm_gains[0], biases[0])[1]
        input_part, gain_early, bias_early = norm_early(times_transpose(proj_low, weight_in))
        small = (
            jnp.stack([gain_early, gain_late]),
            jnp.stack([bias_early, bias_late]),
            grad_kernel,
            grad_first,
            grad_second,
            grad_last,
            grad_bias,
        )
        factors = (
            layer_normed_low,
            proj_low,
            layer_gated_tok,
            branch_low,
            layer_second_low,
            pre_low,
            layer_hidden_low,
            out_low,
        )
        input_grad, small, factors = (middle_grad + input_part, small, factors)
        accum = small if accum is None else jax.tree.map(jnp.add, accum, small)
        factor_list.append(factors)
        grad_list.append(input_grad)
        if position < micro_count:
            received_grad = passed_along(input_grad.astype(jnp.bfloat16), "section", -1).astype(
                input_grad.dtype
            )
    joined = [jnp.concatenate([item[slot] for item in factor_list], 0) for slot in range(8)]
    acc_in = contract_rows(joined[0], joined[1])
    acc_out = contract_rows(joined[2], joined[3])
    acc_up = contract_rows(joined[4], joined[5])
    acc_down = contract_rows(joined[6], joined[7])
    acc_gain, acc_bias, acc_kernel, acc_first, acc_second, acc_last, acc_direct = accum
    full_last = lax.dynamic_update_slice_in_dim(
        jnp.zeros((acc_last.shape[0], model_width), jnp.float32), acc_last, chan_start, 1
    )
    full_direct = lax.dynamic_update_slice_in_dim(
        jnp.zeros((model_width,), jnp.float32), acc_direct, chan_start, 0
    )
    sum_in, sum_out, sum_up, sum_down = (
        lax.psum_scatter(acc_in, ("dp", "seq"), scatter_dimension=0, tiled=True),
        lax.psum_scatter(acc_out, ("dp", "seq"), scatter_dimension=0, tiled=True),
        lax.psum_scatter(acc_up, ("dp", "seq"), scatter_dimension=0, tiled=True),
        lax.psum_scatter(acc_down, ("dp", "seq"), scatter_dimension=0, tiled=True),
    )
    sum_gain, sum_bias, sum_kernel, sum_first, sum_second, sum_last, sum_direct = lax.psum(
        (acc_gain, acc_bias, acc_kernel, acc_first, acc_second, full_last, full_direct),
        ("dp", "seq"),
    )
    block_outputs = jnp.stack(
        [
            jnp.where(section_first, results[index], results[index + 1])
            for index in range(micro_count)
        ]
    )
    input_grads = jnp.stack(
        [
            jnp.where(section_first, grad_list[index + 1], grad_list[index])
            for index in range(micro_count)
        ]
    )
    return (
        block_outputs[None, :, None],
        input_grads[None, :, None],
        sum_gain[None],
        sum_bias[None],
        sum_in[None],
        sum_kernel[None],
        sum_first[None],
        sum_second[None],
        sum_last[None],
        sum_direct[None],
        sum_out[None],
        sum_up[None],
        sum_down[None],
    )


def solution(mesh):
    in_specs = (
        P(None, "dp", "seq", None),
        P(None, "dp", "seq", None),
        P(None, "dp"),
        P("section", None, None),
        P("section", None, None),
        P("section", ("dp", "seq"), None),
        P("section", None, None),
        P("section", None, None),
        P("section", None, None),
        P("section", None, None),
        P("section", None),
        P("section", None),
        P("section", ("dp", "seq"), None),
        P("section", ("dp", "seq"), None),
        P("section", ("dp", "seq"), None),
    )
    out_specs = (
        P("section", None, "dp", "seq", None),
        P("section", None, "dp", "seq", None),
        P("section", None, None),
        P("section", None, None),
        P("section", ("dp", "seq"), None),
        P("section", None, None),
        P("section", None, None),
        P("section", None, None),
        P("section", None, None),
        P("section", None),
        P("section", ("dp", "seq"), None),
        P("section", ("dp", "seq"), None),
        P("section", ("dp", "seq"), None),
    )
    return jax.shard_map(
        per_device, mesh=mesh, in_specs=in_specs, out_specs=out_specs, check_vma=False
    )
```

profile of v0, /device:TPU:0, one launch (start us, length us, event | category | flops | bytes accessed | tf_op | source)
XLA Modules:
  0.0 2763.7 jit_solution(13512101610588521571)
XLA Ops:
  18.6 89.2 %all-gather.5.cloned.1.call-done = bf16[1,1024,3072]{2,1,0:T(8,128)(2,1)} async-done(((bf16[1,64,3072]{2,1,0:T(8,128)(2,1)}), bf16[1,1024,3072]{2,1,0:T(8,128)(2,1)}) %all-gather.5.cloned.1.call-update) | async-done | bytes 6291472 | tf_op jit(solution)/shard_map/all_gather | solution.py:167
  246.4 42.2 %all-gather.11.cloned.1.call-done = bf16[1,4096,1024]{2,1,0:T(8,128)(2,1)} async-done(((bf16[1,256,1024]{2,1,0:T(8,128)(2,1)}), bf16[1,4096,1024]{2,1,0:T(8,128)(2,1)}) %all-gather.11.cloned.1.call-update) | async-done | bytes 8388624 | tf_op jit(solution)/shard_map/all_gather | solution.py:170
  288.7 113.3 %all-gather.9.cloned.1.call-done = bf16[1,1024,4096]{2,1,0:T(8,128)(2,1)} async-done(((bf16[1,64,4096]{2,1,0:T(8,128)(2,1)}), bf16[1,1024,4096]{2,1,0:T(8,128)(2,1)}) %all-gather.9.cloned.1.call-update) | async-done | bytes 8388624 | tf_op jit(solution)/shard_map/all_gather | solution.py:169
  402.0 12.4 fusion.1751
  457.9 16.3 all-to-all-done.2
  579.4 12.4 fusion.312
  648.4 12.3 fusion.622
  678.9 11.9 fusion.72
  906.1 19.8 all-to-all-done.9
  941.5 15.5 multiply_reduce_fusion.7
  1024.3 14.1 all-to-all-done.14
  1171.6 20.3 all-to-all-done.13
  1211.2 15.3 multiply_reduce_fusion.4
  1291.6 17.5 all-to-all-done.4
  1394.8 10.3 fusion.169
  1537.6 12.1 fusion.30
  1551.1 12.1 fusion.36
  1583.2 11.6 fusion.631
  1601.0 23.0 all-reduce.16.cloned.1.call-done
  1625.4 111.1 %all-reduce.14.cloned.1.call-done = f32[1,64,1024]{2,1,0:T(8,128)} async-done(((f32[1,64,1024]{2,1,0:T(8,128)}), f32[1,64,1024]{2,1,0:T(8,128)}) %all-reduce.14.cloned.1.call-update) | async-done | bytes 262160 | tf_op jit(solution)/shard_map/psum | solution.py:375
  1736.4 97.2 %reduce-scatter.7.cloned.1.call-done = f32[64,1024]{1,0:T(8,128)} async-done(((f32[1024,1024]{1,0:T(8,128)}), f32[64,1024]{1,0:T(8,128)}) %reduce-scatter.7.cloned.1.call-update) | async-done | bytes 262160 | tf_op jit(solution)/shard_map/reduce_scatter | solution.py:371
  1833.6 210.8 %reduce-scatter.5.cloned.1.call-done = f32[64,3072]{1,0:T(8,128)} async-done(((f32[1024,3072]{1,0:T(8,128)}), f32[64,3072]{1,0:T(8,128)}) %reduce-scatter.5.cloned.1.call-update) | async-done | bytes 786448 | tf_op jit(solution)/shard_map/reduce_scatter | solution.py:370
  2044.4 348.9 %reduce-scatter.9.cloned.1.call-done = f32[64,4096]{1,0:T(8,128)} async-done(((f32[1024,4096]{1,0:T(8,128)}), f32[64,4096]{1,0:T(8,128)}) %reduce-scatter.9.cloned.1.call-update) | async-done | bytes 1048592 | tf_op jit(solution)/shard_map/reduce_scatter | solution.py:372
  2393.3 354.8 %reduce-scatter.11.cloned.1.call-done = f32[256,1024]{1,0:T(8,128)} async-done(((f32[4096,1024]{1,0:T(8,128)}), f32[256,1024]{1,0:T(8,128)}) %reduce-scatter.11.cloned.1.call-update) | async-done | bytes 1048592 | tf_op jit(solution)/shard_map/reduce_scatter | solution.py:373
  (1032 shorter events, 1138.9 us)
Async XLA Ops:
  7.3 100.5 %all-gather.5.cloned.1.call-start = ((), (), s32[]{:S(2)}) async-start(), calls=%async_computation.22 | async-start | bytes 6684672 | tf_op jit(solution)/shard_map/all_gather | solution.py:167
  8.0 225.0 %all-gather.7.cloned.1.call-start = ((), (), s32[]{:S(2)}) async-start(), calls=%async_computation.23 | async-start | bytes 2228224 | tf_op jit(solution)/shard_map/all_gather | solution.py:168
  8.7 279.9 %all-gather.11.cloned.1.call-start = ((), (), s32[]{:S(2)}) async-start(), calls=%async_computation.25 | async-start | bytes 8912896 | tf_op jit(solution)/shard_map/all_gather | solution.py:170
  9.5 392.5 %all-gather.9.cloned.1.call-start = ((), (), s32[]{:S(2)}) async-start(), calls=%async_computation.24 | async-start | bytes 8912896 | tf_op jit(solution)/shard_map/all_gather | solution.py:169
  123.6 30.7 %all-to-all-start = ((bf16[3,1024,256]{2,0,1:T(4,128)(2,1)}), bf16[3,1024,256]{2,0,1:T(4,128)(2,1)S(1)}, u32[]{:S(2)}, u32[]{:S(2)}) async-start(bf16[3,1024,256]{2,0,1:T(4,128)(2,1)} %copy.429), calls=%async_computation | async-start | bytes 4194304 | tf_op jit(solution)/shard_map/all_to_all | solution.py:204
  444.8 29.4 %all-to-all-start.2 = ((bf16[3,1024,256]{2,0,1:T(4,128)(2,1)}), bf16[3,1024,256]{2,0,1:T(4,128)(2,1)}, u32[]{:S(2)}, u32[]{:S(2)}) async-start(bf16[3,1024,256]{2,0,1:T(4,128)(2,1)} %copy.471), calls=%async_computation.2 | async-start | bytes 4194304 | tf_op jit(solution)/shard_map/all_to_all | solution.py:204
  474.2 29.1 %all-to-all-start.6 = ((bf16[3,1024,256]{2,0,1:T(4,128)(2,1)}), bf16[3,1024,256]{2,0,1:T(4,128)(2,1)}, u32[]{:S(2)}, u32[]{:S(2)}) async-start(bf16[3,1024,256]{2,0,1:T(4,128)(2,1)} %copy.529), calls=%async_computation.6 | async-start | bytes 4194304 | tf_op jit(solution)/shard_map/all_to_all | solution.py:204
  640.4 25.7 all-to-all-start.7
  664.0 34.2 %collective-permute-start.3 = (bf16[256,1024]{1,0:T(8,128)(2,1)}, bf16[256,1024]{1,0:T(8,128)(2,1)}, u32[]{:S(2)}, u32[]{:S(2)}) collective-permute-start(bf16[256,1024]{1,0:T(8,128)(2,1)} %get-tuple-element.219), channel_id=1, source_target_pairs={{0,16},{1,17},{2,18},{3,19},{4,20},{5,21},{6,22},{7,23},{8,24},{9,... | collective-permute-start | bytes 1572872 | tf_op jit(solution)/shard_map/ppermute | solution.py:15
  707.0 33.7 %collective-permute-start.8 = (f32[2,3072]{1,0:T(2,128)}, f32[2,3072]{1,0:T(2,128)}, u32[]{:S(2)}, u32[]{:S(2)}) collective-permute-start(f32[2,3072]{1,0:T(2,128)} %slice.410), channel_id=1, source_target_pairs={{0,1},{1,2},{2,3},{4,5},{5,6},{6,7},{8,9},{9,10},{10,11},{12,13},{... | collective-permute-start | bytes 73736 | tf_op jit(solution)/shard_map/ppermute | solution.py:15
  714.2 36.0 %all-to-all-start.8 = ((bf16[4,256,256]{1,2,0:T(8,128)(2,1)}), bf16[4,256,256]{1,2,0:T(8,128)(2,1)}, u32[]{:S(2)}, u32[]{:S(2)}) async-start(bf16[4,256,256]{1,2,0:T(8,128)(2,1)} %bitcast.1435), calls=%async_computation.8 | async-start | bytes 1048576 | tf_op jit(solution)/shard_map/all_to_all | solution.py:294
  725.4 216.1 %collective-permute-start.11 = (f32[2,3072]{1,0:T(2,128)}, f32[2,3072]{1,0:T(2,128)}, u32[]{:S(2)}, u32[]{:S(2)}) collective-permute-start(f32[2,3072]{1,0:T(2,128)} %slice.420), channel_id=1, source_target_pairs={{0,1},{1,2},{2,3},{4,5},{5,6},{6,7},{8,9},{9,10},{10,11},{12,13},{... | collective-permute-start | bytes 73736 | tf_op jit(solution)/shard_map/ppermute | solution.py:15
  737.4 473.8 %collective-permute-start.4 = (f32[2,3072]{1,0:T(2,128)}, f32[2,3072]{1,0:T(2,128)}, u32[]{:S(2)}, u32[]{:S(2)}) collective-permute-start(f32[2,3072]{1,0:T(2,128)} %slice.393), channel_id=1, source_target_pairs={{0,1},{1,2},{2,3},{4,5},{5,6},{6,7},{8,9},{9,10},{10,11},{12,13},{... | collective-permute-start | bytes 73736 | tf_op jit(solution)/shard_map/ppermute | solution.py:15
  897.0 29.0 %all-to-all-start.9 = ((bf16[3,256,1024]{1,0,2:T(4,128)(2,1)}), bf16[3,256,1024]{1,0,2:T(4,128)(2,1)}, u32[]{:S(2)}, u32[]{:S(2)}) async-start(bf16[3,256,1024]{1,0,2:T(4,128)(2,1)} %copy.568), calls=%async_computation.9 | async-start | bytes 4194304 | tf_op jit(solution)/shard_map/all_to_all | solution.py:312
  1006.7 31.6 %all-to-all-start.14 = ((bf16[3,1024,256]{2,0,1:T(4,128)(2,1)}), bf16[3,1024,256]{2,0,1:T(4,128)(2,1)}, u32[]{:S(2)}, u32[]{:S(2)}) async-start(bf16[3,1024,256]{2,0,1:T(4,128)(2,1)} %copy.621), calls=%async_computation.14 | async-start | bytes 4194304 | tf_op jit(solution)/shard_map/all_to_all | solution.py:204
  1161.8 30.1 %all-to-all-start.13 = ((bf16[3,256,1024]{1,0,2:T(4,128)(2,1)}), bf16[3,256,1024]{1,0,2:T(4,128)(2,1)}, u32[]{:S(2)}, u32[]{:S(2)}) async-start(bf16[3,256,1024]{1,0,2:T(4,128)(2,1)} %copy.614), calls=%async_computation.13 | async-start | bytes 4194304 | tf_op jit(solution)/shard_map/all_to_all | solution.py:312
  1278.2 30.9 %all-to-all-start.4 = ((bf16[3,1024,256]{2,0,1:T(4,128)(2,1)}), bf16[3,1024,256]{2,0,1:T(4,128)(2,1)}, u32[]{:S(2)}, u32[]{:S(2)}) async-start(bf16[3,1024,256]{2,0,1:T(4,128)(2,1)} %copy.500), calls=%async_computation.4 | async-start | bytes 4194304 | tf_op jit(solution)/shard_map/all_to_all | solution.py:204
  1444.6 39.6 %all-to-all-start.17 = ((bf16[3,256,1024]{1,0,2:T(4,128)(2,1)}), bf16[3,256,1024]{1,0,2:T(4,128)(2,1)}, u32[]{:S(2)}, u32[]{:S(2)}) async-start(bf16[3,256,1024]{1,0,2:T(4,128)(2,1)} %copy.660), calls=%async_computation.17 | async-start | bytes 4194304 | tf_op jit(solution)/shard_map/all_to_all | solution.py:312
  1449.2 174.9 %all-reduce.16.cloned.1.call-start = ((), (), s32[]{:S(2)}) async-start(), calls=%async_computation.31 | async-start | bytes 221184 | tf_op jit(solution)/shard_map/psum | solution.py:375
  1516.5 220.0 %all-reduce.14.cloned.1.call-start = ((), (), s32[]{:S(2)}) async-start(), calls=%async_computation.27 | async-start | bytes 524288 | tf_op jit(solution)/shard_map/psum | solution.py:375
  1519.3 314.3 %reduce-scatter.7.cloned.1.call-start = ((), (), s32[]{:S(2)}) async-start(), calls=%async_computation.28 | async-start | bytes 4456448 | tf_op jit(solution)/shard_map/reduce_scatter | solution.py:371
  1524.8 519.6 %reduce-scatter.5.cloned.1.call-start = ((), (), s32[]{:S(2)}) async-start(), calls=%async_computation.26 | async-start | bytes 13369344 | tf_op jit(solution)/shard_map/reduce_scatter | solution.py:370
  1536.3 857.0 %reduce-scatter.9.cloned.1.call-start = ((), (), s32[]{:S(2)}) async-start(), calls=%async_computation.29 | async-start | bytes 17825792 | tf_op jit(solution)/shard_map/reduce_scatter | solution.py:372
  1549.7 1198.3 %reduce-scatter.11.cloned.1.call-start = ((), (), s32[]{:S(2)}) async-start(), calls=%async_computation.30 | async-start | bytes 17825792 | tf_op jit(solution)/shard_map/reduce_scatter | solution.py:373
  (284 other events, 2992.2 us)
Sparse Core Ops, SparseCore 0:
  10.9 96.8 all-gather.4
  110.5 61.6 all-gather.6
  175.0 113.6 all-gather.10
  291.3 110.6 all-gather.8
  1516.6 107.4 all-reduce.15
  1629.7 106.7 all-reduce.13
  1739.4 94.1 reduce-scatter.6
  1840.8 203.5 reduce-scatter.4
  2047.3 345.9 reduce-scatter.8
  2396.0 352.0 reduce-scatter.10
where the time goes:
time: 2780 us; the launch traced here: 2760 us
  waiting for transfers between devices  1530 us (55%)
  matrix products  749 us (27%)
  local copies, waits for them, and re-layouts  216 us (8%)
  other arithmetic  134 us (5%)
  starting transfers between devices  117 us (4%)
    reduce_scatter x1, waiting for transfers between devices, per_device(): lax.psum_scatter(acc_down, ('dp', 'seq'), scatter_dimension=0, tiled=True)  355 us
    reduce_scatter x1, waiting for transfers between devices, per_device(): lax.psum_scatter(acc_up, ('dp', 'seq'), scatter_dimension=0, tiled=True)  349 us
    reduce_scatter x1, waiting for transfers between devices, per_device(): lax.psum_scatter(acc_in, ('dp', 'seq'), scatter_dimension=0, tiled=True)  211 us
    psum x2, waiting for transfers between devices, per_device(): lax.psum((acc_gain, acc_bias, acc_kernel, acc_first, acc_second, full_las...  134 us
    all_gather x1, waiting for transfers between devices, per_device(): lax.all_gather(up_weight, ('dp', 'seq'), axis=1, tiled=True)  113 us
    reduce_scatter x1, waiting for transfers between devices, per_device(): lax.psum_scatter(acc_out, ('dp', 'seq'), scatter_dimension=0, tiled=True)  97.2 us
    all_gather x1, waiting for transfers between devices, per_device(): lax.all_gather(mixer_in, ('dp', 'seq'), axis=1, tiled=True)  89.2 us
    all_to_all x6, waiting for transfers between devices, layer_forward(): lax.all_to_all(arranged, 'seq', split_axis=1, concat_axis=2, tiled=True)  72 us
  transfers between devices with their start and end apart: 41, of which 23 were waited for; matrix products, arithmetic and copies ran while one was open for 25% of the time, Pallas kernels for 0%

commit v1 on v0

v1 whole, which is shorter than its diff:
```python
from functools import partial
import math

import jax
import jax.numpy as jnp
import numpy as np
from jax import lax
from jax.experimental import pallas as pl
from jax.experimental.pallas import tpu as pltpu
from jax.sharding import PartitionSpec as P

precise = lax.Precision.HIGHEST
low = jnp.bfloat16
f32 = jnp.float32
MESH = pl.DeviceIdType.MESH


def dot(a, b, dims):
    return lax.dot_general(a, b, (dims, ((), ())), preferred_element_type=f32)


def mm(a, b):
    return dot(a, b, ((1,), (0,)))


def mm_t(a, b):
    return dot(a, b, ((1,), (1,)))


def t_mm(a, b):
    return dot(a, b, ((0,), (0,)))


def norm_stats(x):
    mean = jnp.mean(x, axis=-1, keepdims=True)
    centred = x - mean
    inverse = lax.rsqrt(jnp.mean(centred * centred, axis=-1, keepdims=True) + 1e-05)
    return centred * inverse, inverse


def norm_back(grad, x, gain):
    hat, inverse = norm_stats(x)
    scaled = grad * gain
    back = inverse * (
        scaled
        - jnp.mean(scaled, axis=-1, keepdims=True)
        - hat * jnp.mean(scaled * hat, axis=-1, keepdims=True)
    )
    return back, jnp.sum(grad * hat, 0), jnp.sum(grad, 0)


def gelu_both(x):
    scale = math.sqrt(2.0 / math.pi)
    inner = scale * (x + 0.044715 * x * x * x)
    bend = jnp.tanh(inner)
    value = 0.5 * x * (1.0 + bend)
    slope = 0.5 * (1.0 + bend) + 0.5 * x * (1.0 - bend * bend) * scale * (
        1.0 + 3.0 * 0.044715 * x * x
    )
    return value, slope


def position_table(length):
    offsets = jnp.arange(length, dtype=jnp.float32)
    frequencies = jnp.linspace(0.0001, 15.0, 16, dtype=jnp.float32)
    angles = 2.0 * math.pi * offsets[:, None] * frequencies[None, :] / length
    return jnp.concatenate(
        [offsets[:, None] / (length - 1), jnp.cos(angles), -jnp.sin(angles)], axis=1
    )


def position_rows(length):
    offsets = np.arange(length, dtype=np.float32)
    frequencies = np.linspace(0.0001, 15.0, 16, dtype=np.float32)
    angles = np.float32(2.0 * math.pi) * offsets[:, None] * frequencies[None, :] / np.float32(length)
    return np.concatenate(
        [offsets[:, None] / np.float32(length - 1), np.cos(angles), -np.sin(angles)], axis=1
    )


def filter_taps(first_w, second_w, last_w, rates, length):
    embedding = position_table(length)
    hidden = jnp.sin(jnp.dot(embedding, first_w, precision=precise))
    hidden = jnp.sin(jnp.dot(hidden, second_w, precision=precise))
    offsets = jnp.arange(length, dtype=jnp.float32)
    return jnp.dot(hidden, last_w, precision=precise) * jnp.exp(-offsets[:, None] * rates[None, :])


def wave_tables(length):
    turns = (2 * np.arange(length)[:, None] + 1) * np.arange(length)[None, :] % (4 * length)
    angles = turns * (math.pi / (2 * length))
    both = np.concatenate([np.cos(angles), np.sin(angles)], 0)
    return both.astype(jnp.bfloat16)


def shifted(x, by):
    if by > 0:
        return jnp.pad(x[:-by], ((by, 0), (0, 0)))
    return jnp.pad(x[-by:], ((0, -by), (0, 0)))


def neighbours(me):
    return (me + 1 - 2 * (me % 2), (me + 2) % 4, 3 - me)


def greet(devices):
    barrier = pltpu.get_barrier_semaphore()
    for device in devices:
        pl.semaphore_signal(barrier, inc=1, device_id=device, device_id_type=MESH)
    return len(devices)


def all_here(greeted):
    pl.semaphore_wait(pltpu.get_barrier_semaphore(), greeted)


def in_plane(peers):
    return [{"seq": peer} for peer in peers]


def along_planes():
    here = lax.axis_index("dp")
    return here, here + 1 - 2 * (here % 2), (here + 2) % 4


def other_core():
    return {"section": 1 - lax.axis_index("section")}


def plane_devices():
    _, near, far = along_planes()
    return [{"dp": near}, {"dp": far}]


def add_low(target, source):
    def add(at):
        target[at, :] = (target[at, :].astype(f32) + source[at, :].astype(f32)).astype(low)

    by_rows(target.shape[0], 32, add)


def swap_begin(pairs, core_sems):
    section = lax.axis_index("section")
    copies = [
        remote_to(made.at[1 - section], other, core_sems, at, other_core())
        for at, (made, other) in enumerate(pairs)
    ]
    for copy in copies:
        copy.start()
    return copies


def swap_end(copies, pairs):
    section = lax.axis_index("section")
    for copy, (made, other) in zip(copies, pairs):
        copy.wait_recv()
        for block in range(other.shape[0]):
            add_low(made.at[section, block], other.at[block])


class PlaneSum:
    def __init__(self, pack, mine, arrived, sems, load_sems):
        self.here, self.near, self.far = along_planes()
        self.pack, self.mine, self.arrived = pack, mine, arrived
        self.sems, self.load_sems = sems, load_sems

    def begin(self):
        self.sends = [
            remote_to(self.pack.at[block], self.arrived.at[slot], self.sems, slot, {"dp": self.near})
            for slot, block in enumerate(((self.near + 2) % 4, self.near))
        ]
        for copy in self.sends:
            copy.start()
        self.loads = fetch(
            [(self.pack.at[self.far], self.mine.at[0]), (self.pack.at[self.here], self.mine.at[1])],
            self.load_sems,
        )

    def forward(self):
        self.loads[0].wait()
        self.sends[0].wait_recv()
        add_low(self.mine.at[0], self.arrived.at[0])
        copy = remote_to(self.mine.at[0], self.arrived.at[2], self.sems, 2, {"dp": self.far})
        copy.start()
        self.sends.append(copy)

    def end(self, result):
        self.loads[1].wait()
        self.sends[1].wait_recv()
        self.sends[2].wait_recv()

        def add(at):
            total = self.mine[1, at, :].astype(f32)
            for slot in (1, 2):
                total = total + self.arrived[slot, at, :].astype(f32)
            result[at, :] = total.astype(low)

        by_rows(result.shape[0], 32, add)


def plane_sum_scratch(half_pack):
    _, rows, cols = half_pack.shape
    return [
        pltpu.VMEM((2, rows, cols), low),
        pltpu.VMEM((3, rows, cols), low),
        pltpu.SemaphoreType.DMA((2, 3)),
        pltpu.SemaphoreType.DMA((2,)),
    ]


def remote_to(source, target, sems, slot, device):
    return pltpu.make_async_remote_copy(
        src_ref=source,
        dst_ref=target,
        send_sem=sems.at[0, slot],
        recv_sem=sems.at[1, slot],
        device_id=device,
        device_id_type=MESH,
    )


def remote(source, target, sems, slot, peer):
    return remote_to(source, target, sems, slot, {"seq": peer})


def rows_of(index, count):
    return pl.ds(pl.multiple_of(index * count, count), count)


def half_of(ref, index, part, count):
    half = count // 2
    return ref.at[pl.ds(pl.multiple_of(index * count + part * half, half), half)]


def gather_begin(gather, sems, me, peers, count):
    x, y, _ = peers
    first, second = half_of(gather, me, 0, count), half_of(gather, me, 1, count)
    copies = [
        remote(first, first, sems, 0, x),
        remote(second, second, sems, 2, y),
        remote(second, second, sems, 1, x),
        remote(first, first, sems, 3, y),
    ]
    for copy in copies:
        copy.start()
    return copies


def gather_forward(gather, sems, peers, count):
    x, y, _ = peers
    from_x, from_y = half_of(gather, x, 0, count), half_of(gather, y, 1, count)
    remote(from_x, from_x, sems, 0, x).wait_recv()
    onward = remote(from_x, from_x, sems, 4, y)
    onward.start()
    remote(from_y, from_y, sems, 2, y).wait_recv()
    across = remote(from_y, from_y, sems, 5, x)
    across.start()
    return [onward, across]


def gather_wait(gather, sems, slot, peers, count):
    for part, at in (((1, 1),), ((0, 3),), ((0, 4), (1, 5)))[slot]:
        block = half_of(gather, peers[slot], part, count)
        remote(block, block, sems, at, peers[slot]).wait_recv()


HALF_ORDER = ((0, 0), (1, 1), (0, 1), (1, 0), (2, 0), (2, 1))


def half_rows(index, part, count):
    half = count // 2
    return pl.ds(pl.multiple_of(index * count + part * half, half), half)


def gather_wait_half(gather, sems, slot, part, peers, count):
    at = {(0, 1): 1, (1, 0): 3, (2, 0): 4, (2, 1): 5}.get((slot, part))
    if at is not None:
        block = half_of(gather, peers[slot], part, count)
        remote(block, block, sems, at, peers[slot]).wait_recv()


def reduce_send_half(slot, part, send, recv, sems, peers):
    half = send.shape[1] // 2
    quarter = half // 2
    plan = {
        (0, 0): [(0, half, 0, 0)],
        (1, 1): [(half, half, 1, 1)],
        (2, 0): [(0, quarter, 2, 0), (quarter, quarter, 3, 0)],
        (2, 1): [(half, quarter, 4, 1), (half + quarter, quarter, 5, 1)],
    }.get((slot, part), [])
    copies = [
        remote(
            send.at[slot, pl.ds(start, size)], recv.at[slot, pl.ds(start, size)], sems, at,
            peers[to],
        )
        for start, size, at, to in plan
    ]
    for copy in copies:
        copy.start()
    return copies


def reduce_send(slot, send, recv, sems, peers):
    x, y, _ = peers
    half = send.shape[1] // 2
    quarter = half // 2
    if slot == 2:
        plan = [(0, quarter, 2, x), (half, quarter, 4, y), (quarter, quarter, 3, x)]
        plan.append((half + quarter, quarter, 5, y))
    else:
        plan = [(slot * half, half, slot, (x, y)[slot])]
    copies = [
        remote(
            send.at[slot, pl.ds(start, size)], recv.at[slot, pl.ds(start, size)], sems, at, peer
        )
        for start, size, at, peer in plan
    ]
    for copy in copies:
        copy.start()
    return copies


def reduce_pass(send, recv, sems, peers):
    x, y, _ = peers
    half = send.shape[1] // 2
    quarter = half // 2
    copies = []
    for start, at, source, slot, peer in (
        (half, 4, y, 0, x),
        (0, 2, x, 1, y),
        (half + quarter, 5, y, 0, x),
        (quarter, 3, x, 1, y),
    ):
        rows = pl.ds(start, quarter)
        remote(send.at[2, rows], recv.at[2, rows], sems, at, source).wait_recv()
        add_low(send.at[slot, rows], recv.at[2, rows])
        copy = remote(send.at[slot, rows], recv.at[slot, rows], sems, at + 4, peer)
        copy.start()
        copies.append(copy)
    return copies


def reduce_wait(send, recv, sems, peers):
    x, y, _ = peers
    half = send.shape[1] // 2
    quarter = half // 2
    for slot, start, size, at, peer in (
        (0, 0, half, 0, x),
        (1, half, half, 1, y),
        (0, half, quarter, 8, x),
        (1, 0, quarter, 6, y),
        (0, half + quarter, quarter, 9, x),
        (1, quarter, quarter, 7, y),
    ):
        rows = pl.ds(start, size)
        remote(send.at[slot, rows], recv.at[slot, rows], sems, at, peer).wait_recv()


def by_rows(total, step, body):
    def run(i, carry):
        body(pl.ds(pl.multiple_of(i * step, step), step))
        return carry

    lax.fori_loop(0, total // step, run, 0)


def valid_rows(lengths, start, count):
    at = lax.broadcasted_iota(jnp.int32, (count, 1), 0) + start
    return (at < lengths[0, lax.axis_index("section")]).astype(f32)


def normed_rows(x, gain, shift):
    mean = jnp.mean(x, axis=-1, keepdims=True)
    centred = x - mean
    inverse = lax.rsqrt(jnp.mean(centred * centred, axis=-1, keepdims=True) + 1e-05)
    return centred * inverse * gain + shift


def norm_back_rows(grad, x, gain):
    mean = jnp.mean(x, axis=-1, keepdims=True)
    centred = x - mean
    inverse = lax.rsqrt(jnp.mean(centred * centred, axis=-1, keepdims=True) + 1e-05)
    hat = centred * inverse
    scaled = grad * gain
    back = inverse * (
        scaled
        - jnp.mean(scaled, axis=-1, keepdims=True)
        - hat * jnp.mean(scaled * hat, axis=-1, keepdims=True)
    )
    return back, jnp.sum(grad * hat, axis=0, keepdims=True), jnp.sum(grad, axis=0, keepdims=True)


def norm_into(gather, start, x, gain, shift):
    step = 32

    def body(i, carry):
        rows = pl.ds(pl.multiple_of(i * step, step), step)
        at = pl.ds(pl.multiple_of(start + i * step, step), step)
        gather[at, :] = normed_rows(x[rows, :].astype(f32), gain, shift).astype(low)
        return carry

    lax.fori_loop(0, x.shape[0] // step, body, 0)


def masked_into(gather, start, grad, lengths):
    step = 32

    def body(i, carry):
        rows = pl.ds(pl.multiple_of(i * step, step), step)
        at = pl.ds(pl.multiple_of(start + i * step, step), step)
        value = grad[rows, :].astype(f32) * valid_rows(lengths, start + i * step, step)
        gather[at, :] = value.astype(low)
        return carry

    lax.fori_loop(0, grad.shape[0] // step, body, 0)


def add_parts(own, recv, x, start, lengths):
    def body(rows):
        total = own[rows, :] + recv[0, rows, :].astype(f32) + recv[1, rows, :].astype(f32)
        mask = valid_rows(lengths, start + rows.start, 32)
        own[rows, :] = x[rows, :].astype(f32) + mask * total

    by_rows(own.shape[0], 32, body)


def norm_back_parts(own, recv, grad, x, gain, sums):
    sums[...] = jnp.zeros(sums.shape, f32)

    def body(rows):
        total = own[rows, :] + recv[0, rows, :].astype(f32) + recv[1, rows, :].astype(f32)
        back, gain_sum, shift_sum = norm_back_rows(total, x[rows, :].astype(f32), gain)
        own[rows, :] = grad[rows, :].astype(f32) + back
        sums[0:1, :] += gain_sum
        sums[1:2, :] += shift_sum

    by_rows(own.shape[0], 32, body)


def fetch(pairs, sems, first=0):
    copies = [
        pltpu.make_async_copy(source, target, sems.at[first + at])
        for at, (source, target) in enumerate(pairs)
    ]
    for copy in copies:
        copy.start()
    return copies


def weight_pairs_mixer(pack, win, wout):
    rows, cols = wout.shape[2], wout.shape[3] // 4
    split = win.shape[3]
    pairs = [(pack.at[:, :, :, pl.ds(0, split)], win)]
    for q in range(4):
        pairs.append(
            (
                pack.at[:, :, pl.ds(q * rows, rows), pl.ds(split, cols)],
                wout.at[:, :, :, pl.ds(q * cols, cols)],
            )
        )
    return pairs


def half_pairs_mixer(half_pack, win, wout):
    rows, cols = wout.shape[2], wout.shape[3] // 4
    split = win.shape[3]
    section = lax.axis_index("section")
    pairs = [(win.at[section], half_pack.at[:, :, pl.ds(0, split)])]
    for q in range(4):
        pairs.append(
            (
                wout.at[section, :, :, pl.ds(q * cols, cols)],
                half_pack.at[:, pl.ds(q * rows, rows), pl.ds(split, cols)],
            )
        )
    return pairs


class ChipGather:
    def __init__(self, own, pack, plane_sems, core_sems):
        self.section = lax.axis_index("section")
        here, near, far = along_planes()
        self.pack, self.plane_sems, self.core_sems = pack, plane_sems, core_sems
        self.near, self.far = near, far
        self.order = (here, near, far, (near + 2) % 4)
        self.own = own
        self.sends = []

    def move(self, at, sems, slot, device):
        block = self.pack.at[self.section, self.order[at]]
        copy = remote_to(self.own if at == 0 else block, block, sems, slot, device)
        copy.start()
        self.sends.append(copy)

    def to_core(self, slot):
        self.move(slot, self.core_sems, slot, other_core())

    def begin(self, load_sem):
        self.move(0, self.plane_sems, 1, {"dp": self.far})
        self.move(0, self.plane_sems, 0, {"dp": self.near})
        self.to_core(0)
        self.keep = pltpu.make_async_copy(
            self.own, self.pack.at[self.section, self.order[0]], load_sem
        )
        self.keep.start()

    def arrived(self, slot):
        block = self.pack.at[self.section, self.order[slot + 1]]
        remote_to(block, block, self.plane_sems, slot, {"dp": self.near}).wait_recv()

    def forward(self):
        self.arrived(1)
        self.move(2, self.plane_sems, 2, {"dp": self.near})
        self.to_core(2)
        self.arrived(0)
        self.to_core(1)

    def end(self):
        self.arrived(2)
        self.to_core(3)
        self.keep.wait()
        for slot in range(4):
            block = self.pack.at[1 - self.section, self.order[slot]]
            remote_to(block, block, self.core_sems, slot, other_core()).wait_recv()


def sine_pair(x):
    turns = jnp.floor(x * (2.0 / math.pi) + 0.5)
    rest = x - turns * 1.5703125
    rest = rest - turns * 4.837512969970703125e-4
    rest = rest - turns * 7.54978995489188e-8
    square = rest * rest
    sine = -1.9515295891e-4 * square + 8.3321608736e-3
    sine = (sine * square - 1.6666654611e-1) * square * rest + rest
    cosine = 2.443315711809948e-5 * square - 1.388731625493765e-3
    cosine = (cosine * square + 4.166664568298827e-2) * square * square - 0.5 * square + 1.0
    halves = jnp.floor(turns * 0.5)
    odd = turns - 2.0 * halves
    back = halves - 2.0 * jnp.floor(halves * 0.5)
    swapped = odd > 0.5
    side = 1.0 - 2.0 * back
    wave = jnp.where(swapped, cosine, sine) * side
    slope = jnp.where(swapped, -sine, cosine) * side
    return wave, slope


def network_rows(small, embedding, network, taps_low, i):
    step = 256
    waves1, waves2, steep1, steep2 = network
    knots = waves1.shape[1]
    pair = (pl.ds(i * step, step), pl.ds(embedding.shape[0] // 2 + i * step, step))

    def layer(sources, weights, waves, steep):
        inner = jnp.concatenate([dot_exact(item, weights) for item in sources], 1)
        wave, slope = sine_pair(inner)
        for at, rows in enumerate(pair):
            cols = slice(at * knots, (at + 1) * knots)
            waves[rows, :] = wave[:, cols]
            steep[rows, :] = slope[:, cols]

    layer([embedding[rows, 0:64] for rows in pair], small[64:128, 128:192], waves1, steep1)
    layer([waves1[rows, :] for rows in pair], small[64:128, 0:64], waves2, steep2)
    for rows in pair:
        times = lax.broadcasted_iota(jnp.int32, (step, 1), 0) + rows.start
        fade = jnp.exp(-times.astype(f32) * small[154:155, :])
        taps_low[rows, :] = (dot_exact(waves2[rows, :], small[0:64, :]) * fade).astype(low)


def ff_blocks(
    gather, wup, wdown, value, slope, result_out, send, recv, gather_sems, reduce_sems, me, peers,
    pause,
):
    count, width = result_out.shape
    half = wup.shape[3]
    sends = []
    for slot, part in ((None, None), *HALF_ORDER):
        if slot is None:
            rows, sent = rows_of(me, count), None
        else:
            rows = half_rows(peers[slot], part, count)
            sent = slice(part * count // 2, (part + 1) * count // 2)
            gather_wait_half(gather, gather_sems, slot, part, peers, count)

        def hidden(i, carry):
            cols = pl.ds(pl.multiple_of(i * 256, 256), 256)
            for h in range(2):
                pre = mm(gather[rows, :], wup[h, :, :, cols].reshape(width, 256))
                after, steep = gelu_both(pre)
                at = pl.ds(pl.multiple_of(h * half + i * 256, 256), 256)
                value[rows, at] = after.astype(low)
                slope[rows, at] = steep.astype(low)
            return carry

        lax.fori_loop(0, half // 256, hidden, 0)
        for h in range(2):
            cols = slice(h * width // 2, (h + 1) * width // 2)
            out = mm(value[rows, :], wdown[h].reshape(2 * half, width // 2))
            if slot is None:
                result_out[:, cols] = out
            else:
                send[slot, sent, cols] = out.astype(low)
        if slot is not None:
            sends += reduce_send_half(slot, part, send, recv, reduce_sems, peers)
            pause(slot, part)
    return sends


def mixer_forward_kernel(
    s, gathers, x, *refs
):
    if gathers:
        (
            cotangent, embedding, lengths, w_in, w_out, w_up, w_down, gain, shift, tap_rows, first_w,
            second_w, last_w, direct, rates, waves_hbm, back_hbm,
            pack_out, ff_out, late_out, par_out, small_out, next_pack_out, ff_part_out,
            *refs,
        ) = refs
        network_outs, next_outs, refs = refs[:5], refs[5:10], refs[10:]
        second_out, value_out, slope_out, result_out, *refs = refs
        (
            *refs, waves1, waves2, steep1, steep2, taps_low, pack, ff_all, late, next_pack, core_sems,
            plane_sems, ff_core_sems, ff_plane_sems, next_core_sems, next_plane_sems, late_sems,
            pack_sems, mixer_parts, ff_parts, par_all, small_all, stage_in, stage_out, stage_up,
            in_sems, out_sems, up_sems, down_sems, par_sems, small_sems,
            second, ff_send, ff_recv, second_sems, ff_sems, network_sems,
        ) = refs
        x = x.at[lax.axis_index("section"), 0]
        cotangent = cotangent.at[lax.axis_index("section"), 0]
        network = (waves1, waves2, steep1, steep2)
    else:
        par_all, small_all, lengths, weights_hbm, filt_hbm, waves_hbm, back_hbm, *refs = refs
    (
        normed_out, proj_out, stream_out, prod_out, spec_out, filtered_out, gated_out, middle_out,
        gather, win, wout, filt, waves, back, proj, proj_low, streams, prod, spec, mixed, filtered,
        gated, send, recv, gather_sems, reduce_sems, load_sems, store_sems,
    ) = refs
    par, small = par_all.at[s], small_all.at[s]
    me = lax.axis_index("seq")
    peers = neighbours(me)
    count, width = x.shape
    length = gather.shape[0]
    chans = prod.shape[1]
    half = win.shape[3]
    if gathers:
        section = lax.axis_index("section")
        targets = shuffle_targets(section, me, peers)
        greeted = greet([device for _, _, device in targets] + plane_devices())
    else:
        greeted = greet(in_plane(peers[:2]))
    tables = fetch([(waves_hbm, waves), (back_hbm, back)], load_sems)
    sends = []
    if gathers:
        shuffle_stage(w_in, w_out, w_up, stage_in, stage_out, stage_up)
        parameters_stage(
            me, par_all.at[section], small_all.at[section], gain, shift, tap_rows, first_w, second_w,
            last_w, direct, rates,
        )
        all_here(greeted)
        sends += shuffle_send(
            section, me, targets, (stage_in, stage_out, stage_up, w_down), (mixer_parts, ff_parts),
            (par_all, small_all), (in_sems, out_sems, up_sems, down_sems, par_sems, small_sems),
        )
        mixer_pack = ChipGather(mixer_parts.at[0], pack, plane_sems, core_sems)
        ff_pack = ChipGather(ff_parts.at[0], ff_all, ff_plane_sems, ff_core_sems)
        for sems, item in ((par_sems, par_all), (small_sems, small_all)):
            block = item.at[1 - section]
            remote_to(block, block, sems, 0, other_core()).wait_recv()
        norm_into(gather, me * count, x, par[0:1, :], par[1:2, :])
        shuffle_wait_mixer(section, me, targets, mixer_parts, stage_in, in_sems, out_sems)
        mixer_pack.begin(pack_sems.at[0])
        sends += gather_begin(gather, gather_sems, me, peers, count)
        masked_into(late, me * count, cotangent, lengths)
    else:
        weights = fetch(weight_pairs_mixer(weights_hbm, win, wout), load_sems, 2)
        filt_load = fetch([(filt_hbm, filt)], load_sems, 7)
        norm_into(gather, me * count, x, par[0:1, :], par[1:2, :])
        all_here(greeted)
        sends += gather_begin(gather, gather_sems, me, peers, count)
    proj[0:8, :] = jnp.zeros((8, proj.shape[1]), f32)
    tile_rows = 256

    def filter_spectrum(i, carry):
        rows = pl.ds(pl.multiple_of(i * tile_rows, tile_rows), tile_rows)
        filt[rows, :] = mm(waves[rows, :], taps_low[...])
        return carry

    stores = []
    if gathers:
        network_rows(small, embedding, network, taps_low, 0)
    sends += gather_forward(gather, gather_sems, peers, count)
    if gathers:
        sends += gather_begin(late, late_sems, me, peers, count)
        mixer_pack.forward()
        shuffle_wait_ff(section, me, targets, ff_parts, stage_up, up_sems, down_sems)
        ff_pack.begin(pack_sems.at[1])
        network_rows(small, embedding, network, taps_low, 1)
        tables[0].wait()
        lax.fori_loop(0, 2 * length // tile_rows, filter_spectrum, 0)
        network_stores = fetch(list(zip((filt, *network), network_outs)), network_sems)
        mixer_pack.end()
        weights = fetch(weight_pairs_mixer(pack, win, wout), load_sems, 2)
        stores += fetch(
            [
                (pack, pack_out),
                (par_all, par_out),
                (small_all, small_out),
                (ff_parts.at[1], ff_part_out),
            ],
            pack_sems,
            4,
        )
    else:
        tables[0].wait()
    weights[0].wait()
    for slot in (None, 0, 1, 2):
        source = me if slot is None else peers[slot]
        if slot is not None:
            gather_wait(gather, gather_sems, slot, peers, count)
        block = gather[rows_of(source, count), :]
        for h in range(2):
            proj[pl.ds(pl.multiple_of(source * count + 8, 8), count), h * half : (h + 1) * half] = mm(
                block, win[h].reshape(width, half)
            )
    if gathers:
        sends += gather_forward(late, late_sems, peers, count)
    step = 128

    def short_conv(i, carry):
        start = pl.multiple_of(i * step, step)
        for g in range(3):
            cols = slice(g * chans, (g + 1) * chans)
            tile = proj[pl.ds(start, step + 8), cols]
            proj_low[pl.ds(start, step), cols] = tile[8:].astype(low)
            value = (
                small[144 + 3 * g : 145 + 3 * g, :] * tile[8:]
                + small[145 + 3 * g : 146 + 3 * g, :] * pltpu.roll(tile, 1, 0)[8:]
                + small[146 + 3 * g : 147 + 3 * g, :] * pltpu.roll(tile, 2, 0)[8:]
            )
            streams[pl.ds(start, step), cols] = value.astype(low)
        first = streams[pl.ds(start, step), 0:chans].astype(f32)
        third = streams[pl.ds(start, step), 2 * chans : 3 * chans].astype(f32)
        prod[pl.ds(start, step), :] = (first * third * valid_rows(lengths, start, step)).astype(low)
        return carry

    lax.fori_loop(0, length // step, short_conv, 0)
    stores += fetch(
        [(gather, normed_out), (proj_low, proj_out), (streams, stream_out), (prod, prod_out)],
        store_sems,
    )
    if not gathers:
        filt_load[0].wait()

    def spectrum(i, carry):
        up = pl.ds(pl.multiple_of(i * tile_rows, tile_rows), tile_rows)
        down = pl.ds(pl.multiple_of(i * tile_rows + length, tile_rows), tile_rows)
        prod_cos = mm(waves[up, :], prod[...])
        prod_sin = mm(waves[down, :], prod[...])
        filt_cos, filt_sin = filt[up, :], filt[down, :]
        spec[up, :] = prod_cos.astype(low)
        spec[down, :] = prod_sin.astype(low)
        mixed[up, :] = (prod_cos * filt_cos - prod_sin * filt_sin).astype(low)
        mixed[down, :] = (prod_cos * filt_sin + prod_sin * filt_cos).astype(low)
        return carry

    lax.fori_loop(0, length // tile_rows, spectrum, 0)
    tables[1].wait()
    for load in weights[1:]:
        load.wait()
    for slot in (2, 0, 1, None):
        target = me if slot is None else peers[slot]
        rows = rows_of(target, count)
        value = mm(back[rows, :], mixed[...]) * (1.0 / length)
        value = value + small[153:154, :] * prod[rows, :].astype(f32)
        filtered[rows, :] = value
        gate = (streams[rows, chans : 2 * chans].astype(f32) * value).astype(low)
        gated[rows, :] = gate
        outs = [mm(gate, wout[h].reshape(chans, width // 2)) for h in range(2)]
        for h in range(2):
            cols = slice(h * width // 2, (h + 1) * width // 2)
            if slot is None:
                middle_out[:, cols] = outs[h]
            else:
                send[slot, :, cols] = outs[h].astype(low)
        if slot is not None:
            sends += reduce_send(slot, send, recv, reduce_sems, peers)
    if gathers:
        ff_pack.forward()
        for slot in range(3):
            gather_wait(late, late_sems, slot, peers, count)
        stores += fetch([(late, late_out)], pack_sems, 2)
    sends += reduce_pass(send, recv, reduce_sems, peers)
    stores += fetch(
        [(spec, spec_out), (filtered, filtered_out), (gated, gated_out)],
        store_sems,
        4,
    )
    if gathers:
        for store in network_stores:
            store.wait()
        for i in range(2):
            network_rows(small_all.at[1], embedding, network, taps_low, i)
        lax.fori_loop(0, 2 * length // tile_rows, filter_spectrum, 0)
        network_stores = fetch(list(zip((filt, *network), next_outs)), network_sems)
    reduce_wait(send, recv, reduce_sems, peers)
    add_parts(middle_out, recv, x, me * count, lengths)
    if gathers:
        next_mixer = ChipGather(mixer_parts.at[1], next_pack, next_plane_sems, next_core_sems)
        norm_into(second, me * count, middle_out, par[2:3, :], par[3:4, :])
        sends += gather_begin(second, second_sems, me, peers, count)
        sends += gather_forward(second, second_sems, peers, count)
        ff_pack.end()
        next_mixer.begin(pack_sems.at[8])
        stores += fetch([(ff_all, ff_out)], pack_sems, 3)
        rows_up = ff_all.shape[2] // 2
        value, slope = waves.at[pl.ds(0, length)], waves.at[pl.ds(length, length)]

        def pause(slot, part):
            if (slot, part) == (1, 1):
                next_mixer.forward()

        sends += ff_blocks(
            second, ff_all.at[:, :, pl.ds(0, rows_up)], ff_all.at[:, :, pl.ds(rows_up, rows_up)],
            value, slope, result_out, ff_send, ff_recv, second_sems, ff_sems, me, peers, pause,
        )
        sends += reduce_pass(ff_send, ff_recv, ff_sems, peers)
        stores += fetch([(second, second_out), (value, value_out), (slope, slope_out)], pack_sems, 9)
        next_mixer.end()
        stores += fetch([(next_pack, next_pack_out)], pack_sems, 12)
        reduce_wait(ff_send, ff_recv, ff_sems, peers)
        add_parts(result_out, ff_recv, middle_out, me * count, lengths)
        sends += mixer_pack.sends + ff_pack.sends + next_mixer.sends
        stores += network_stores
    for copy in sends:
        copy.wait_send()
    for store in stores:
        store.wait()


def ff_turn_kernel(
    s, cotangent, x, par_all, lengths, pack, late_hbm,
    half_out, result_out, middle_grad_out, sums_out,
    gather, late, wup, wdown, value, pre, wgrad, other, send, recv, send_back, recv_back,
    gather_sems, reduce_sems, load_sems, store_sems, back_sems, core_sems,
):
    par = par_all.at[s]
    grad = cotangent.at[lax.axis_index("section"), 0]
    me = lax.axis_index("seq")
    peers = neighbours(me)
    count, width = x.shape
    half = wup.shape[3]
    rows_up = wup.shape[2]
    greeted = greet(in_plane(peers[:2]) + [other_core()])
    loads = fetch(
        [
            (pack.at[:, :, pl.ds(0, rows_up), :], wup),
            (pack.at[:, :, pl.ds(rows_up, wdown.shape[2]), :], wdown),
            (late_hbm, late),
        ],
        load_sems,
    )
    norm_into(gather, me * count, x, par[2:3, :], par[3:4, :])
    all_here(greeted)
    sends = gather_begin(gather, gather_sems, me, peers, count)
    for load in loads:
        load.wait()
    for slot, part in ((None, None), *HALF_ORDER):
        if slot is None:
            rows, sent = rows_of(me, count), None
        else:
            rows = half_rows(peers[slot], part, count)
            sent = slice(part * count // 2, (part + 1) * count // 2)
            gather_wait_half(gather, gather_sems, slot, part, peers, count)

        def hidden(i, carry):
            cols = pl.ds(pl.multiple_of(i * rows_up, rows_up), rows_up)
            for h in range(2):
                block = h * (half // rows_up) + i
                at = pl.ds(pl.multiple_of(block * rows_up, rows_up), rows_up)
                after, steep = gelu_both(
                    mm(gather[rows, :], wup[h, :, :, cols].reshape(width, rows_up))
                )
                value[rows, at] = after.astype(low)
                back = mm_t(late[rows, : width // 2], wdown[0, block]) + mm_t(
                    late[rows, width // 2 :], wdown[1, block]
                )
                pre[rows, at] = (back * steep).astype(low)
            return carry

        lax.fori_loop(0, half // rows_up, hidden, 0)

        def through(i, carry):
            cols = pl.ds(pl.multiple_of(i * rows_up, rows_up), rows_up)
            back = mm_t(pre[rows, :half], wup[0, i]) + mm_t(pre[rows, half:], wup[1, i])
            if slot is None:
                middle_grad_out[:, cols] = back
            else:
                send_back[slot, sent, cols] = back.astype(low)
            return carry

        lax.fori_loop(0, width // rows_up, through, 0)
        if slot is None:
            sends += gather_forward(gather, gather_sems, peers, count)
        else:
            sends += reduce_send_half(slot, part, send_back, recv_back, back_sems, peers)
    for slot in (2, 0, 1, None):
        rows = rows_of(me if slot is None else peers[slot], count)
        for h in range(2):
            cols = slice(h * width // 2, (h + 1) * width // 2)
            out = mm(value[rows, :], wdown[h].reshape(2 * half, width // 2))
            if slot is None:
                result_out[:, cols] = out
            else:
                send[slot, :, cols] = out.astype(low)
    sends += reduce_pass(send_back, recv_back, back_sems, peers)
    for slot in (2, 0, 1):
        sends += reduce_send(slot, send, recv, reduce_sems, peers)

    def weights(i, carry):
        cols = pl.ds(pl.multiple_of(i * rows_up, rows_up), rows_up)
        for h in range(2):
            wgrad[h, i, 0:rows_up, :] = t_mm(
                gather[:, cols], pre[:, h * half : (h + 1) * half]
            ).astype(low)
            wgrad[h, i, rows_up : 2 * rows_up, :] = t_mm(
                value[:, cols], late[:, h * width // 2 : (h + 1) * width // 2]
            ).astype(low)
        return carry

    lax.fori_loop(0, width // rows_up, weights, 0)
    swapped = [(wgrad, other)]
    swaps = swap_begin(swapped, core_sems)
    sends += swaps
    sends += reduce_pass(send, recv, reduce_sems, peers)
    reduce_wait(send_back, recv_back, back_sems, peers)
    norm_back_parts(middle_grad_out, recv_back, grad, x, par[2:3, :], sums_out)
    swap_end(swaps, swapped)
    stores = fetch([(wgrad.at[lax.axis_index("section")], half_out)], store_sems)
    reduce_wait(send, recv, reduce_sems, peers)
    add_parts(result_out, recv, x, me * count, lengths)
    for copy in sends:
        copy.wait_send()
    for store in stores:
        store.wait()


def ff_backward_kernel(
    s, grad, middle, par_all, lengths, pack, second_hbm, value_hbm, slope_hbm, earlier, out0, out1,
    half_out, middle_grad_out, sums_out, summed, block_outputs,
    gather, wup, wdown, second, value, slope, pre, wgrad, other, send, recv, gather_sems,
    reduce_sems, load_sems, store_sems, mine, arrived, plane_sems, sum_sems, core_sems, layer_sems,
    keep_sems,
):
    par = par_all.at[s]
    me = lax.axis_index("seq")
    peers = neighbours(me)
    count, width = grad.shape
    greeted = greet(in_plane(peers[:2]) + plane_devices() + [other_core()])
    half = wup.shape[3]
    units = 2 * half
    up_rows = wup.shape[2]
    loads = fetch(
        [
            (pack.at[:, :, pl.ds(0, up_rows), :], wup),
            (pack.at[:, :, pl.ds(up_rows, wdown.shape[2]), :], wdown),
            (slope_hbm, slope),
            (second_hbm, second),
            (value_hbm, value),
        ],
        load_sems,
    )
    masked_into(gather, me * count, grad, lengths)
    all_here(greeted)
    sends = gather_begin(gather, gather_sems, me, peers, count)
    plane_sum = PlaneSum(earlier, mine, arrived, plane_sems, sum_sems)
    plane_sum.begin()
    by_layer(True, ((out0, out1, block_outputs),), layer_sems, keep_sems)
    for load in loads[:3]:
        load.wait()
    for slot, part in ((None, None), *HALF_ORDER):
        if slot is None:
            rows, sent = rows_of(me, count), None
        else:
            rows = half_rows(peers[slot], part, count)
            sent = slice(part * count // 2, (part + 1) * count // 2)
            gather_wait_half(gather, gather_sems, slot, part, peers, count)

        def hidden(i, carry):
            cols = pl.ds(pl.multiple_of(i * up_rows, up_rows), up_rows)
            back = mm_t(gather[rows, : width // 2], wdown[0, i]) + mm_t(
                gather[rows, width // 2 :], wdown[1, i]
            )
            pre[rows, cols] = (back * slope[rows, cols].astype(f32)).astype(low)
            return carry

        lax.fori_loop(0, units // up_rows, hidden, 0)

        def through(i, carry):
            cols = pl.ds(pl.multiple_of(i * up_rows, up_rows), up_rows)
            back = mm_t(pre[rows, :half], wup[0, i]) + mm_t(pre[rows, half:], wup[1, i])
            if slot is None:
                middle_grad_out[:, cols] = back
            else:
                send[slot, sent, cols] = back.astype(low)
            return carry

        lax.fori_loop(0, width // up_rows, through, 0)
        if slot is None:
            sends += gather_forward(gather, gather_sems, peers, count)
        else:
            sends += reduce_send_half(slot, part, send, recv, reduce_sems, peers)
    plane_sum.forward()
    for load in loads[3:]:
        load.wait()

    def weights(i, carry):
        cols = pl.ds(pl.multiple_of(i * up_rows, up_rows), up_rows)
        for h in range(2):
            wgrad[h, i, 0:up_rows, :] = t_mm(
                second[:, cols], pre[:, h * half : (h + 1) * half]
            ).astype(low)
            wgrad[h, i, up_rows : 2 * up_rows, :] = t_mm(
                value[:, cols], gather[:, h * width // 2 : (h + 1) * width // 2]
            ).astype(low)
        return carry

    lax.fori_loop(0, width // up_rows, weights, 0)
    swapped = [(wgrad, other)]
    swaps = swap_begin(swapped, core_sems)
    sends += swaps
    sends += reduce_pass(send, recv, reduce_sems, peers)
    swap_end(swaps, swapped)
    stores = fetch([(wgrad.at[lax.axis_index("section")], half_out)], store_sems)
    plane_sum.end(summed)
    sends += plane_sum.sends
    reduce_wait(send, recv, reduce_sems, peers)
    norm_back_parts(middle_grad_out, recv, grad, middle, par[2:3, :], sums_out)
    by_layer(False, ((out0, out1, block_outputs),), layer_sems, keep_sems)
    for copy in sends:
        copy.wait_send()
    for store in stores:
        store.wait()


def t_mm_exact(a, b):
    return lax.dot_general(
        a, b, (((0,), (0,)), ((), ())), preferred_element_type=f32, precision=precise
    )


def mm_t_exact(a, b):
    return lax.dot_general(
        a, b, (((1,), (1,)), ((), ())), preferred_element_type=f32, precision=precise
    )


def dot_exact(a, b):
    return jnp.dot(a, b, preferred_element_type=f32, precision=precise)


def by_layer(begin, triples, layer_sems, keep_sems):
    section = lax.axis_index("section")
    for index in range(2):

        @pl.when(section == index)
        def _():
            for at, (first, second, target) in enumerate(triples):
                kept, sent = (first, second) if index == 0 else (second, first)
                slot = target.at[index]
                copies = (
                    pltpu.make_async_copy(kept, slot, keep_sems.at[at]),
                    remote_to(sent, slot, layer_sems, at, other_core()),
                )
                for copy in copies:
                    if begin:
                        copy.start()
                    else:
                        copy.wait()


def mixer_backward_kernel(
    s, grad, x, par_all, small_all, embedding, late, lengths, pack, filt_hbm, waves_hbm, back_hbm, normed_hbm, proj_hbm,
    stream_hbm, prod_hbm, spec_hbm, filtered_hbm, gated_hbm, waves1_hbm, waves2_hbm, steep1_hbm,
    steep2_hbm, earlier,
    half_out, small_out, input_grad_out, summed,
    gather, win, wout, filt, waves, back, normed, proj, streams, prod, spec, filtered, gated,
    gated_grad, filtered_grad, both, grad_spec, grad_sum, filter_grad, mixed, proj_grad, wgrad_in, wgrad_out_part,
    other_in, other_out, waves1, waves2, steep1, steep2, sums, taps_sum, send, recv, gather_sems, reduce_sems, load_sems, store_sems,
    mine, arrived, plane_sems, sum_sems, core_sems,
):
    par, small = par_all.at[s], small_all.at[s]
    me = lax.axis_index("seq")
    peers = neighbours(me)
    if s == 0:
        x = x.at[lax.axis_index("section"), 0]
    count, width = grad.shape
    greeted = greet(in_plane(peers[:2]) + plane_devices() + [other_core()])
    length = gather.shape[0]
    chans = prod.shape[1]
    half = win.shape[3]
    depth = win.shape[2]
    loads = fetch(
        weight_pairs_mixer(pack, win, wout)
        + [
            (stream_hbm, streams),
            (waves_hbm, waves),
            (filt_hbm, filt),
            (spec_hbm, spec),
            (back_hbm, back),
            (prod_hbm, prod),
            (filtered_hbm, filtered),
            (proj_hbm, proj),
            (normed_hbm, normed),
            (gated_hbm, gated),
            (waves1_hbm, waves1),
            (waves2_hbm, waves2),
            (steep1_hbm, steep1),
            (steep2_hbm, steep2),
        ],
        load_sems,
    )
    masked_into(gather, me * count, grad, lengths)
    all_here(greeted)
    sends = gather_begin(gather, gather_sems, me, peers, count)
    plane_sum = PlaneSum(earlier, mine, arrived, plane_sems, sum_sems)
    plane_sum.begin()
    for load in loads[1:6]:
        load.wait()
    tile_rows = 256
    for slot in (None, 0, 1, 2):
        source = me if slot is None else peers[slot]
        rows = rows_of(source, count)
        if slot is not None:
            gather_wait(gather, gather_sems, slot, peers, count)
        value = (
            mm_t(gather[rows, : width // 2], wout[0].reshape(chans, width // 2))
            + mm_t(gather[rows, width // 2 :], wout[1].reshape(chans, width // 2))
        ).astype(low)
        gated_grad[rows, :] = value
        filtered_grad[rows, :] = (
            value.astype(f32) * streams[rows, chans : 2 * chans].astype(f32)
        ).astype(low)
        if slot is None:
            sends += gather_forward(gather, gather_sems, peers, count)
            for load in loads[6:]:
                load.wait()
            loads[0].wait()
        if slot == 2:
            plane_sum.forward()

        def spectrum(i, carry):
            up = pl.ds(pl.multiple_of(i * tile_rows, tile_rows), tile_rows)
            down = pl.ds(pl.multiple_of(i * tile_rows + length, tile_rows), tile_rows)
            fg_cos = mm(waves[up, rows], filtered_grad[rows, :])
            fg_sin = mm(waves[down, rows], filtered_grad[rows, :])
            if slot is not None:
                fg_cos = fg_cos + grad_sum[up, :]
                fg_sin = fg_sin + grad_sum[down, :]
            if slot != 2:
                grad_sum[up, :] = fg_cos
                grad_sum[down, :] = fg_sin
            else:
                filt_cos, filt_sin = filt[up, :], filt[down, :]
                grad_spec[up, :] = fg_cos.astype(low)
                grad_spec[down, :] = fg_sin.astype(low)
                both[up, :] = (filt_cos * fg_cos + filt_sin * fg_sin).astype(low)
                both[down, :] = (filt_cos * fg_sin - filt_sin * fg_cos).astype(low)
            return carry

        lax.fori_loop(0, length // tile_rows, spectrum, 0)
    mixed[pl.ds(length, 8), :] = jnp.zeros((8, mixed.shape[1]), f32)

    def streams_back(i, carry):
        rows = pl.ds(pl.multiple_of(i * tile_rows, tile_rows), tile_rows)
        value = mm(back[rows, :], both[...]) * (1.0 / length)
        fg = filtered_grad[rows, :].astype(f32)
        prod_grad = (value + small[153:154, :] * fg).astype(low).astype(f32)
        mixed[rows, 0:chans] = (
            (prod_grad * streams[rows, 2 * chans : 3 * chans].astype(f32)).astype(low).astype(f32)
        )
        mixed[rows, chans : 2 * chans] = (
            (gated_grad[rows, :].astype(f32) * filtered[rows, :]).astype(low).astype(f32)
        )
        mixed[rows, 2 * chans : 3 * chans] = (
            (prod_grad * streams[rows, 0:chans].astype(f32)).astype(low).astype(f32)
        )
        return carry + jnp.sum(fg * prod[rows, :].astype(f32), axis=0, keepdims=True)

    small_out[...] = jnp.zeros(small_out.shape, f32)
    small_out[153:154, :] = lax.fori_loop(
        0, length // tile_rows, streams_back, jnp.zeros((1, chans), f32)
    )
    step = 128
    for slot in (2, 0, 1, None):
        target = me if slot is None else peers[slot]

        def short_back(i, carry):
            start = pl.multiple_of(target * count + i * step, step)
            for g in range(3):
                cols = slice(g * chans, (g + 1) * chans)
                tile = mixed[pl.ds(start, step + 8), cols]
                now = tile[:step]
                after = pltpu.roll(tile, step + 7, 0)[:step]
                later = pltpu.roll(tile, step + 6, 0)[:step]
                proj_grad[pl.ds(start, step), cols] = (
                    small[144 + 3 * g : 145 + 3 * g, :] * now
                    + small[145 + 3 * g : 146 + 3 * g, :] * after
                    + small[146 + 3 * g : 147 + 3 * g, :] * later
                ).astype(low)
            return carry

        lax.fori_loop(0, count // step, short_back, 0)
        rows = rows_of(target, count)

        def through(i, carry):
            cols = pl.ds(pl.multiple_of(i * depth, depth), depth)
            value = mm_t(proj_grad[rows, :half], win[0, i]) + mm_t(proj_grad[rows, half:], win[1, i])
            if slot is None:
                input_grad_out[:, cols] = value
            else:
                send[slot, :, cols] = value.astype(low)
            return carry

        lax.fori_loop(0, width // depth, through, 0)
        if slot is not None:
            sends += reduce_send(slot, send, recv, reduce_sems, peers)

    def weights(i, carry):
        cols = pl.ds(pl.multiple_of(i * depth, depth), depth)
        for h in range(2):
            wgrad_in[h, i] = t_mm(normed[:, cols], proj_grad[:, h * half : (h + 1) * half]).astype(
                low
            )
        return carry

    lax.fori_loop(0, width // depth, weights, 0)
    for h in range(2):
        value = t_mm(gated[...], gather[:, h * width // 2 : (h + 1) * width // 2]).astype(low)
        wgrad_out_part[h] = value.reshape(wgrad_out_part.shape[1:])
    swapped = [(wgrad_in, other_in), (wgrad_out_part, other_out)]
    swaps = swap_begin(swapped, core_sems)
    sends += swaps
    sends += reduce_pass(send, recv, reduce_sems, peers)
    taps_sum[...] = jnp.zeros(taps_sum.shape, f32)

    def tap_sums(i, carry):
        start = pl.multiple_of(i * step, step)
        for g in range(3):
            cols = slice(g * chans, (g + 1) * chans)
            tile = mixed[pl.ds(start, step + 8), cols]
            seen = proj[pl.ds(start, step), cols].astype(f32)
            for at in range(3):
                shift = pltpu.roll(tile, step + 8 - at, 0)[:step] if at else tile[:step]
                taps_sum[8 * at : 8 * at + 8, cols] += jnp.sum(
                    (seen * shift).reshape(step // 8, 8, chans), axis=0
                )
        return carry

    lax.fori_loop(0, length // step, tap_sums, 0)

    def filter_spectrum(i, carry):
        up = pl.ds(pl.multiple_of(i * tile_rows, tile_rows), tile_rows)
        down = pl.ds(pl.multiple_of(i * tile_rows + length, tile_rows), tile_rows)
        prod_cos, prod_sin = spec[up, :].astype(f32), spec[down, :].astype(f32)
        fg_cos, fg_sin = grad_spec[up, :].astype(f32), grad_spec[down, :].astype(f32)
        both[up, :] = (prod_cos * fg_cos + prod_sin * fg_sin).astype(low)
        both[down, :] = (prod_cos * fg_sin - prod_sin * fg_cos).astype(low)
        return carry

    lax.fori_loop(0, length // tile_rows, filter_spectrum, 0)

    def filter_back(i, carry):
        rows = pl.ds(pl.multiple_of(i * tile_rows, tile_rows), tile_rows)
        times = lax.broadcasted_iota(jnp.int32, (tile_rows, 1), 0) + i * tile_rows
        fade = jnp.exp(-times.astype(f32) * small[154:155, :])
        filter_grad[rows, :] = mm(back[rows, :], both[...]) * (1.0 / length) * fade
        return carry

    lax.fori_loop(0, length // tile_rows, filter_back, 0)
    small_out[0:64, :] = t_mm_exact(waves2[...], filter_grad[...])
    back2 = mm_t_exact(filter_grad[...], small[0:64, :]) * steep2[...]
    small_out[64:128, 0:64] = t_mm_exact(waves1[...], back2)
    back1 = mm_t_exact(back2, small[64:128, 0:64]) * steep1[...]
    small_out[64:128, 128:192] = t_mm_exact(embedding[:, 0:64], back1)
    for g in range(3):
        for at in range(3):
            small_out[144 + 3 * g + at : 145 + 3 * g + at, :] = jnp.sum(
                taps_sum[8 * at : 8 * at + 8, g * chans : (g + 1) * chans], axis=0, keepdims=True
            )
    swap_end(swaps, swapped)
    stores = fetch(half_pairs_mixer(half_out, wgrad_in, wgrad_out_part), store_sems)
    plane_sum.end(summed)
    sends += plane_sum.sends
    reduce_wait(send, recv, reduce_sems, peers)
    norm_back_parts(input_grad_out, recv, grad, x, par[0:1, :], sums)
    for q in range(width // chans):
        cols = slice(q * chans, (q + 1) * chans)
        small_out[128 + 2 * q : 130 + 2 * q, :] = sums[:, cols]
        small_out[136 + 2 * q : 138 + 2 * q, :] = late[:, cols]
    for copy in sends:
        copy.wait_send()
    for store in stores:
        store.wait()


def run_kernel(kernel, name, collective_id, operands, in_vmem, outs, out_vmem, scratch, flops):
    inside = pl.BlockSpec(memory_space=pltpu.VMEM)
    outside = pl.BlockSpec(memory_space=pl.ANY)
    scalars = pl.BlockSpec(memory_space=pltpu.SMEM)
    return pl.pallas_call(
        kernel,
        out_shape=[jax.ShapeDtypeStruct(shape, kind) for shape, kind in outs],
        in_specs=[
            scalars if item.dtype == jnp.int32 else inside if at in in_vmem else outside
            for at, item in enumerate(operands)
        ],
        out_specs=[inside if at in out_vmem else outside for at in range(len(outs))],
        scratch_shapes=scratch,
        compiler_params=pltpu.CompilerParams(
            collective_id=collective_id, has_side_effects=True, vmem_limit_bytes=60 * 2**20
        ),
        cost_estimate=pl.CostEstimate(flops=flops, bytes_accessed=2**25, transcendentals=0),
        name=name,
    )(*operands)


def exchange_scratch(count, width):
    return [pltpu.VMEM((3, count, width), low), pltpu.VMEM((3, count, width), low)]


def exchange_semaphores(count):
    return [pltpu.SemaphoreType.DMA((2, count)), pltpu.SemaphoreType.DMA((count,))]


def semaphores(loads, stores):
    return [
        pltpu.SemaphoreType.DMA((2, 6)),
        pltpu.SemaphoreType.DMA((2, 10)),
        pltpu.SemaphoreType.DMA((loads,)),
        pltpu.SemaphoreType.DMA((stores,)),
    ]


def mixer_weights_scratch(pack, width):
    _, dp_count, depth, cols = pack.shape
    return [
        pltpu.VMEM((2, dp_count, depth, 3 * cols // 4), low),
        pltpu.VMEM((2, dp_count, depth // 4, cols), low),
    ]


def mixer_forward(s, x, lengths, weights, waves, back, gathered):
    gathers = gathered is not None
    count, width = x.shape[-2:]
    length = waves.shape[1]
    chans, half = width // 4, width // 2
    knots, dp_count = chans // 4, lax.axis_size("dp")
    pack_shape = (2, dp_count, width // dp_count, half)
    pack = jax.ShapeDtypeStruct(pack_shape, low)
    vm, dma = pltpu.VMEM, pltpu.SemaphoreType.DMA
    outs = [
        ((length, width), low),
        ((length, 3 * chans), low),
        ((length, 3 * chans), low),
        ((length, chans), low),
        ((2 * length, chans), low),
        ((length, chans), f32),
        ((length, chans), low),
        ((count, width), f32),
    ]
    more = []
    if gathers:
        cotangent, embedding = gathered
        depth = weights[0].shape[0]
        units = 2 * half
        ff_shape = (2, dp_count, 2 * width // dp_count, half)
        half_in = 3 * chans // 2
        filters = [((2 * length, chans), f32), *[((length, knots), f32)] * 4]
        outs = [
            (pack_shape, low),
            (ff_shape, low),
            ((length, width), low),
            ((2, 8, width), f32),
            ((2, 160, chans), f32),
            (pack_shape, low),
            (ff_shape[2:], low),
            *filters,
            *filters,
            ((length, width), low),
            ((length, units), low),
            ((length, units), low),
            ((count, width), f32),
        ] + outs
        more = [
            *[vm((length, knots), f32)] * 4,
            vm((length, chans), low),
            vm(pack_shape, low),
            vm(ff_shape, low),
            vm((length, width), low),
            vm(pack_shape, low),
            *[dma((2, 4)), dma((2, 3))] * 3,
            dma((2, 6)),
            dma((13,)),
            vm((2, *pack_shape[2:]), low),
            vm((2, *ff_shape[2:]), low),
            vm((2, 8, width), f32),
            vm((2, 160, chans), f32),
            vm((2, 4, depth, half_in), low),
            vm((2, 4 * depth, half_in // 3), low),
            vm((2, 4, depth, half), low),
            dma((2, 7)),
            dma((2, 1)),
            dma((2, 7)),
            dma((2, 1)),
            dma((2, 1)),
            dma((2, 1)),
            vm((length, width), low),
            *exchange_scratch(count, width),
            dma((2, 6)),
            dma((2, 10)),
            dma((5,)),
        ]
        operands = (cotangent, embedding, lengths, *weights, waves, back)
        inside = range(len(operands) - 1)
        out_inside = (len(outs) - 9, len(outs) - 1)
    else:
        par, small, weights, filt = weights
        operands = (par, small, lengths, weights, filt, waves, back)
        inside = range(3)
        out_inside = (len(outs) - 1,)
    return run_kernel(
        partial(mixer_forward_kernel, s, gathers),
        "opening" if gathers else "mixer_forward",
        1 + s,
        (x, *operands),
        inside,
        outs,
        out_inside,
        [vm((length, width), low)]
        + mixer_weights_scratch(pack, width)
        + [
            vm((2 * length, chans), f32),
            vm((2 * length, length), low),
            vm((length, 2 * length), low),
            vm((length + 8, 3 * chans), f32),
            vm((length, 3 * chans), low),
            vm((length, 3 * chans), low),
            vm((length, chans), low),
            vm((2 * length, chans), low),
            vm((2 * length, chans), low),
            vm((length, chans), f32),
            vm((length, chans), low),
        ]
        + exchange_scratch(count, width)
        + semaphores(8, 7)
        + more,
        10**10,
    )


def ff_turn(s, cotangent, x, par, lengths, pack, late):
    count, width = x.shape
    _, dp_count, rows, half = pack.shape
    length, units = 4 * count, 2 * half
    vm = pltpu.VMEM
    return run_kernel(
        partial(ff_turn_kernel, s),
        "ff_turn",
        4,
        (cotangent, x, par, lengths, pack, late),
        range(3),
        [(pack.shape[1:], low), ((count, width), f32), ((count, width), f32), ((2, width), f32)],
        (1, 2, 3),
        [vm((length, width), low)] * 2
        + [vm((2, dp_count, rows // 2, half), low)] * 2
        + [vm((length, units), low)] * 2
        + [vm(pack.shape, low), vm(pack.shape[1:], low)]
        + exchange_scratch(count, width) * 2
        + semaphores(3, 1)
        + [pltpu.SemaphoreType.DMA((2, 10)), pltpu.SemaphoreType.DMA((2, 1))],
        3 * 10**10,
    )


def ff_backward(s, grad, middle, par, lengths, pack, second, value, slope, earlier, results):
    count, width = grad.shape
    _, dp_count, rows, half = pack.shape
    length, units = value.shape
    vm = pltpu.VMEM
    weights = [vm((2, dp_count, rows // 2, half), low)] * 2
    return run_kernel(
        partial(ff_backward_kernel, s),
        "ff_backward",
        5,
        (grad, middle, par, lengths, pack, second, value, slope, earlier, *results),
        (0, 1, 2, 9, 10),
        [
            (pack.shape[1:], low),
            ((count, width), f32),
            ((2, width), f32),
            (earlier.shape[1:], low),
            ((2, count, width), f32),
        ],
        (1, 2, 3),
        [vm((length, width), low)]
        + weights
        + [vm((length, width), low)]
        + [vm((length, units), low)] * 3
        + [vm(pack.shape, low), vm(pack.shape[1:], low)]
        + exchange_scratch(count, width)
        + semaphores(5, 1)
        + plane_sum_scratch(earlier)
        + [pltpu.SemaphoreType.DMA((2, 1))]
        + exchange_semaphores(1),
        2 * 10**10,
    )


def mixer_backward(
    s, grad, x, par, small, embedding, late, lengths, pack, waves, back, kept, earlier
):
    normed, proj, streams, prod, spec, filtered, gated, filt, *network = kept
    count, width = grad.shape
    length, chans = prod.shape
    knots = network[0].shape[1]
    vm = pltpu.VMEM
    weights = mixer_weights_scratch(pack, width)
    return run_kernel(
        partial(mixer_backward_kernel, s),
        "mixer_backward",
        7 + s,
        (grad, x, par, small, embedding, late, lengths, pack, filt, waves, back, normed, proj,
         streams, prod, spec, filtered, gated, *network, earlier),
        range(6),
        [
            (pack.shape[1:], low),
            (small.shape[1:], f32),
            ((count, width), f32),
            (earlier.shape[1:], low),
        ],
        (1, 2, 3),
        [vm((length, width), low)]
        + weights
        + [
            vm((2 * length, chans), f32),
            vm((2 * length, length), low),
            vm((length, 2 * length), low),
            vm((length, width), low),
            vm((length, 3 * chans), low),
            vm((length, 3 * chans), low),
            vm((length, chans), low),
            vm((2 * length, chans), low),
            vm((length, chans), f32),
            vm((length, chans), low),
            vm((length, chans), low),
            vm((length, chans), low),
            vm((2 * length, chans), low),
            vm((2 * length, chans), low),
            vm((2 * length, chans), f32),
            vm((length, chans), f32),
            vm((length + 8, 3 * chans), f32),
            vm((length, 3 * chans), low),
        ]
        + weights
        + [vm(item.shape[1:], low) for item in weights]
        + [vm((length, knots), f32)] * 4
        + [vm((2, width), f32), vm((24, 3 * chans), f32)]
        + exchange_scratch(count, width)
        + semaphores(19, 5)
        + plane_sum_scratch(earlier)
        + [pltpu.SemaphoreType.DMA((2, 2))],
        2 * 10**10,
    )


def shuffle_stage(w_in, w_out, w_up, stage_in, stage_out, stage_up):
    depth, chans = w_in.shape[0], w_out.shape[1] // 4
    count = lax.axis_size("dp")
    half_in = stage_in.shape[3]
    piece = chans // count
    for h in range(2):
        for j in range(4):
            for c in range(0, half_in, 2 * piece):
                pair = []
                for col in (c, c + piece):
                    g, d = divmod((h * half_in + col) // piece, count)
                    at = ((g * count + d) * 4 + j) * piece
                    pair.append(w_in[:, at : at + piece].astype(f32))
                stage_in[h, j, :, c : c + 2 * piece] = jnp.concatenate(pair, 1).astype(low)
            for d in range(2):
                at = ((2 * h + d) * 4 + j) * chans
                stage_up[h, j, :, d * chans : (d + 1) * chans] = w_up[:, at : at + chans]
    part = half_in // 3
    for h in range(2):
        for q in range(4):
            at = (h * 4 + q) * part
            stage_out[h, q * depth : (q + 1) * depth, :] = w_out[:, at : at + part]


def parameters_stage(me, par, small, gain, shift, taps, first, second, last, direct, rates):
    chans = small.shape[1]
    count = lax.axis_size("dp")
    piece = chans // count
    width = last.shape[2]
    par[0:1, :] = gain[0, 0:1, :]
    par[1:2, :] = shift[0, 0:1, :]
    par[2:3, :] = gain[0, 1:2, :]
    par[3:4, :] = shift[0, 1:2, :]
    par[4:8, :] = jnp.zeros((4, width), f32)
    small[64:160, :] = jnp.zeros((96, chans), f32)
    small[64:128, 0:64] = second[0]
    for row in range(first.shape[0]):
        small[64 + row : 65 + row, 128:192] = first[row]
    for j in range(4):

        @pl.when(me == j)
        def _():
            for d in range(0, count, 2):
                cols = slice(d * piece, (d + 2) * piece)

                def picked(ref, rows, base=0):
                    at = [base + ((d + k) * 4 + j) * piece for k in range(2)]
                    return jnp.concatenate([ref[rows, a : a + piece] for a in at], 1)

                small[0:64, cols] = picked(last.at[0], slice(0, 64))
                for g in range(3):
                    for tap in range(3):
                        row = 144 + 3 * g + tap
                        small[row : row + 1, cols] = picked(
                            taps.at[tap], slice(0, 1), g * width
                        )
                small[153:154, cols] = picked(direct, slice(0, 1))
                small[154:155, cols] = picked(rates, slice(0, 1))


def shuffle_send(section, me, targets, sources, parts, parameters, sems):
    stage_in, stage_out, stage_up, w_down = sources
    mixer_parts, ff_parts = parts
    in_sems, out_sems, up_sems, down_sems, par_sems, small_sems = sems
    depth, half_in = stage_in.shape[2:]
    half = stage_up.shape[3]
    copies = [
        remote_to(item.at[section], item.at[section], at, 0, other_core())
        for item, at in zip(parameters, (par_sems, small_sems))
    ]
    for e, (t, seq, device) in enumerate(targets):
        target = mixer_parts.at[section, rows_of(me, depth), pl.ds(0, half_in)]
        copies.append(remote_to(stage_in.at[t, seq], target, in_sems, e, device))
    target = mixer_parts.at[section, :, pl.ds(half_in, half_in // 3)]
    copies.append(remote_to(stage_out.at[1 - section], target, out_sems, 0, other_core()))
    for e, (t, seq, device) in enumerate(targets):
        target = ff_parts.at[section, rows_of(me, depth), :]
        copies.append(remote_to(stage_up.at[t, seq], target, up_sems, e, device))
    cols = pl.ds(pl.multiple_of((1 - section) * half, half), half)
    target = ff_parts.at[section, pl.ds(4 * depth, 4 * depth), :]
    copies.append(remote_to(w_down.at[:, cols], target, down_sems, 0, other_core()))
    for copy in copies:
        copy.start()
    mixer_parts[section, rows_of(me, depth), 0:half_in] = stage_in[section, me]
    mixer_parts[section, :, half_in:] = stage_out[section]
    ff_parts[section, rows_of(me, depth), :] = stage_up[section, me]
    cols = pl.ds(pl.multiple_of(section * half, half), half)
    ff_parts[section, 4 * depth : 8 * depth, :] = w_down[:, cols]
    return copies


def shuffle_wait_mixer(section, me, targets, parts, stage_in, in_sems, out_sems):
    depth, half_in = stage_in.shape[2:]
    for e, (t, seq, device) in enumerate(targets):
        block = parts.at[t, rows_of(seq, depth), pl.ds(0, half_in)]
        remote_to(block, block, in_sems, e, device).wait_recv()
    block = parts.at[1 - section, :, pl.ds(half_in, half_in // 3)]
    remote_to(block, block, out_sems, 0, other_core()).wait_recv()


def shuffle_wait_ff(section, me, targets, parts, stage_up, up_sems, down_sems):
    depth = stage_up.shape[2]
    for e, (t, seq, device) in enumerate(targets):
        block = parts.at[t, rows_of(seq, depth), :]
        remote_to(block, block, up_sems, e, device).wait_recv()
    block = parts.at[1 - section, pl.ds(4 * depth, 4 * depth), :]
    remote_to(block, block, down_sems, 0, other_core()).wait_recv()


def shuffle_targets(section, me, peers):
    targets = [(section, peer, {"seq": peer}) for peer in peers]
    targets.append((1 - section, me, other_core()))
    targets += [(1 - section, peer, {**other_core(), "seq": peer}) for peer in peers]
    return targets


def finish_kernel(
    vec0, vec1, mixer0, mixer1, ff0, ff1, grad0, grad1,
    input_grads, got_in, got_out, got_up, got_down, vec_out,
    mine0, arrived0, plane_sems0, sum_sems0, mine1, arrived1, plane_sems1, sum_sems1,
    vec_other, vec_sum, vec_arrived, vec_all, stage_mixer, stage_ff, own_sems, load_sems,
    layer_sems, keep_sems, vec_core_sems, vec_sum_sems, vec_plane_sems, vec_seq_sems, in_sems, out_sems, up_sems, down_sems,
):
    section = lax.axis_index("section")
    me = lax.axis_index("seq")
    here, near, far = along_planes()
    planes = (near, far, (near + 2) % 4)
    peers = neighbours(me)
    depth, half_in = got_in.shape[2:]
    targets = shuffle_targets(section, me, peers)
    greeted = greet([device for _, _, device in targets] + [{"dp": plane} for plane in planes])
    middle = mixer0.shape[2] // 2
    chunks = (pl.ds(0, middle), pl.ds(middle, middle))
    in_cols = (pl.ds(0, middle), pl.ds(middle, half_in - middle))

    def columns(e, at):
        t, seq, device = targets[e]
        return remote_to(
            stage_mixer.at[t, rows_of(seq, depth), in_cols[at]],
            got_in.at[section, me, :, in_cols[at]],
            in_sems,
            2 * e + at,
            device,
        )

    out_columns = remote_to(
        stage_mixer.at[1 - section, :, pl.ds(half_in, half_in // 3)], got_out.at[section], out_sems,
        0, other_core(),
    )

    def send_layer(s, at):
        for index in range(2):

            @pl.when(section == index)
            def _():
                for e in range(3) if index == s else range(3, 7):
                    columns(e, at).start()
                if at == 1 and index != s:
                    out_columns.start()

    all_here(greeted)
    for index, vec in enumerate((vec1, vec0)):

        @pl.when(section == index)
        def _():
            remote_to(vec, vec_other, vec_core_sems, 0, other_core()).start()

    sends = []
    vec_swap = remote_to(vec_other, vec_other, vec_core_sems, 0, other_core())
    vec_swap.wait_recv()
    sends.append(vec_swap)

    @pl.when(section == 0)
    def _():
        vec_sum[...] = vec0[...] + vec_other[...]

    @pl.when(section == 1)
    def _():
        vec_sum[...] = vec1[...] + vec_other[...]

    count = 4
    chunk = vec_sum.shape[0] // count
    moves = [
        remote_to(
            vec_sum.at[rows_of(plane, chunk)], vec_arrived.at[slot], vec_sum_sems, slot,
            {"dp": plane},
        )
        for slot, plane in enumerate(planes)
    ]
    for copy in moves:
        copy.start()
    sends += moves
    plane_sums = [
        PlaneSum(mixer0.at[:, :, chunks[0]], mine0, arrived0, plane_sems0, sum_sems0),
        PlaneSum(mixer0.at[:, :, chunks[1]], mine1, arrived1, plane_sems1, sum_sems1),
    ]
    for plane_sum in plane_sums:
        plane_sum.begin()
    loads = fetch(
        [(ff0, stage_ff.at[0]), (ff1, stage_ff.at[1]), (mixer1, stage_mixer.at[1])], load_sems
    )
    by_layer(True, ((grad0, grad1, input_grads),), layer_sems, keep_sems)
    for load in loads:
        load.wait()
    ups = []
    for e, (t, seq, device) in enumerate(targets):
        ups.append(
            remote_to(
                stage_ff.at[t, rows_of(seq, depth), :], got_up.at[section, me], up_sems, e, device
            )
        )
    downs = [
        remote_to(
            stage_ff.at[1 - section, pl.ds(4 * depth, 4 * depth), :], got_down.at[section],
            down_sems, 0, other_core(),
        )
    ]
    for copy in ups + downs:
        copy.start()
    sends += ups + downs
    send_layer(1, 0)
    send_layer(1, 1)
    keeps = fetch(
        [
            (stage_ff.at[section, rows_of(me, depth), :], got_up.at[section, me]),
            (stage_ff.at[section, pl.ds(4 * depth, 4 * depth), :], got_down.at[section]),
        ],
        own_sems,
    )

    for copy in moves:
        copy.wait_recv()
    own_chunk = rows_of(here, chunk)
    total = vec_sum[own_chunk, :]
    for slot in range(len(planes)):
        total = total + vec_arrived[slot]
    vec_all[me, own_chunk, :] = total
    moves = [
        remote_to(
            vec_all.at[me, own_chunk], vec_all.at[me, own_chunk], vec_plane_sems, slot,
            {"dp": plane},
        )
        for slot, plane in enumerate(planes)
    ]
    for copy in moves:
        copy.start()
    sends += moves
    for plane_sum in plane_sums:
        plane_sum.forward()
    for slot, plane in enumerate(planes):
        block = vec_all.at[me, rows_of(plane, chunk)]
        remote_to(block, block, vec_plane_sems, slot, {"dp": plane}).wait_recv()
    moves = [
        remote(vec_all.at[me], vec_all.at[me], vec_seq_sems, slot, peer)
        for slot, peer in enumerate(peers)
    ]
    for copy in moves:
        copy.start()
    sends += moves

    for at, plane_sum in enumerate(plane_sums):
        plane_sum.end(stage_mixer.at[0, :, chunks[at]])
        sends += plane_sum.sends
        send_layer(0, at)
    sends += [columns(e, at) for e in range(7) for at in range(2)] + [out_columns]
    keeps += fetch(
        [
            (
                stage_mixer.at[section, rows_of(me, depth), pl.ds(0, half_in)],
                got_in.at[section, me],
            ),
            (stage_mixer.at[section, :, pl.ds(half_in, half_in // 3)], got_out.at[section]),
        ],
        own_sems,
        2,
    )
    for slot, peer in enumerate(peers):
        block = vec_all.at[peer]
        remote(block, block, vec_seq_sems, slot, peer).wait_recv()
    keeps += fetch([(vec_all, vec_out)], own_sems, 4)
    for e, (t, seq, device) in enumerate(targets):
        block = got_up.at[t, seq]
        remote_to(block, block, up_sems, e, device).wait_recv()
        for at in range(2):
            block = got_in.at[t, seq, :, in_cols[at]]
            remote_to(block, block, in_sems, 2 * e + at, device).wait_recv()
    downs[0].wait_recv()
    out_columns.wait_recv()
    by_layer(False, ((grad0, grad1, input_grads),), layer_sems, keep_sems)
    for copy in sends:
        copy.wait_send()
    for keep in keeps:
        keep.wait()


def unpack_kernel(
    blocks, grads, got_in, got_out, got_up, got_down, vec_all,
    block_outputs, input_grads, g_in, g_out, g_up, g_down, g_gain, g_bias, g_taps, g_first,
    g_second, g_last, g_direct,
    stage_blocks, stage_grads, load_sems, copy_sems,
):
    loads = fetch([(blocks, stage_blocks), (grads, stage_grads)], load_sems)
    depth = g_in.shape[0]
    half_in, half_up = got_in.shape[3], got_up.shape[3]
    chans = vec_all.shape[2]
    count = 4
    piece = chans // count
    for j in range(4):
        for d in range(count):
            at = (d * 4 + j) * chans
            h, col = divmod(d * chans, half_up)
            g_up[:, at : at + chans] = got_up[h, j, :, col : col + chans].astype(f32)
    for h in range(2):
        g_down[:, h * half_up : (h + 1) * half_up] = got_down[h].astype(f32)
    for load in loads:
        load.wait()
    copies = fetch([(stage_blocks, block_outputs), (stage_grads, input_grads)], copy_sems)
    for g in range(3):
        for d in range(count):
            h, col = divmod(g * chans + d * piece, half_in)
            for j in range(0, 4, 2):
                at = ((g * count + d) * 4 + j) * piece
                g_in[:, at : at + 2 * piece] = jnp.concatenate(
                    [got_in[h, j + k, :, col : col + piece].astype(f32) for k in range(2)], 1
                )
    part = half_in // 3
    for h in range(2):
        for q in range(4):
            at = (h * 4 + q) * part
            g_out[:, at : at + part] = got_out[h, q * depth : (q + 1) * depth, :].astype(f32)
    first = sum_of(vec_all, slice(64, 64 + g_first.shape[0]), slice(128, 192))
    for row in range(g_first.shape[0]):
        g_first[row] = first[row : row + 1]
    g_second[...] = sum_of(vec_all, slice(64, 128), slice(0, 64))
    for q in range(4):
        cols = slice(q * chans, (q + 1) * chans)
        early = sum_of(vec_all, slice(128 + 2 * q, 130 + 2 * q), slice(None))
        late = sum_of(vec_all, slice(136 + 2 * q, 138 + 2 * q), slice(None))
        g_gain[0:1, cols] = early[0:1]
        g_gain[1:2, cols] = late[0:1]
        g_bias[0:1, cols] = early[1:2]
        g_bias[1:2, cols] = late[1:2]
    for d in range(count):
        cols = slice(d * piece, (d + 1) * piece)
        for j in range(0, 4, 2):
            at = (d * 4 + j) * piece
            pair = slice(at, at + 2 * piece)

            def joined(rows):
                return jnp.concatenate([vec_all[j, rows, cols], vec_all[j + 1, rows, cols]], 1)

            g_last[:, pair] = joined(slice(0, 64))
            for g in range(3):
                for tap in range(3):
                    row = 144 + 3 * g + tap
                    start = g * 4 * chans + at
                    g_taps[tap, :, start : start + 2 * piece] = joined(slice(row, row + 1))
            g_direct[:, pair] = joined(slice(153, 154))

    for copy in copies:
        copy.wait()


def sum_of(blocks, rows, cols):
    return (blocks[0, rows, cols] + blocks[1, rows, cols]) + (
        blocks[2, rows, cols] + blocks[3, rows, cols]
    )


def finish(vec0, vec1, mixer0, mixer1, ff0, ff1, grad0, grad1):
    count, width = grad0.shape
    dp_count, rows, half = mixer0.shape
    depth = rows // 4
    chans = vec0.shape[1]
    half_in = 3 * chans // 2
    vm, dma = pltpu.VMEM, pltpu.SemaphoreType.DMA
    vec_rows = vec0.shape[0]
    chunk = jax.ShapeDtypeStruct((dp_count, rows, half // 2), low)
    return run_kernel(
        finish_kernel,
        "finish",
        10,
        (vec0, vec1, mixer0, mixer1, ff0, ff1, grad0, grad1),
        (0, 1, 6, 7),
        [
            ((2, count, width), f32),
            ((2, 4, depth, half_in), low),
            ((2, rows, half_in // 3), low),
            ((2, 4, depth, half), low),
            ((2, rows, half), low),
            ((4, vec_rows, chans), f32),
        ],
        (),
        plane_sum_scratch(chunk)
        + plane_sum_scratch(chunk)
        + [
            vm((vec_rows, chans), f32),
            vm((vec_rows, chans), f32),
            vm((3, vec_rows // 4, chans), f32),
            vm((4, vec_rows, chans), f32),
            vm((2, *mixer1.shape), low),
            vm((2, *ff1.shape), low),
            dma((5,)),
            dma((3,)),
            *exchange_semaphores(1),
            dma((2, 1)),
            dma((2, 3)),
            dma((2, 3)),
            dma((2, 3)),
            dma((2, 14)),
            dma((2, 1)),
            dma((2, 7)),
            dma((2, 1)),
        ],
        10**9,
    )


def unpack(blocks, grads, got, first_shape):
    width = blocks.shape[2]
    depth = got[0].shape[2]
    units = 4 * 2 * got[2].shape[3]
    knots = first_shape[1]
    inside = pl.BlockSpec(memory_space=pltpu.VMEM)
    outside = pl.BlockSpec(memory_space=pl.ANY)
    shapes = (
        blocks.shape, grads.shape, (depth, 3 * width), (depth, width), (depth, units),
        (4 * depth, width), (2, width), (2, width), (3, 1, 3 * width),
        (first_shape[0], 1, knots), (knots, knots),
        (knots, width), (1, width),
    )
    return pl.pallas_call(
        unpack_kernel,
        out_shape=[jax.ShapeDtypeStruct(shape, f32) for shape in shapes],
        in_specs=[outside] * 2 + [inside] * 5,
        out_specs=[outside] * 2 + [inside] * 11,
        scratch_shapes=[
            pltpu.VMEM(blocks.shape, f32),
            pltpu.VMEM(grads.shape, f32),
            pltpu.SemaphoreType.DMA((2,)),
            pltpu.SemaphoreType.DMA((2,)),
        ],
        compiler_params=pltpu.CompilerParams(vmem_limit_bytes=56 * 2**20),
        name="unpack",
    )(blocks, grads, *got)


def any_device(
    tokens,
    cotangent,
    lengths,
    norm_gain,
    norm_bias,
    mixer_in,
    short_kernel,
    filter_first,
    filter_second,
    filter_last,
    filter_bias,
    decay_rates,
    mixer_out,
    up_weight,
    down_weight,
):
    section = lax.axis_index("section")
    seq_index = lax.axis_index("seq")
    seq_count = lax.axis_size("seq")
    dp_count = lax.axis_size("dp")
    own_layer_first = section == 0
    local_len = tokens.shape[2]
    width = tokens.shape[3]
    hidden = up_weight.shape[2]
    row_len = local_len * seq_count
    chans = width // seq_count
    units = hidden // seq_count

    def share_columns(block, groups):
        rows = block.shape[0]
        inner = block.shape[1] // (groups * dp_count * seq_count)
        split = block.reshape(rows, groups, dp_count, seq_count, inner)
        split = jnp.transpose(split, (3, 0, 1, 2, 4))
        moved = lax.all_to_all(split, "seq", split_axis=0, concat_axis=0, tiled=True)
        return moved.reshape(seq_count * rows, groups * dp_count * inner)

    def unshare_columns(block, groups):
        rows = block.shape[0] // seq_count
        inner = block.shape[1] // (groups * dp_count)
        split = block.reshape(seq_count, rows, groups, dp_count, inner)
        moved = lax.all_to_all(split, "seq", split_axis=0, concat_axis=0, tiled=True)
        moved = jnp.transpose(moved, (1, 2, 3, 0, 4))
        return moved.reshape(rows, groups * dp_count * seq_count * inner)

    def gathered(block):
        whole = lax.all_gather(block, ("section", "dp"))
        return whole.reshape(2, dp_count * block.shape[0], block.shape[1])

    weights = (
        gathered(share_columns(mixer_in[0], 3)),
        gathered(mixer_out[0]),
        gathered(share_columns(up_weight[0], 1)),
        gathered(down_weight[0]),
    )

    def both(value):
        return lax.all_gather(value[0], "section")

    gains, shifts = both(norm_gain), both(norm_bias)
    taps, first_w, second_w = both(short_kernel), both(filter_first), both(filter_second)
    last_w, direct, rates = both(filter_last), both(filter_bias), both(decay_rates)

    def mine(value):
        lead = value.shape[:-1]
        split = value.reshape(*lead, dp_count, seq_count, -1)
        picked = lax.dynamic_index_in_dim(split, seq_index, len(lead) + 1, False)
        return picked.reshape(*lead, chans)

    def placed(value):
        lead = value.shape[:-1]
        split = value.reshape(*lead, dp_count, 1, -1)
        inner = split.shape[-1]
        empty = jnp.zeros((*lead, dp_count, seq_count, inner), value.dtype)
        at = [0] * len(lead) + [0, seq_index, 0]
        return lax.dynamic_update_slice(empty, split, at).reshape(*lead, width)

    waves = jnp.asarray(wave_tables(row_len))
    waves_back = waves

    def to_waves(x):
        both_parts = mm(waves, x)
        return both_parts[:row_len], both_parts[row_len:]

    def from_waves(cos_part, sin_part):
        joined = jnp.concatenate([cos_part, sin_part], 0).astype(low)
        return t_mm(waves_back, joined) * (1.0 / row_len)

    def ag(x):
        return lax.all_gather(x, "seq", axis=0, tiled=True)

    def rs(x):
        return lax.psum_scatter(x.astype(low), "seq", scatter_dimension=0, tiled=True).astype(f32)

    length_now = lax.dynamic_index_in_dim(lengths, section, 0, False)[0]
    positions = seq_index * local_len + jnp.arange(local_len)
    mask = (positions < length_now).astype(f32)[:, None]
    row_mask = (jnp.arange(row_len) < length_now).astype(f32)[:, None]
    own_tokens = lax.dynamic_index_in_dim(tokens, section, 0, False)[0].astype(f32)
    own_cotangent = lax.dynamic_index_in_dim(cotangent, section, 0, False)[0].astype(f32)

    def layer_forward(s, inputs):
        w_in, w_out, w_up, w_down = [w[s] for w in weights]
        kernel = mine(taps[s].reshape(3, 3, width))
        last_mine, direct_mine, rates_mine = mine(last_w[s]), mine(direct[s]), mine(rates[s])

        def own_filter(a, b, c):
            return filter_taps(a, b, c, rates_mine, row_len)

        filter_rows, filter_back = jax.vjp(own_filter, first_w[s], second_w[s], last_mine)
        filt_cos, filt_sin = to_waves(filter_rows.astype(low))
        normed = (norm_stats(inputs)[0] * gains[s, 0] + shifts[s, 0]).astype(low)
        normed = ag(normed)
        projected = [mm(normed, w_in[:, g * chans : (g + 1) * chans]) for g in range(3)]
        streams = [
            (
                kernel[0, g] * projected[g]
                + kernel[1, g] * shifted(projected[g], 1)
                + kernel[2, g] * shifted(projected[g], 2)
            ).astype(low)
            for g in range(3)
        ]
        wide = [x.astype(f32) for x in streams]
        product = (wide[0] * wide[2] * row_mask).astype(low)
        prod_cos, prod_sin = to_waves(product)
        filtered = from_waves(
            prod_cos * filt_cos - prod_sin * filt_sin, prod_cos * filt_sin + prod_sin * filt_cos
        ) + direct_mine * product.astype(f32)
        gated = (wide[1] * filtered).astype(low)
        middle = inputs + mask * rs(mm(gated, w_out))
        second = (norm_stats(middle)[0] * gains[s, 1] + shifts[s, 1]).astype(low)
        second = ag(second)
        value, slope = gelu_both(mm(second, w_up))
        value = value.astype(low)
        slope = slope.astype(low)
        result = middle + mask * rs(mm(value, w_down))
        saved = (
            inputs, normed, projected, wide, product, prod_cos, prod_sin, filt_cos, filt_sin,
            filtered, gated, middle, second, value, slope, kernel, direct_mine, filter_back,
        )
        return result, saved

    def layer_backward(s, grad, saved):
        w_in, w_out, w_up, w_down = [w[s] for w in weights]
        (
            inputs, normed, projected, wide, product, prod_cos, prod_sin, filt_cos, filt_sin,
            filtered, gated, middle, second, value, slope, kernel, direct_mine, filter_back,
        ) = saved
        out_low = ag((grad * mask).astype(low))
        pre = (mm_t(out_low, w_down) * slope.astype(f32)).astype(low)
        grad_down = t_mm(value, out_low)
        grad_up = t_mm(second, pre)
        mid_part, gain_late, bias_late = norm_back(rs(mm_t(pre, w_up)), middle, gains[s, 1])
        middle_grad = grad + mid_part
        branch = ag((middle_grad * mask).astype(low))
        gated_grad = mm_t(branch, w_out).astype(low)
        grad_out = t_mm(gated, branch)
        gated_grad = gated_grad.astype(f32)
        filtered_grad = (gated_grad * wide[1]).astype(low)
        fg_cos, fg_sin = to_waves(filtered_grad)
        fg_wide = filtered_grad.astype(f32)
        prod32 = product.astype(f32)
        product_grad = from_waves(
            filt_cos * fg_cos + filt_sin * fg_sin, filt_cos * fg_sin - filt_sin * fg_cos
        ) + direct_mine * fg_wide
        product_grad = product_grad.astype(low).astype(f32)
        filter_grad = from_waves(
            prod_cos * fg_cos + prod_sin * fg_sin, prod_cos * fg_sin - prod_sin * fg_cos
        )
        grad_first, grad_second, grad_last = filter_back(filter_grad)
        grad_direct = jnp.sum(fg_wide * prod32, 0)
        mixed = [
            (product_grad * wide[2]).astype(low).astype(f32),
            (gated_grad * filtered).astype(low).astype(f32),
            (product_grad * wide[0]).astype(low).astype(f32),
        ]
        proj = [
            (
                kernel[0, g] * mixed[g]
                + kernel[1, g] * shifted(mixed[g], -1)
                + kernel[2, g] * shifted(mixed[g], -2)
            ).astype(low)
            for g in range(3)
        ]
        grad_taps = jnp.stack(
            [
                jnp.stack(
                    [jnp.sum(mixed[g] * (shifted(projected[g], k) if k else projected[g]), 0) for g in range(3)]
                )
                for k in range(3)
            ]
        )
        proj = jnp.concatenate(proj, 1)
        grad_in = t_mm(normed, proj)
        in_part, gain_early, bias_early = norm_back(rs(mm_t(proj, w_in)), inputs, gains[s, 0])
        small = (
            jnp.stack([gain_early, gain_late]),
            jnp.stack([bias_early, bias_late]),
            placed(grad_taps).reshape(3, 3 * width),
            grad_first,
            grad_second,
            placed(grad_last),
            placed(grad_direct),
        )
        large = (grad_in, grad_out, grad_up, grad_down)
        return middle_grad + in_part, small, large

    first_out, first_saved = layer_forward(0, own_tokens)
    second_out, second_saved = layer_forward(1, first_out)
    second_grad, second_small, second_large = layer_backward(1, own_cotangent, second_saved)
    first_grad, first_small, first_large = layer_backward(0, second_grad, first_saved)

    swap = [(0, 1), (1, 0)]

    def by_layer(first, second):
        other = lax.ppermute(jnp.where(own_layer_first, second, first), "section", swap)
        return jnp.where(
            own_layer_first, jnp.stack([first, other]), jnp.stack([other, second])
        )[None, :, None]

    def summed(first, second):
        stacked = jnp.stack([first, second]).astype(low)
        rows = first.shape[0] // dp_count
        stacked = stacked.reshape(2 * dp_count, rows, first.shape[1])
        return lax.psum_scatter(stacked, ("section", "dp"), scatter_dimension=0, tiled=True)[0]

    sums = [summed(a, b) for a, b in zip(first_large, second_large)]
    sum_in = unshare_columns(sums[0], 3).astype(f32)
    sum_out = sums[1].astype(f32)
    sum_up = unshare_columns(sums[2], 1).astype(f32)
    sum_down = sums[3].astype(f32)
    stacked = jax.tree.map(lambda a, b: jnp.stack([a, b]), first_small, second_small)
    small = lax.psum(stacked, ("section", "dp", "seq"))
    small = [lax.dynamic_slice_in_dim(x, section, 1, 0) for x in small]
    sum_gain, sum_bias, sum_taps, sum_first, sum_second, sum_last, sum_direct = small
    return (
        by_layer(first_out, second_out),
        by_layer(first_grad, second_grad),
        sum_gain,
        sum_bias,
        sum_in[None],
        sum_taps,
        sum_first,
        sum_second,
        sum_last,
        sum_direct,
        sum_out[None],
        sum_up[None],
        sum_down[None],
    )


def plane_device(
    tokens,
    cotangent,
    lengths,
    norm_gain,
    norm_bias,
    mixer_in,
    short_kernel,
    filter_first,
    filter_second,
    filter_last,
    filter_bias,
    decay_rates,
    mixer_out,
    up_weight,
    down_weight,
):
    section = lax.axis_index("section")
    seq_count = lax.axis_size("seq")
    dp_count = lax.axis_size("dp")
    row_len = tokens.shape[2] * seq_count
    lengths = jnp.transpose(lengths)
    short_kernel = jnp.transpose(short_kernel, (1, 0, 2))
    filter_first = jnp.transpose(filter_first, (1, 0, 2))

    def gathered(part):
        whole = lax.all_gather(part, ("section", "dp"))
        return whole.reshape(2, dp_count, *part.shape)

    tables = wave_tables(row_len)
    waves = jnp.asarray(tables)
    waves_back = jnp.asarray(np.ascontiguousarray(tables.T))
    embedding = jnp.asarray(np.pad(position_rows(row_len), ((0, 0), (0, 95))))

    weights = (
        mixer_in[0], mixer_out[0], up_weight[0], down_weight[0], norm_gain, norm_bias, short_kernel,
        filter_first, filter_second, filter_last, filter_bias, decay_rates,
    )
    (
        first_mixer_pack, first_ff_pack, cotangent_low, par, small, second_mixer_pack, ff_part,
        *outs,
    ) = mixer_forward(
        0, tokens, lengths, weights, waves, waves_back, (cotangent, embedding)
    )
    first_filter, second_filter, first_saved, outs = outs[:5], outs[5:10], outs[10:13], outs[13:]
    first_out, *first_kept, first_middle = outs
    second_ff_pack = gathered(ff_part)
    *second_kept, second_middle = mixer_forward(
        1, first_out, lengths, (par, small, second_mixer_pack, second_filter[0]), waves, waves_back,
        None,
    )
    first_kept, second_kept = [*first_kept, *first_filter], [*second_kept, *second_filter]
    second_ff, second_out, middle_grad, late = ff_turn(
        1, cotangent, second_middle, par, lengths, second_ff_pack, cotangent_low
    )

    def mixer_back(s, grad, x, late, pack, kept, earlier):
        return mixer_backward(
            s, grad, x, par, small, embedding, late, lengths, pack, waves, waves_back, kept, earlier
        )

    second_mixer, second_vec, second_grad, second_ff = mixer_back(
        1, middle_grad, first_out, late, second_mixer_pack, second_kept, second_ff
    )
    first_ff, middle_grad, late, second_mixer, block_outputs = ff_backward(
        0, second_grad, first_middle, par, lengths, first_ff_pack, *first_saved, second_mixer,
        (first_out, second_out),
    )
    first_mixer, first_vec, first_grad, first_ff = mixer_back(
        0, middle_grad, tokens, late, first_mixer_pack, first_kept, first_ff
    )
    input_grads, *got = finish(
        first_vec, second_vec, first_mixer, second_mixer, first_ff, second_ff, first_grad,
        second_grad,
    )
    (
        block_outputs, input_grads, sum_in, sum_out, sum_up, sum_down, sum_gain, sum_bias, sum_taps,
        sum_first, sum_second, sum_last, sum_direct,
    ) = unpack(block_outputs, input_grads, got, filter_first.shape[::2])
    return (
        block_outputs[None, :, None],
        input_grads[None, :, None],
        sum_gain[None],
        sum_bias[None],
        sum_in[None],
        jnp.transpose(sum_taps, (1, 0, 2)),
        jnp.transpose(sum_first, (1, 0, 2)),
        sum_second[None],
        sum_last[None],
        sum_direct,
        sum_out[None],
        sum_up[None],
        sum_down[None],
    )


def solution(mesh):
    in_specs = (
        P(None, "dp", "seq", None),
        P(None, "dp", "seq", None),
        P(None, "dp"),
        P("section", None, None),
        P("section", None, None),
        P("section", ("dp", "seq"), None),
        P("section", None, None),
        P("section", None, None),
        P("section", None, None),
        P("section", None, None),
        P("section", None),
        P("section", None),
        P("section", ("dp", "seq"), None),
        P("section", ("dp", "seq"), None),
        P("section", ("dp", "seq"), None),
    )
    out_specs = (
        P("section", None, "dp", "seq", None),
        P("section", None, "dp", "seq", None),
        P("section", None, None),
        P("section", None, None),
        P("section", ("dp", "seq"), None),
        P("section", None, None),
        P("section", None, None),
        P("section", None, None),
        P("section", None, None),
        P("section", None),
        P("section", ("dp", "seq"), None),
        P("section", ("dp", "seq"), None),
        P("section", ("dp", "seq"), None),
    )
    planes = mesh.shape["seq"] == 4 and mesh.shape["dp"] == 4
    per_device = plane_device if planes else any_device
    return jax.shard_map(
        per_device, mesh=mesh, in_specs=in_specs, out_specs=out_specs, check_vma=False
    )
```

time: 2780 us -> 432 us (0.16)
  waiting for transfers between devices: 1530 us -> 0.04 us
  matrix products: 749 us -> 0 us
  Pallas kernels: 0 us -> 410 us
  local copies, waits for them, and re-layouts: 216 us -> 0 us
  other arithmetic: 134 us -> 0 us
  starting transfers between devices: 117 us -> 0.04 us
    reduce_scatter x4 -> x0, waiting for transfers between devices: 1010 us -> none  [the longest x1 355 us: per_device(): lax.psum_scatter(acc_down, ('dp', 'seq'), scatter_dimension=0, tiled=True)]
    dot_general x184 -> x0, matrix products: 749 us -> none  [the longest x9 65 us: from_spectrum(): jnp.einsum('nk,ckm->cnm', lead_sin, turned_im, precision=precise)]
    pallas_call x0 -> x8, Pallas kernels: none -> 410 us  [the longest x7 402 us: run_kernel(): pl.pallas_call(kernel, out_shape=[jax.ShapeDtypeStruct(shape, kind) for s...]
    all_gather x4 -> x1, waiting for transfers between devices: 245 us -> 0.02 us  [gathered(): whole = lax.all_gather(part, ('section', 'dp'))]
    psum x2 -> x0, waiting for transfers between devices: 134 us -> none  [per_device(): lax.psum((acc_gain, acc_bias, acc_kernel, acc_first, acc_second, full_las...]
    all_to_all x18 -> x0, waiting for transfers between devices: 132 us -> none  [the longest x6 72 us: layer_forward(): lax.all_to_all(arranged, 'seq', split_axis=1, concat_axis=2, tiled=True)]
    all_to_all x18 -> x0, starting transfers between devices: 83.4 us -> none  [the longest x6 28.4 us: layer_forward(): lax.all_to_all(arranged, 'seq', split_axis=1, concat_axis=2, tiled=True)]
    reduce_sum x26 -> x0, other arithmetic: 61.2 us -> none  [the longest x3 40.4 us: per_device(): jnp.sum(mixed_grad * earlier[1:-1], 0)]
  transfers between devices with their start and end apart: 41 -> 1, of which waited for: 23 -> 0; matrix products, arithmetic and copies ran while one was open for 25% -> 0% of each run, Pallas kernels for 0% -> 11%
where the time goes in v1:
time: 432 us; the launch traced here: 425 us
  Pallas kernels  410 us (95%)
  between operations  14.6 us (3%)
    pallas_call x7, Pallas kernels, run_kernel(): pl.pallas_call(kernel, out_shape=[jax.ShapeDtypeStruct(shape, kind) for s...  402 us
  transfers between devices with their start and end apart: 1, of which 0 were waited for; matrix products, arithmetic and copies ran while one was open for 0% of the time, Pallas kernels for 11%

profile of v1, /device:TPU:0, one launch (start us, length us, event | category | flops | bytes accessed | tf_op | source)
XLA Modules:
  0.0 424.7 jit_solution(13543554064333588534)
XLA Ops:
  7.2 0.0 all-gather.3.cloned.1.call-start
  7.2 115.5 %opening.1 = (bf16[2,4,256,512]{3,2,1,0:T(8,128)(2,1)}, bf16[2,4,512,512]{3,2,1,0:T(8,128)(2,1)}, bf16[1024,1024]{1,0:T(8,128)(2,1)}, f32[2,8,1024]{2,1,0:T(8,12...) custom-call(bf16[2,1,256,1024]{3,2,1,0:T(8,128)(2,1)} %x.3, ...), custom_call_target="tpu_custom_call" | custom-call | flops 10000000000 | bytes 33554432 | tf_op jit(solution)/shard_map/opening/pallas_call | solution.py:1309
  122.8 0.0 all-gather.3.cloned.1.call-update
  122.8 47.2 %mixer_forward.1 = (bf16[1024,1024]{1,0:T(8,128)(2,1)}, bf16[1024,768]{1,0:T(8,128)(2,1)}, bf16[1024,768]{1,0:T(8,128)(2,1)}, bf16[1024,256]{1,0:T(8,128)(2,1)},...) custom-call(f32[256,1024]{1,0:T(8,128)} %get-tuple-element.86.x.out0, ...), custom_call_target="tpu_custom_call" | custom-call | flops 10000000000 | bytes 33554432 | tf_op jit(solution)/shard_map/mixer_forward/pallas_call | solution.py:1309
  170.0 0.0 all-gather.3.cloned.1.call-done
  170.0 58.4 %ff_turn.1 = (bf16[4,512,512]{2,1,0:T(8,128)(2,1)}, f32[256,1024]{1,0:T(8,128)}, f32[256,1024]{1,0:T(8,128)}, f32[2,1024]{1,0:T(2,128)}) custom-call(bf16[2,1,256,1024]{3,2,1,0:T(8,128)(2,1)} %cotangent.1, f32[256,1024]{1,0:T(8,128)} %get-tuple-element.91.x, f32[2,8,1024]{2,1,0:T(8,128)} %get-tuple-element.87.refs_0_.par_all, s32[1,2]{1,0:T(1,128)} %bitcast.45, ...), custom_call_target="tpu_custom_call" | custom-call | flops 30000001024 | bytes 33554432 | tf_op jit(solution)/shard_map/ff_turn/pallas_call | solution.py:1309
  228.4 48.9 %mixer_backward.2 = (bf16[4,256,512]{2,1,0:T(8,128)(2,1)}, f32[160,256]{1,0:T(8,128)}, f32[256,1024]{1,0:T(8,128)}, bf16[512,512]{1,0:T(8,128)(2,1)}) custom-call(f32[256,1024]{1,0:T(8,128)} %get-tuple-element.94.grad, f32[256,1024]{1,0:T(8,128)} %get-tuple-element.86.x.out0, f32[2,8,1024]{2,1,0:T(8,128)} %get-tuple-element.87.refs_0_.par_all, ...), custom_call_target="tpu_custom_call" | custom-call | flops 20000000000 | bytes 33554432 | tf_op jit(solution)/shard_map/mixer_backward/pallas_call | solution.py:1309
  277.3 43.6 %ff_backward.1 = (bf16[4,512,512]{2,1,0:T(8,128)(2,1)}, f32[256,1024]{1,0:T(8,128)}, f32[2,1024]{1,0:T(2,128)}, bf16[256,512]{1,0:T(8,128)(2,1)}, f32[2,256,1024]{2,1,0:T(8,128)}) custom-call(f32[256,1024]{1,0:T(8,128)} %get-tuple-element.108.grad.grad1, f32[256,1024]{1,0:T(8,128)} %get-tuple-element.109.middle, ...), custom_call_target="tpu_custom_call" | custom-call | flops 20000000000 | bytes 33554432 | tf_op jit(solution)/shard_map/ff_backward/pallas_call | solution.py:1309
  321.0 49.6 %mixer_backward.3 = (bf16[4,256,512]{2,1,0:T(8,128)(2,1)}, f32[160,256]{1,0:T(8,128)}, f32[256,1024]{1,0:T(8,128)}, bf16[512,512]{1,0:T(8,128)(2,1)}) custom-call(f32[256,1024]{1,0:T(8,128)} %get-tuple-element.117.grad, bf16[2,1,256,1024]{3,2,1,0:T(8,128)(2,1)} %x.3, f32[2,8,1024]{2,1,0:T(8,128)} %get-tuple-element.87.refs_0_.par_all, ...), custom_call_target="tpu_custom_call" | custom-call | flops 20000000000 | bytes 33554432 | tf_op jit(solution)/shard_map/mixer_backward/pallas_call | solution.py:1309
  370.5 39.3 %finish.1 = (f32[2,256,1024]{2,1,0:T(8,128)}, bf16[2,4,64,384]{3,2,1,0:T(8,128)(2,1)}, bf16[2,256,128]{2,1,0:T(8,128)(2,1)}, bf16[2,4,64,512]{3,2,1,0:T(8,128)(2...) custom-call(f32[160,256]{1,0:T(8,128)} %get-tuple-element.133.vec0, f32[160,256]{1,0:T(8,128)} %get-tuple-element.134.vec1, ...), custom_call_target="tpu_custom_call" | custom-call | flops 1000000000 | bytes 33554432 | tf_op jit(solution)/shard_map/finish/pallas_call | solution.py:1309
  409.8 7.6 %unpack.1 = (f32[2,256,1024]{2,1,0:T(8,128)}, f32[2,256,1024]{2,1,0:T(8,128)}, f32[64,3072]{1,0:T(8,128)}, f32[64,1024]{1,0:T(8,128)}, f32[64,4096]{1,0:T(8,128)...) custom-call(f32[2,256,1024]{2,1,0:T(8,128)} %get-tuple-element.116.b, ...), custom_call_target="tpu_custom_call" | custom-call | tf_op jit(solution)/shard_map/unpack/pallas_call | solution.py:2006
Async XLA Ops:
  7.2 162.8 %all-gather.3.cloned.1.call-start = ((), (), s32[]{:S(2)}) async-start(), calls=%async_computation | async-start | bytes 4718592 | tf_op jit(solution)/shard_map/all_gather | solution.py:2300
Sparse Core Ops, SparseCore 0:
  122.9 46.2 all-gather.2

commit v2 on v1

--- a/solution.py
+++ b/solution.py
@@ -618,8 +618,8 @@
         network_outs, next_outs, refs = refs[:5], refs[5:10], refs[10:]
         second_out, value_out, slope_out, result_out, *refs = refs
         (
-            *refs, waves1, waves2, steep1, steep2, taps_low, pack, ff_all, late, next_pack, core_sems,
-            plane_sems, ff_core_sems, ff_plane_sems, next_core_sems, next_plane_sems, late_sems,
+            *refs, waves1, waves2, steep1, steep2, taps_low, raw_out, ff_all, late, next_pack, core_sems,
+            plane_sems, out_core_sems, out_plane_sems, ff_core_sems, ff_plane_sems, next_core_sems, next_plane_sems, late_sems,
             pack_sems, mixer_parts, ff_parts, par_all, small_all, stage_in, stage_out, stage_up,
             in_sems, out_sems, up_sems, down_sems, par_sems, small_sems,
             second, ff_send, ff_recv, second_sems, ff_sems, network_sems,
@@ -660,14 +660,16 @@
             section, me, targets, (stage_in, stage_out, stage_up, w_down), (mixer_parts, ff_parts),
             (par_all, small_all), (in_sems, out_sems, up_sems, down_sems, par_sems, small_sems),
         )
-        mixer_pack = ChipGather(mixer_parts.at[0], pack, plane_sems, core_sems)
+        in_cols, out_cols = pl.ds(0, half), pl.ds(half, raw_out.shape[3])
+        in_pack = ChipGather(mixer_parts.at[0, :, in_cols], win, plane_sems, core_sems)
+        out_pack = ChipGather(mixer_parts.at[0, :, out_cols], raw_out, out_plane_sems, out_core_sems)
         ff_pack = ChipGather(ff_parts.at[0], ff_all, ff_plane_sems, ff_core_sems)
         for sems, item in ((par_sems, par_all), (small_sems, small_all)):
             block = item.at[1 - section]
             remote_to(block, block, sems, 0, other_core()).wait_recv()
         norm_into(gather, me * count, x, par[0:1, :], par[1:2, :])
         shuffle_wait_mixer(section, me, targets, mixer_parts, stage_in, in_sems, out_sems)
-        mixer_pack.begin(pack_sems.at[0])
+        in_pack.begin(pack_sems.at[0])
         sends += gather_begin(gather, gather_sems, me, peers, count)
         masked_into(late, me * count, cotangent, lengths)
     else:
@@ -690,18 +692,19 @@
     sends += gather_forward(gather, gather_sems, peers, count)
     if gathers:
         sends += gather_begin(late, late_sems, me, peers, count)
-        mixer_pack.forward()
-        shuffle_wait_ff(section, me, targets, ff_parts, stage_up, up_sems, down_sems)
-        ff_pack.begin(pack_sems.at[1])
+        in_pack.forward()
+        out_pack.begin(pack_sems.at[13])
         network_rows(small, embedding, network, taps_low, 1)
         tables[0].wait()
         lax.fori_loop(0, 2 * length // tile_rows, filter_spectrum, 0)
         network_stores = fetch(list(zip((filt, *network), network_outs)), network_sems)
-        mixer_pack.end()
-        weights = fetch(weight_pairs_mixer(pack, win, wout), load_sems, 2)
+        out_pack.forward()
+        shuffle_wait_ff(section, me, targets, ff_parts, stage_up, up_sems, down_sems)
+        ff_pack.begin(pack_sems.at[1])
+        in_pack.end()
         stores += fetch(
             [
-                (pack, pack_out),
+                (win, pack_out.at[:, :, :, in_cols]),
                 (par_all, par_out),
                 (small_all, small_out),
                 (ff_parts.at[1], ff_part_out),
@@ -711,7 +714,8 @@
         )
     else:
         tables[0].wait()
-    weights[0].wait()
+    if not gathers:
+        weights[0].wait()
     for slot in (None, 0, 1, 2):
         source = me if slot is None else peers[slot]
         if slot is not None:
@@ -764,8 +768,26 @@
 
     lax.fori_loop(0, length // tile_rows, spectrum, 0)
     tables[1].wait()
-    for load in weights[1:]:
-        load.wait()
+    if gathers:
+        out_pack.end()
+        cols = raw_out.shape[3]
+        weights = fetch(
+            [
+                (
+                    raw_out.at[:, :, pl.ds(q * wout.shape[2], wout.shape[2]), :],
+                    wout.at[:, :, :, pl.ds(q * cols, cols)],
+                )
+                for q in range(4)
+            ],
+            load_sems,
+            3,
+        )
+        stores += fetch([(raw_out, pack_out.at[:, :, :, out_cols])], pack_sems, 14)
+        for load in weights:
+            load.wait()
+    else:
+        for load in weights[1:]:
+            load.wait()
     for slot in (2, 0, 1, None):
         target = me if slot is None else peers[slot]
         rows = rows_of(target, count)
@@ -828,7 +850,7 @@
         stores += fetch([(next_pack, next_pack_out)], pack_sems, 12)
         reduce_wait(ff_send, ff_recv, ff_sems, peers)
         add_parts(result_out, ff_recv, middle_out, me * count, lengths)
-        sends += mixer_pack.sends + ff_pack.sends + next_mixer.sends
+        sends += in_pack.sends + out_pack.sends + ff_pack.sends + next_mixer.sends
         stores += network_stores
     for copy in sends:
         copy.wait_send()
@@ -838,9 +860,9 @@
 
 def ff_turn_kernel(
     s, cotangent, x, par_all, lengths, pack, late_hbm,
-    half_out, result_out, middle_grad_out, sums_out,
-    gather, late, wup, wdown, value, pre, wgrad, other, send, recv, send_back, recv_back,
-    gather_sems, reduce_sems, load_sems, store_sems, back_sems, core_sems,
+    half_out, parts_out, result_out, middle_grad_out, sums_out,
+    gather, late, wup, wdown, value, pre, wgrad, other, send, send_back, recv_back,
+    gather_sems, back_sems, load_sems, store_sems, core_sems,
 ):
     par = par_all.at[s]
     grad = cotangent.at[lax.axis_index("section"), 0]
@@ -912,8 +934,7 @@
             else:
                 send[slot, :, cols] = out.astype(low)
     sends += reduce_pass(send_back, recv_back, back_sems, peers)
-    for slot in (2, 0, 1):
-        sends += reduce_send(slot, send, recv, reduce_sems, peers)
+    stores = fetch([(send, parts_out)], store_sems, 1)
 
     def weights(i, carry):
         cols = pl.ds(pl.multiple_of(i * rows_up, rows_up), rows_up)
@@ -930,13 +951,10 @@
     swapped = [(wgrad, other)]
     swaps = swap_begin(swapped, core_sems)
     sends += swaps
-    sends += reduce_pass(send, recv, reduce_sems, peers)
     reduce_wait(send_back, recv_back, back_sems, peers)
     norm_back_parts(middle_grad_out, recv_back, grad, x, par[2:3, :], sums_out)
     swap_end(swaps, swapped)
-    stores = fetch([(wgrad.at[lax.axis_index("section")], half_out)], store_sems)
-    reduce_wait(send, recv, reduce_sems, peers)
-    add_parts(result_out, recv, x, me * count, lengths)
+    stores += fetch([(wgrad.at[lax.axis_index("section")], half_out)], store_sems)
     for copy in sends:
         copy.wait_send()
     for store in stores:
@@ -944,11 +962,10 @@
 
 
 def ff_backward_kernel(
-    s, grad, middle, par_all, lengths, pack, second_hbm, value_hbm, slope_hbm, earlier, out0, out1,
-    half_out, middle_grad_out, sums_out, summed, block_outputs,
+    s, grad, middle, par_all, lengths, pack, second_hbm, value_hbm, slope_hbm, earlier,
+    half_out, middle_grad_out, sums_out, summed,
     gather, wup, wdown, second, value, slope, pre, wgrad, other, send, recv, gather_sems,
-    reduce_sems, load_sems, store_sems, mine, arrived, plane_sems, sum_sems, core_sems, layer_sems,
-    keep_sems,
+    reduce_sems, load_sems, store_sems, mine, arrived, plane_sems, sum_sems, core_sems,
 ):
     par = par_all.at[s]
     me = lax.axis_index("seq")
@@ -973,7 +990,6 @@
     sends = gather_begin(gather, gather_sems, me, peers, count)
     plane_sum = PlaneSum(earlier, mine, arrived, plane_sems, sum_sems)
     plane_sum.begin()
-    by_layer(True, ((out0, out1, block_outputs),), layer_sems, keep_sems)
     for load in loads[:3]:
         load.wait()
     for slot, part in ((None, None), *HALF_ORDER):
@@ -1034,7 +1050,6 @@
     sends += plane_sum.sends
     reduce_wait(send, recv, reduce_sems, peers)
     norm_back_parts(middle_grad_out, recv, grad, middle, par[2:3, :], sums_out)
-    by_layer(False, ((out0, out1, block_outputs),), layer_sems, keep_sems)
     for copy in sends:
         copy.wait_send()
     for store in stores:
@@ -1057,13 +1072,13 @@
     return jnp.dot(a, b, preferred_element_type=f32, precision=precise)
 
 
-def by_layer(begin, triples, layer_sems, keep_sems):
+def by_layer(begin, triples, layer_sems, keep_sems, base=0):
     section = lax.axis_index("section")
     for index in range(2):
 
         @pl.when(section == index)
         def _():
-            for at, (first, second, target) in enumerate(triples):
+            for at, (first, second, target) in enumerate(triples, base):
                 kept, sent = (first, second) if index == 0 else (second, first)
                 slot = target.at[index]
                 copies = (
@@ -1393,13 +1408,13 @@
         more = [
             *[vm((length, knots), f32)] * 4,
             vm((length, chans), low),
-            vm(pack_shape, low),
+            vm((*pack_shape[:3], half // 4), low),
             vm(ff_shape, low),
             vm((length, width), low),
             vm(pack_shape, low),
-            *[dma((2, 4)), dma((2, 3))] * 3,
+            *[dma((2, 4)), dma((2, 3))] * 4,
             dma((2, 6)),
-            dma((13,)),
+            dma((15,)),
             vm((2, *pack_shape[2:]), low),
             vm((2, *ff_shape[2:]), low),
             vm((2, 8, width), f32),
@@ -1468,20 +1483,26 @@
         4,
         (cotangent, x, par, lengths, pack, late),
         range(3),
-        [(pack.shape[1:], low), ((count, width), f32), ((count, width), f32), ((2, width), f32)],
-        (1, 2, 3),
+        [
+            (pack.shape[1:], low),
+            ((3, count, width), low),
+            ((count, width), f32),
+            ((count, width), f32),
+            ((2, width), f32),
+        ],
+        (2, 3, 4),
         [vm((length, width), low)] * 2
         + [vm((2, dp_count, rows // 2, half), low)] * 2
         + [vm((length, units), low)] * 2
         + [vm(pack.shape, low), vm(pack.shape[1:], low)]
-        + exchange_scratch(count, width) * 2
-        + semaphores(3, 1)
-        + [pltpu.SemaphoreType.DMA((2, 10)), pltpu.SemaphoreType.DMA((2, 1))],
+        + [vm((3, count, width), low)] * 3
+        + semaphores(3, 2)
+        + [pltpu.SemaphoreType.DMA((2, 1))],
         3 * 10**10,
     )
 
 
-def ff_backward(s, grad, middle, par, lengths, pack, second, value, slope, earlier, results):
+def ff_backward(s, grad, middle, par, lengths, pack, second, value, slope, earlier):
     count, width = grad.shape
     _, dp_count, rows, half = pack.shape
     length, units = value.shape
@@ -1491,14 +1512,13 @@
         partial(ff_backward_kernel, s),
         "ff_backward",
         5,
-        (grad, middle, par, lengths, pack, second, value, slope, earlier, *results),
-        (0, 1, 2, 9, 10),
+        (grad, middle, par, lengths, pack, second, value, slope, earlier),
+        range(3),
         [
             (pack.shape[1:], low),
             ((count, width), f32),
             ((2, width), f32),
             (earlier.shape[1:], low),
-            ((2, count, width), f32),
         ],
         (1, 2, 3),
         [vm((length, width), low)]
@@ -1509,8 +1529,7 @@
         + exchange_scratch(count, width)
         + semaphores(5, 1)
         + plane_sum_scratch(earlier)
-        + [pltpu.SemaphoreType.DMA((2, 1))]
-        + exchange_semaphores(1),
+        + [pltpu.SemaphoreType.DMA((2, 1))],
         2 * 10**10,
     )
 
@@ -1689,11 +1708,12 @@
 
 
 def finish_kernel(
-    vec0, vec1, mixer0, mixer1, ff0, ff1, grad0, grad1,
-    input_grads, got_in, got_out, got_up, got_down, vec_out,
+    vec0, vec1, mixer0, mixer1, ff0, ff1, grad0, grad1, parts, own_part, x, out0, lengths,
+    block_outputs, input_grads, got_in, got_out, got_up, got_down, vec_out,
     mine0, arrived0, plane_sems0, sum_sems0, mine1, arrived1, plane_sems1, sum_sems1,
     vec_other, vec_sum, vec_arrived, vec_all, stage_mixer, stage_ff, own_sems, load_sems,
     layer_sems, keep_sems, vec_core_sems, vec_sum_sems, vec_plane_sems, vec_seq_sems, in_sems, out_sems, up_sems, down_sems,
+    send, recv, out1, reduce_sems,
 ):
     section = lax.axis_index("section")
     me = lax.axis_index("seq")
@@ -1771,10 +1791,19 @@
     for plane_sum in plane_sums:
         plane_sum.begin()
     loads = fetch(
-        [(ff0, stage_ff.at[0]), (ff1, stage_ff.at[1]), (mixer1, stage_mixer.at[1])], load_sems
+        [
+            (parts, send),
+            (ff0, stage_ff.at[0]),
+            (ff1, stage_ff.at[1]),
+            (mixer1, stage_mixer.at[1]),
+        ],
+        load_sems,
     )
     by_layer(True, ((grad0, grad1, input_grads),), layer_sems, keep_sems)
-    for load in loads:
+    loads[0].wait()
+    for slot in (2, 0, 1):
+        sends += reduce_send(slot, send, recv, reduce_sems, peers)
+    for load in loads[1:]:
         load.wait()
     ups = []
     for e, (t, seq, device) in enumerate(targets):
@@ -1821,6 +1850,7 @@
     sends += moves
     for plane_sum in plane_sums:
         plane_sum.forward()
+    sends += reduce_pass(send, recv, reduce_sems, peers)
     for slot, plane in enumerate(planes):
         block = vec_all.at[me, rows_of(plane, chunk)]
         remote_to(block, block, vec_plane_sems, slot, {"dp": plane}).wait_recv()
@@ -1832,6 +1862,15 @@
         copy.start()
     sends += moves
 
+    reduce_wait(send, recv, reduce_sems, peers)
+    start = me * own_part.shape[0]
+
+    def add(rows):
+        total = own_part[rows, :] + recv[0, rows, :].astype(f32) + recv[1, rows, :].astype(f32)
+        out1[rows, :] = x[rows, :] + valid_rows(lengths, start + rows.start, 32) * total
+
+    by_rows(own_part.shape[0], 32, add)
+    by_layer(True, ((out0, out1, block_outputs),), layer_sems, keep_sems, 1)
     for at, plane_sum in enumerate(plane_sums):
         plane_sum.end(stage_mixer.at[0, :, chunks[at]])
         sends += plane_sum.sends
@@ -1861,6 +1900,7 @@
     downs[0].wait_recv()
     out_columns.wait_recv()
     by_layer(False, ((grad0, grad1, input_grads),), layer_sems, keep_sems)
+    by_layer(False, ((out0, out1, block_outputs),), layer_sems, keep_sems, 1)
     for copy in sends:
         copy.wait_send()
     for keep in keeps:
@@ -1941,7 +1981,7 @@
     )
 
 
-def finish(vec0, vec1, mixer0, mixer1, ff0, ff1, grad0, grad1):
+def finish(vec0, vec1, mixer0, mixer1, ff0, ff1, grad0, grad1, parts, own_part, x, out0, lengths):
     count, width = grad0.shape
     dp_count, rows, half = mixer0.shape
     depth = rows // 4
@@ -1954,9 +1994,10 @@
         finish_kernel,
         "finish",
         10,
-        (vec0, vec1, mixer0, mixer1, ff0, ff1, grad0, grad1),
-        (0, 1, 6, 7),
+        (vec0, vec1, mixer0, mixer1, ff0, ff1, grad0, grad1, parts, own_part, x, out0, lengths),
+        (0, 1, 6, 7, 9, 10, 11),
         [
+            ((2, count, width), f32),
             ((2, count, width), f32),
             ((2, 4, depth, half_in), low),
             ((2, rows, half_in // 3), low),
@@ -1975,8 +2016,8 @@
             vm((2, *mixer1.shape), low),
             vm((2, *ff1.shape), low),
             dma((5,)),
-            dma((3,)),
-            *exchange_semaphores(1),
+            dma((4,)),
+            *exchange_semaphores(2),
             dma((2, 1)),
             dma((2, 3)),
             dma((2, 3)),
@@ -1985,6 +2026,9 @@
             dma((2, 1)),
             dma((2, 7)),
             dma((2, 1)),
+            *exchange_scratch(count, width),
+            vm((count, width), f32),
+            dma((2, 10)),
         ],
         10**9,
     )
@@ -2323,7 +2367,7 @@
         None,
     )
     first_kept, second_kept = [*first_kept, *first_filter], [*second_kept, *second_filter]
-    second_ff, second_out, middle_grad, late = ff_turn(
+    second_ff, result_parts, own_part, middle_grad, late = ff_turn(
         1, cotangent, second_middle, par, lengths, second_ff_pack, cotangent_low
     )
 
@@ -2335,16 +2379,15 @@
     second_mixer, second_vec, second_grad, second_ff = mixer_back(
         1, middle_grad, first_out, late, second_mixer_pack, second_kept, second_ff
     )
-    first_ff, middle_grad, late, second_mixer, block_outputs = ff_backward(
-        0, second_grad, first_middle, par, lengths, first_ff_pack, *first_saved, second_mixer,
-        (first_out, second_out),
+    first_ff, middle_grad, late, second_mixer = ff_backward(
+        0, second_grad, first_middle, par, lengths, first_ff_pack, *first_saved, second_mixer
     )
     first_mixer, first_vec, first_grad, first_ff = mixer_back(
         0, middle_grad, tokens, late, first_mixer_pack, first_kept, first_ff
     )
-    input_grads, *got = finish(
+    block_outputs, input_grads, *got = finish(
         first_vec, second_vec, first_mixer, second_mixer, first_ff, second_ff, first_grad,
-        second_grad,
+        second_grad, result_parts, own_part, second_middle, first_out, lengths,
     )
     (
         block_outputs, input_grads, sum_in, sum_out, sum_up, sum_down, sum_gain, sum_bias, sum_taps,

time: 432 us -> 431 us (level)
  no operation moved by 1% of the time
where the time goes in v2:
time: 431 us; the launch traced here: 423 us
  Pallas kernels  409 us (95%)
  between operations  14.6 us (3%)
    pallas_call x7, Pallas kernels, run_kernel(): pl.pallas_call(kernel, out_shape=[jax.ShapeDtypeStruct(shape, kind) for s...  401 us
  transfers between devices with their start and end apart: 1, of which 0 were waited for; matrix products, arithmetic and copies ran while one was open for 0% of the time, Pallas kernels for 11%

profile of v2, /device:TPU:0, one launch (start us, length us, event | category | flops | bytes accessed | tf_op | source)
XLA Modules:
  0.0 423.4 jit_solution(9916157490746084670)
XLA Ops:
  7.2 0.0 all-gather.3.cloned.1.call-start
  7.2 115.8 %opening.1 = (bf16[2,4,256,512]{3,2,1,0:T(8,128)(2,1)}, bf16[2,4,512,512]{3,2,1,0:T(8,128)(2,1)}, bf16[1024,1024]{1,0:T(8,128)(2,1)}, f32[2,8,1024]{2,1,0:T(8,12...) custom-call(bf16[2,1,256,1024]{3,2,1,0:T(8,128)(2,1)} %x.3, ...), custom_call_target="tpu_custom_call" | custom-call | flops 10000000000 | bytes 33554432 | tf_op jit(solution)/shard_map/opening/pallas_call | solution.py:1324
  123.0 0.0 all-gather.3.cloned.1.call-update
  123.0 47.3 %mixer_forward.1 = (bf16[1024,1024]{1,0:T(8,128)(2,1)}, bf16[1024,768]{1,0:T(8,128)(2,1)}, bf16[1024,768]{1,0:T(8,128)(2,1)}, bf16[1024,256]{1,0:T(8,128)(2,1)},...) custom-call(f32[256,1024]{1,0:T(8,128)} %get-tuple-element.87.x.out0, ...), custom_call_target="tpu_custom_call" | custom-call | flops 10000000000 | bytes 33554432 | tf_op jit(solution)/shard_map/mixer_forward/pallas_call | solution.py:1324
  170.4 0.0 all-gather.3.cloned.1.call-done
  170.4 46.3 %ff_turn.1 = (bf16[4,512,512]{2,1,0:T(8,128)(2,1)}, bf16[3,256,1024]{2,1,0:T(8,128)(2,1)}, f32[256,1024]{1,0:T(8,128)}, f32[256,1024]{1,0:T(8,128)}, f32[2,1024]{1,0:T(2,128)}) custom-call(bf16[2,1,256,1024]{3,2,1,0:T(8,128)(2,1)} %cotangent.1, f32[256,1024]{1,0:T(8,128)} %get-tuple-element.92.x, f32[2,8,1024]{2,1,0:T(8,128)} %get-tuple-element.88.refs_0_.par_all, ...), custom_call_target="tpu_custom_call" | custom-call | flops 30000001024 | bytes 33554432 | tf_op jit(solution)/shard_map/ff_turn/pallas_call | solution.py:1324
  216.7 53.9 %mixer_backward.2 = (bf16[4,256,512]{2,1,0:T(8,128)(2,1)}, f32[160,256]{1,0:T(8,128)}, f32[256,1024]{1,0:T(8,128)}, bf16[512,512]{1,0:T(8,128)(2,1)}) custom-call(f32[256,1024]{1,0:T(8,128)} %get-tuple-element.95.grad, f32[256,1024]{1,0:T(8,128)} %get-tuple-element.87.x.out0, f32[2,8,1024]{2,1,0:T(8,128)} %get-tuple-element.88.refs_0_.par_all, ...), custom_call_target="tpu_custom_call" | custom-call | flops 20000000000 | bytes 33554432 | tf_op jit(solution)/shard_map/mixer_backward/pallas_call | solution.py:1324
  270.6 42.3 %ff_backward.1 = (bf16[4,512,512]{2,1,0:T(8,128)(2,1)}, f32[256,1024]{1,0:T(8,128)}, f32[2,1024]{1,0:T(2,128)}, bf16[256,512]{1,0:T(8,128)(2,1)}) custom-call(f32[256,1024]{1,0:T(8,128)} %get-tuple-element.109.grad.grad1, f32[256,1024]{1,0:T(8,128)} %get-tuple-element.110.middle, f32[2,8,1024]{2,1,0:T(8,128)} %get-tuple-element.88.refs_0_.par_all, ...), custom_call_target="tpu_custom_call" | custom-call | flops 20000000000 | bytes 33554432 | tf_op jit(solution)/shard_map/ff_backward/pallas_call | solution.py:1324
  312.9 50.2 %mixer_backward.3 = (bf16[4,256,512]{2,1,0:T(8,128)(2,1)}, f32[160,256]{1,0:T(8,128)}, f32[256,1024]{1,0:T(8,128)}, bf16[512,512]{1,0:T(8,128)(2,1)}) custom-call(f32[256,1024]{1,0:T(8,128)} %get-tuple-element.116.grad, bf16[2,1,256,1024]{3,2,1,0:T(8,128)(2,1)} %x.3, f32[2,8,1024]{2,1,0:T(8,128)} %get-tuple-element.88.refs_0_.par_all, ...), custom_call_target="tpu_custom_call" | custom-call | flops 20000000000 | bytes 33554432 | tf_op jit(solution)/shard_map/mixer_backward/pallas_call | solution.py:1324
  363.2 45.4 %finish.1 = (f32[2,256,1024]{2,1,0:T(8,128)}, f32[2,256,1024]{2,1,0:T(8,128)}, bf16[2,4,64,384]{3,2,1,0:T(8,128)(2,1)}, bf16[2,256,128]{2,1,0:T(8,128)(2,1)}, bf...) custom-call(f32[160,256]{1,0:T(8,128)} %get-tuple-element.132.vec0, ...), custom_call_target="tpu_custom_call" | custom-call | flops 1000000000 | bytes 33554432 | tf_op jit(solution)/shard_map/finish/pallas_call | solution.py:1324
  408.6 7.6 %unpack.1 = (f32[2,256,1024]{2,1,0:T(8,128)}, f32[2,256,1024]{2,1,0:T(8,128)}, f32[64,3072]{1,0:T(8,128)}, f32[64,1024]{1,0:T(8,128)}, f32[64,4096]{1,0:T(8,128)...) custom-call(f32[2,256,1024]{2,1,0:T(8,128)} %get-tuple-element.141.b, ...), custom_call_target="tpu_custom_call" | custom-call | tf_op jit(solution)/shard_map/unpack/pallas_call | solution.py:2050
Async XLA Ops:
  7.2 163.2 %all-gather.3.cloned.1.call-start = ((), (), s32[]{:S(2)}) async-start(), calls=%async_computation | async-start | bytes 4718592 | tf_op jit(solution)/shard_map/all_gather | solution.py:2344
Sparse Core Ops, SparseCore 0:
  123.2 46.2 all-gather.2

commit v3 on v2

--- a/solution.py
+++ b/solution.py
@@ -716,21 +716,10 @@
         tables[0].wait()
     if not gathers:
         weights[0].wait()
-    for slot in (None, 0, 1, 2):
-        source = me if slot is None else peers[slot]
-        if slot is not None:
-            gather_wait(gather, gather_sems, slot, peers, count)
-        block = gather[rows_of(source, count), :]
-        for h in range(2):
-            proj[pl.ds(pl.multiple_of(source * count + 8, 8), count), h * half : (h + 1) * half] = mm(
-                block, win[h].reshape(width, half)
-            )
-    if gathers:
-        sends += gather_forward(late, late_sems, peers, count)
-    step = 128
-
-    def short_conv(i, carry):
-        start = pl.multiple_of(i * step, step)
+    step = 64
+    steps = count // step
+
+    def short_conv(start):
         for g in range(3):
             cols = slice(g * chans, (g + 1) * chans)
             tile = proj[pl.ds(start, step + 8), cols]
@@ -744,9 +733,32 @@
         first = streams[pl.ds(start, step), 0:chans].astype(f32)
         third = streams[pl.ds(start, step), 2 * chans : 3 * chans].astype(f32)
         prod[pl.ds(start, step), :] = (first * third * valid_rows(lengths, start, step)).astype(low)
+
+    def within(source):
+        def body(i, carry):
+            short_conv(pl.multiple_of(source * count + i * step, step))
+            return carry
+
+        lax.fori_loop(1, steps, body, 0)
+
+    for slot in (None, 0, 1, 2):
+        source = me if slot is None else peers[slot]
+        if slot is not None:
+            gather_wait(gather, gather_sems, slot, peers, count)
+        block = gather[rows_of(source, count), :]
+        for h in range(2):
+            proj[pl.ds(pl.multiple_of(source * count + 8, 8), count), h * half : (h + 1) * half] = mm(
+                block, win[h].reshape(width, half)
+            )
+        within(source)
+    if gathers:
+        sends += gather_forward(late, late_sems, peers, count)
+
+    def seams(i, carry):
+        short_conv(pl.multiple_of(i * count, step))
         return carry
 
-    lax.fori_loop(0, length // step, short_conv, 0)
+    lax.fori_loop(0, length // count, seams, 0)
     stores += fetch(
         [(gather, normed_out), (proj_low, proj_out), (streams, stream_out), (prod, prod_out)],
         store_sems,
@@ -951,10 +963,10 @@
     swapped = [(wgrad, other)]
     swaps = swap_begin(swapped, core_sems)
     sends += swaps
+    swap_end(swaps, swapped)
+    stores += fetch([(wgrad.at[lax.axis_index("section")], half_out)], store_sems)
     reduce_wait(send_back, recv_back, back_sems, peers)
     norm_back_parts(middle_grad_out, recv_back, grad, x, par[2:3, :], sums_out)
-    swap_end(swaps, swapped)
-    stores += fetch([(wgrad.at[lax.axis_index("section")], half_out)], store_sems)
     for copy in sends:
         copy.wait_send()
     for store in stores:
@@ -1800,9 +1812,6 @@
         load_sems,
     )
     by_layer(True, ((grad0, grad1, input_grads),), layer_sems, keep_sems)
-    loads[0].wait()
-    for slot in (2, 0, 1):
-        sends += reduce_send(slot, send, recv, reduce_sems, peers)
     for load in loads[1:]:
         load.wait()
     ups = []
@@ -1823,6 +1832,9 @@
     sends += ups + downs
     send_layer(1, 0)
     send_layer(1, 1)
+    loads[0].wait()
+    for slot in (2, 0, 1):
+        sends += reduce_send(slot, send, recv, reduce_sems, peers)
     keeps = fetch(
         [
             (stage_ff.at[section, rows_of(me, depth), :], got_up.at[section, me]),
@@ -1862,20 +1874,20 @@
         copy.start()
     sends += moves
 
-    reduce_wait(send, recv, reduce_sems, peers)
-    start = me * own_part.shape[0]
-
-    def add(rows):
-        total = own_part[rows, :] + recv[0, rows, :].astype(f32) + recv[1, rows, :].astype(f32)
-        out1[rows, :] = x[rows, :] + valid_rows(lengths, start + rows.start, 32) * total
-
-    by_rows(own_part.shape[0], 32, add)
-    by_layer(True, ((out0, out1, block_outputs),), layer_sems, keep_sems, 1)
     for at, plane_sum in enumerate(plane_sums):
         plane_sum.end(stage_mixer.at[0, :, chunks[at]])
         sends += plane_sum.sends
         send_layer(0, at)
     sends += [columns(e, at) for e in range(7) for at in range(2)] + [out_columns]
+    reduce_wait(send, recv, reduce_sems, peers)
+    start = me * own_part.shape[0]
+
+    def add(rows):
+        total = own_part[rows, :] + recv[0, rows, :].astype(f32) + recv[1, rows, :].astype(f32)
+        out1[rows, :] = x[rows, :] + valid_rows(lengths, start + rows.start, 32) * total
+
+    by_rows(own_part.shape[0], 32, add)
+    by_layer(True, ((out0, out1, block_outputs),), layer_sems, keep_sems, 1)
     keeps += fetch(
         [
             (

time: 431 us -> 433 us (level)
  transfers between devices with their start and end apart: 1 -> 1, of which waited for: 0 -> 1; matrix products, arithmetic and copies ran while one was open for 0% -> 0% of each run, Pallas kernels for 11% -> 11%
where the time goes in v3:
time: 433 us; the launch traced here: 425 us
  Pallas kernels  410 us (95%)
  between operations  14.6 us (3%)
    pallas_call x7, Pallas kernels, run_kernel(): pl.pallas_call(kernel, out_shape=[jax.ShapeDtypeStruct(shape, kind) for s...  403 us
  transfers between devices with their start and end apart: 1, of which 1 were waited for; matrix products, arithmetic and copies ran while one was open for 0% of the time, Pallas kernels for 11%

profile of v3, /device:TPU:0, one launch (start us, length us, event | category | flops | bytes accessed | tf_op | source)
XLA Modules:
  0.0 425.0 jit_solution(1131271200745607963)
XLA Ops:
  7.2 0.0 all-gather.3.cloned.1.call-start
  7.2 115.8 %opening.1 = (bf16[2,4,256,512]{3,2,1,0:T(8,128)(2,1)}, bf16[2,4,512,512]{3,2,1,0:T(8,128)(2,1)}, bf16[1024,1024]{1,0:T(8,128)(2,1)}, f32[2,8,1024]{2,1,0:T(8,12...) custom-call(bf16[2,1,256,1024]{3,2,1,0:T(8,128)(2,1)} %x.3, ...), custom_call_target="tpu_custom_call" | custom-call | flops 10000000000 | bytes 33554432 | tf_op jit(solution)/shard_map/opening/pallas_call | solution.py:1336
  123.0 0.0 all-gather.3.cloned.1.call-update
  123.0 46.1 %mixer_forward.1 = (bf16[1024,1024]{1,0:T(8,128)(2,1)}, bf16[1024,768]{1,0:T(8,128)(2,1)}, bf16[1024,768]{1,0:T(8,128)(2,1)}, bf16[1024,256]{1,0:T(8,128)(2,1)},...) custom-call(f32[256,1024]{1,0:T(8,128)} %get-tuple-element.87.x.out0, ...), custom_call_target="tpu_custom_call" | custom-call | flops 10000000000 | bytes 33554432 | tf_op jit(solution)/shard_map/mixer_forward/pallas_call | solution.py:1336
  169.1 0.3 all-gather.3.cloned.1.call-done
  169.4 47.6 %ff_turn.1 = (bf16[4,512,512]{2,1,0:T(8,128)(2,1)}, bf16[3,256,1024]{2,1,0:T(8,128)(2,1)}, f32[256,1024]{1,0:T(8,128)}, f32[256,1024]{1,0:T(8,128)}, f32[2,1024]{1,0:T(2,128)}) custom-call(bf16[2,1,256,1024]{3,2,1,0:T(8,128)(2,1)} %cotangent.1, f32[256,1024]{1,0:T(8,128)} %get-tuple-element.92.x, f32[2,8,1024]{2,1,0:T(8,128)} %get-tuple-element.88.refs_0_.par_all, ...), custom_call_target="tpu_custom_call" | custom-call | flops 30000001024 | bytes 33554432 | tf_op jit(solution)/shard_map/ff_turn/pallas_call | solution.py:1336
  217.0 53.8 %mixer_backward.2 = (bf16[4,256,512]{2,1,0:T(8,128)(2,1)}, f32[160,256]{1,0:T(8,128)}, f32[256,1024]{1,0:T(8,128)}, bf16[512,512]{1,0:T(8,128)(2,1)}) custom-call(f32[256,1024]{1,0:T(8,128)} %get-tuple-element.95.grad, f32[256,1024]{1,0:T(8,128)} %get-tuple-element.87.x.out0, f32[2,8,1024]{2,1,0:T(8,128)} %get-tuple-element.88.refs_0_.par_all, ...), custom_call_target="tpu_custom_call" | custom-call | flops 20000000000 | bytes 33554432 | tf_op jit(solution)/shard_map/mixer_backward/pallas_call | solution.py:1336
  270.8 42.8 %ff_backward.1 = (bf16[4,512,512]{2,1,0:T(8,128)(2,1)}, f32[256,1024]{1,0:T(8,128)}, f32[2,1024]{1,0:T(2,128)}, bf16[256,512]{1,0:T(8,128)(2,1)}) custom-call(f32[256,1024]{1,0:T(8,128)} %get-tuple-element.109.grad.grad1, f32[256,1024]{1,0:T(8,128)} %get-tuple-element.110.middle, f32[2,8,1024]{2,1,0:T(8,128)} %get-tuple-element.88.refs_0_.par_all, ...), custom_call_target="tpu_custom_call" | custom-call | flops 20000000000 | bytes 33554432 | tf_op jit(solution)/shard_map/ff_backward/pallas_call | solution.py:1336
  313.5 51.3 %mixer_backward.3 = (bf16[4,256,512]{2,1,0:T(8,128)(2,1)}, f32[160,256]{1,0:T(8,128)}, f32[256,1024]{1,0:T(8,128)}, bf16[512,512]{1,0:T(8,128)(2,1)}) custom-call(f32[256,1024]{1,0:T(8,128)} %get-tuple-element.116.grad, bf16[2,1,256,1024]{3,2,1,0:T(8,128)(2,1)} %x.3, f32[2,8,1024]{2,1,0:T(8,128)} %get-tuple-element.88.refs_0_.par_all, ...), custom_call_target="tpu_custom_call" | custom-call | flops 20000000000 | bytes 33554432 | tf_op jit(solution)/shard_map/mixer_backward/pallas_call | solution.py:1336
  364.8 45.3 %finish.1 = (f32[2,256,1024]{2,1,0:T(8,128)}, f32[2,256,1024]{2,1,0:T(8,128)}, bf16[2,4,64,384]{3,2,1,0:T(8,128)(2,1)}, bf16[2,256,128]{2,1,0:T(8,128)(2,1)}, bf...) custom-call(f32[160,256]{1,0:T(8,128)} %get-tuple-element.132.vec0, ...), custom_call_target="tpu_custom_call" | custom-call | flops 1000000000 | bytes 33554432 | tf_op jit(solution)/shard_map/finish/pallas_call | solution.py:1336
  410.1 7.6 %unpack.1 = (f32[2,256,1024]{2,1,0:T(8,128)}, f32[2,256,1024]{2,1,0:T(8,128)}, f32[64,3072]{1,0:T(8,128)}, f32[64,1024]{1,0:T(8,128)}, f32[64,4096]{1,0:T(8,128)...) custom-call(f32[2,256,1024]{2,1,0:T(8,128)} %get-tuple-element.141.b, ...), custom_call_target="tpu_custom_call" | custom-call | tf_op jit(solution)/shard_map/unpack/pallas_call | solution.py:2062
Async XLA Ops:
  7.2 162.2 %all-gather.3.cloned.1.call-start = ((), (), s32[]{:S(2)}) async-start(), calls=%async_computation | async-start | bytes 4718592 | tf_op jit(solution)/shard_map/all_gather | solution.py:2356
Sparse Core Ops, SparseCore 0:
  123.2 46.2 all-gather.2

commit v4 on v3

--- a/solution.py
+++ b/solution.py
@@ -872,8 +872,8 @@
 
 def ff_turn_kernel(
     s, cotangent, x, par_all, lengths, pack, late_hbm,
-    half_out, parts_out, result_out, middle_grad_out, sums_out,
-    gather, late, wup, wdown, value, pre, wgrad, other, send, send_back, recv_back,
+    half_out, value_out, middle_grad_out, sums_out,
+    gather, late, wup, wdown, value, pre, wgrad, other, send_back, recv_back,
     gather_sems, back_sems, load_sems, store_sems, core_sems,
 ):
     par = par_all.at[s]
@@ -936,17 +936,8 @@
             sends += gather_forward(gather, gather_sems, peers, count)
         else:
             sends += reduce_send_half(slot, part, send_back, recv_back, back_sems, peers)
-    for slot in (2, 0, 1, None):
-        rows = rows_of(me if slot is None else peers[slot], count)
-        for h in range(2):
-            cols = slice(h * width // 2, (h + 1) * width // 2)
-            out = mm(value[rows, :], wdown[h].reshape(2 * half, width // 2))
-            if slot is None:
-                result_out[:, cols] = out
-            else:
-                send[slot, :, cols] = out.astype(low)
     sends += reduce_pass(send_back, recv_back, back_sems, peers)
-    stores = fetch([(send, parts_out)], store_sems, 1)
+    stores = fetch([(value, value_out)], store_sems, 1)
 
     def weights(i, carry):
         cols = pl.ds(pl.multiple_of(i * rows_up, rows_up), rows_up)
@@ -963,10 +954,10 @@
     swapped = [(wgrad, other)]
     swaps = swap_begin(swapped, core_sems)
     sends += swaps
+    reduce_wait(send_back, recv_back, back_sems, peers)
+    norm_back_parts(middle_grad_out, recv_back, grad, x, par[2:3, :], sums_out)
     swap_end(swaps, swapped)
     stores += fetch([(wgrad.at[lax.axis_index("section")], half_out)], store_sems)
-    reduce_wait(send_back, recv_back, back_sems, peers)
-    norm_back_parts(middle_grad_out, recv_back, grad, x, par[2:3, :], sums_out)
     for copy in sends:
         copy.wait_send()
     for store in stores:
@@ -1497,17 +1488,16 @@
         range(3),
         [
             (pack.shape[1:], low),
-            ((3, count, width), low),
-            ((count, width), f32),
+            ((length, units), low),
             ((count, width), f32),
             ((2, width), f32),
         ],
-        (2, 3, 4),
+        (2, 3),
         [vm((length, width), low)] * 2
         + [vm((2, dp_count, rows // 2, half), low)] * 2
         + [vm((length, units), low)] * 2
         + [vm(pack.shape, low), vm(pack.shape[1:], low)]
-        + [vm((3, count, width), low)] * 3
+        + exchange_scratch(count, width)
         + semaphores(3, 2)
         + [pltpu.SemaphoreType.DMA((2, 1))],
         3 * 10**10,
@@ -1720,12 +1710,12 @@
 
 
 def finish_kernel(
-    vec0, vec1, mixer0, mixer1, ff0, ff1, grad0, grad1, parts, own_part, x, out0, lengths,
+    vec0, vec1, mixer0, mixer1, ff0, ff1, grad0, grad1, value_hbm, pack_hbm, x, out0, lengths,
     block_outputs, input_grads, got_in, got_out, got_up, got_down, vec_out,
     mine0, arrived0, plane_sems0, sum_sems0, mine1, arrived1, plane_sems1, sum_sems1,
     vec_other, vec_sum, vec_arrived, vec_all, stage_mixer, stage_ff, own_sems, load_sems,
     layer_sems, keep_sems, vec_core_sems, vec_sum_sems, vec_plane_sems, vec_seq_sems, in_sems, out_sems, up_sems, down_sems,
-    send, recv, out1, reduce_sems,
+    send, recv, out1, reduce_sems, value, wdown, early_sems,
 ):
     section = lax.axis_index("section")
     me = lax.axis_index("seq")
@@ -1735,6 +1725,10 @@
     depth, half_in = got_in.shape[2:]
     targets = shuffle_targets(section, me, peers)
     greeted = greet([device for _, _, device in targets] + [{"dp": plane} for plane in planes])
+    inner = wdown.shape[2]
+    early = fetch(
+        [(value_hbm, value), (pack_hbm.at[:, :, pl.ds(inner, inner)], wdown)], early_sems
+    )
     middle = mixer0.shape[2] // 2
     chunks = (pl.ds(0, middle), pl.ds(middle, middle))
     in_cols = (pl.ds(0, middle), pl.ds(middle, half_in - middle))
@@ -1772,6 +1766,22 @@
             remote_to(vec, vec_other, vec_core_sems, 0, other_core()).start()
 
     sends = []
+    count, width = x.shape
+
+    def result_part(slot):
+        rows = rows_of(me if slot is None else peers[slot], count)
+        for h in range(2):
+            cols = slice(h * width // 2, (h + 1) * width // 2)
+            out = mm(value[rows, :], wdown[h].reshape(4 * inner, width // 2))
+            if slot is None:
+                out1[:, cols] = out
+            else:
+                send[slot, :, cols] = out.astype(low)
+        return [] if slot is None else reduce_send(slot, send, recv, reduce_sems, peers)
+
+    for load in early:
+        load.wait()
+    sends += result_part(2)
     vec_swap = remote_to(vec_other, vec_other, vec_core_sems, 0, other_core())
     vec_swap.wait_recv()
     sends.append(vec_swap)
@@ -1784,8 +1794,7 @@
     def _():
         vec_sum[...] = vec1[...] + vec_other[...]
 
-    count = 4
-    chunk = vec_sum.shape[0] // count
+    chunk = vec_sum.shape[0] // 4
     moves = [
         remote_to(
             vec_sum.at[rows_of(plane, chunk)], vec_arrived.at[slot], vec_sum_sems, slot,
@@ -1804,7 +1813,6 @@
         plane_sum.begin()
     loads = fetch(
         [
-            (parts, send),
             (ff0, stage_ff.at[0]),
             (ff1, stage_ff.at[1]),
             (mixer1, stage_mixer.at[1]),
@@ -1812,7 +1820,9 @@
         load_sems,
     )
     by_layer(True, ((grad0, grad1, input_grads),), layer_sems, keep_sems)
-    for load in loads[1:]:
+    sends += result_part(0)
+    sends += result_part(1)
+    for load in loads:
         load.wait()
     ups = []
     for e, (t, seq, device) in enumerate(targets):
@@ -1832,9 +1842,6 @@
     sends += ups + downs
     send_layer(1, 0)
     send_layer(1, 1)
-    loads[0].wait()
-    for slot in (2, 0, 1):
-        sends += reduce_send(slot, send, recv, reduce_sems, peers)
     keeps = fetch(
         [
             (stage_ff.at[section, rows_of(me, depth), :], got_up.at[section, me]),
@@ -1843,6 +1850,7 @@
         own_sems,
     )
 
+    result_part(None)
     for copy in moves:
         copy.wait_recv()
     own_chunk = rows_of(here, chunk)
@@ -1880,13 +1888,7 @@
         send_layer(0, at)
     sends += [columns(e, at) for e in range(7) for at in range(2)] + [out_columns]
     reduce_wait(send, recv, reduce_sems, peers)
-    start = me * own_part.shape[0]
-
-    def add(rows):
-        total = own_part[rows, :] + recv[0, rows, :].astype(f32) + recv[1, rows, :].astype(f32)
-        out1[rows, :] = x[rows, :] + valid_rows(lengths, start + rows.start, 32) * total
-
-    by_rows(own_part.shape[0], 32, add)
+    add_parts(out1, recv, x, me * count, lengths)
     by_layer(True, ((out0, out1, block_outputs),), layer_sems, keep_sems, 1)
     keeps += fetch(
         [
@@ -1993,7 +1995,9 @@
     )
 
 
-def finish(vec0, vec1, mixer0, mixer1, ff0, ff1, grad0, grad1, parts, own_part, x, out0, lengths):
+def finish(
+    vec0, vec1, mixer0, mixer1, ff0, ff1, grad0, grad1, value, pack, x, out0, lengths
+):
     count, width = grad0.shape
     dp_count, rows, half = mixer0.shape
     depth = rows // 4
@@ -2006,8 +2010,8 @@
         finish_kernel,
         "finish",
         10,
-        (vec0, vec1, mixer0, mixer1, ff0, ff1, grad0, grad1, parts, own_part, x, out0, lengths),
-        (0, 1, 6, 7, 9, 10, 11),
+        (vec0, vec1, mixer0, mixer1, ff0, ff1, grad0, grad1, value, pack, x, out0, lengths),
+        (0, 1, 6, 7, 10, 11),
         [
             ((2, count, width), f32),
             ((2, count, width), f32),
@@ -2028,7 +2032,7 @@
             vm((2, *mixer1.shape), low),
             vm((2, *ff1.shape), low),
             dma((5,)),
-            dma((4,)),
+            dma((3,)),
             *exchange_semaphores(2),
             dma((2, 1)),
             dma((2, 3)),
@@ -2041,6 +2045,9 @@
             *exchange_scratch(count, width),
             vm((count, width), f32),
             dma((2, 10)),
+            vm(value.shape, low),
+            vm((*pack.shape[:2], pack.shape[2] // 2, pack.shape[3]), low),
+            dma((2,)),
         ],
         10**9,
     )
@@ -2379,7 +2386,7 @@
         None,
     )
     first_kept, second_kept = [*first_kept, *first_filter], [*second_kept, *second_filter]
-    second_ff, result_parts, own_part, middle_grad, late = ff_turn(
+    second_ff, second_value, middle_grad, late = ff_turn(
         1, cotangent, second_middle, par, lengths, second_ff_pack, cotangent_low
     )
 
@@ -2399,7 +2406,7 @@
     )
     block_outputs, input_grads, *got = finish(
         first_vec, second_vec, first_mixer, second_mixer, first_ff, second_ff, first_grad,
-        second_grad, result_parts, own_part, second_middle, first_out, lengths,
+        second_grad, second_value, second_ff_pack, second_middle, first_out, lengths,
     )
     (
         block_outputs, input_grads, sum_in, sum_out, sum_up, sum_down, sum_gain, sum_bias, sum_taps,

time: 433 us -> 428 us (0.988)
    pallas_call x7, Pallas kernels: 403 us -> 398 us  [run_kernel(): pl.pallas_call(kernel, out_shape=[jax.ShapeDtypeStruct(shape, kind) for s...]
where the time goes in v4:
time: 428 us; the launch traced here: 420 us
  Pallas kernels  406 us (95%)
  between operations  14.6 us (3%)
    pallas_call x7, Pallas kernels, run_kernel(): pl.pallas_call(kernel, out_shape=[jax.ShapeDtypeStruct(shape, kind) for s...  398 us
  transfers between devices with their start and end apart: 1, of which 1 were waited for; matrix products, arithmetic and copies ran while one was open for 0% of the time, Pallas kernels for 11%

profile of v4, /device:TPU:0, one launch (start us, length us, event | category | flops | bytes accessed | tf_op | source)
XLA Modules:
  0.0 420.4 jit_solution(155935623930860298)
XLA Ops:
  7.2 0.0 all-gather.3.cloned.1.call-start
  7.2 115.8 %opening.1 = (bf16[2,4,256,512]{3,2,1,0:T(8,128)(2,1)}, bf16[2,4,512,512]{3,2,1,0:T(8,128)(2,1)}, bf16[1024,1024]{1,0:T(8,128)(2,1)}, f32[2,8,1024]{2,1,0:T(8,12...) custom-call(bf16[2,1,256,1024]{3,2,1,0:T(8,128)(2,1)} %x.3, ...), custom_call_target="tpu_custom_call" | custom-call | flops 10000000000 | bytes 33554432 | tf_op jit(solution)/shard_map/opening/pallas_call | solution.py:1327
  123.0 0.0 all-gather.3.cloned.1.call-update
  123.1 46.1 %mixer_forward.1 = (bf16[1024,1024]{1,0:T(8,128)(2,1)}, bf16[1024,768]{1,0:T(8,128)(2,1)}, bf16[1024,768]{1,0:T(8,128)(2,1)}, bf16[1024,256]{1,0:T(8,128)(2,1)},...) custom-call(f32[256,1024]{1,0:T(8,128)} %get-tuple-element.86.x.out0, ...), custom_call_target="tpu_custom_call" | custom-call | flops 10000000000 | bytes 33554432 | tf_op jit(solution)/shard_map/mixer_forward/pallas_call | solution.py:1327
  169.2 0.2 all-gather.3.cloned.1.call-done
  169.4 47.1 %ff_turn.1 = (bf16[4,512,512]{2,1,0:T(8,128)(2,1)}, bf16[1024,1024]{1,0:T(8,128)(2,1)}, f32[256,1024]{1,0:T(8,128)}, f32[2,1024]{1,0:T(2,128)}) custom-call(bf16[2,1,256,1024]{3,2,1,0:T(8,128)(2,1)} %cotangent.1, f32[256,1024]{1,0:T(8,128)} %get-tuple-element.91.x, f32[2,8,1024]{2,1,0:T(8,128)} %get-tuple-element.87.refs_0_.par_all, s32[1,2]{1,0:T(1,128)} %bitcast.28, ...), custom_call_target="tpu_custom_call" | custom-call | flops 30000001024 | bytes 33554432 | tf_op jit(solution)/shard_map/ff_turn/pallas_call | solution.py:1327
  216.6 52.7 %mixer_backward.2 = (bf16[4,256,512]{2,1,0:T(8,128)(2,1)}, f32[160,256]{1,0:T(8,128)}, f32[256,1024]{1,0:T(8,128)}, bf16[512,512]{1,0:T(8,128)(2,1)}) custom-call(f32[256,1024]{1,0:T(8,128)} %get-tuple-element.94.grad, f32[256,1024]{1,0:T(8,128)} %get-tuple-element.86.x.out0, f32[2,8,1024]{2,1,0:T(8,128)} %get-tuple-element.87.refs_0_.par_all, ...), custom_call_target="tpu_custom_call" | custom-call | flops 20000000000 | bytes 33554432 | tf_op jit(solution)/shard_map/mixer_backward/pallas_call | solution.py:1327
  269.3 43.1 %ff_backward.1 = (bf16[4,512,512]{2,1,0:T(8,128)(2,1)}, f32[256,1024]{1,0:T(8,128)}, f32[2,1024]{1,0:T(2,128)}, bf16[256,512]{1,0:T(8,128)(2,1)}) custom-call(f32[256,1024]{1,0:T(8,128)} %get-tuple-element.108.grad.grad1, f32[256,1024]{1,0:T(8,128)} %get-tuple-element.109.middle, f32[2,8,1024]{2,1,0:T(8,128)} %get-tuple-element.87.refs_0_.par_all, ...), custom_call_target="tpu_custom_call" | custom-call | flops 20000000000 | bytes 33554432 | tf_op jit(solution)/shard_map/ff_backward/pallas_call | solution.py:1327
  312.4 51.0 %mixer_backward.3 = (bf16[4,256,512]{2,1,0:T(8,128)(2,1)}, f32[160,256]{1,0:T(8,128)}, f32[256,1024]{1,0:T(8,128)}, bf16[512,512]{1,0:T(8,128)(2,1)}) custom-call(f32[256,1024]{1,0:T(8,128)} %get-tuple-element.115.grad, bf16[2,1,256,1024]{3,2,1,0:T(8,128)(2,1)} %x.3, f32[2,8,1024]{2,1,0:T(8,128)} %get-tuple-element.87.refs_0_.par_all, ...), custom_call_target="tpu_custom_call" | custom-call | flops 20000000000 | bytes 33554432 | tf_op jit(solution)/shard_map/mixer_backward/pallas_call | solution.py:1327
  363.4 42.1 %finish.1 = (f32[2,256,1024]{2,1,0:T(8,128)}, f32[2,256,1024]{2,1,0:T(8,128)}, bf16[2,4,64,384]{3,2,1,0:T(8,128)(2,1)}, bf16[2,256,128]{2,1,0:T(8,128)(2,1)}, bf...) custom-call(f32[160,256]{1,0:T(8,128)} %get-tuple-element.131.vec0, ...), custom_call_target="tpu_custom_call" | custom-call | flops 1000000000 | bytes 33554432 | tf_op jit(solution)/shard_map/finish/pallas_call | solution.py:1327
  405.5 7.6 %unpack.1 = (f32[2,256,1024]{2,1,0:T(8,128)}, f32[2,256,1024]{2,1,0:T(8,128)}, f32[64,3072]{1,0:T(8,128)}, f32[64,1024]{1,0:T(8,128)}, f32[64,4096]{1,0:T(8,128)...) custom-call(f32[2,256,1024]{2,1,0:T(8,128)} %get-tuple-element.139.b, ...), custom_call_target="tpu_custom_call" | custom-call | tf_op jit(solution)/shard_map/unpack/pallas_call | solution.py:2069
Async XLA Ops:
  7.2 162.3 %all-gather.3.cloned.1.call-start = ((), (), s32[]{:S(2)}) async-start(), calls=%async_computation | async-start | bytes 4718592 | tf_op jit(solution)/shard_map/all_gather | solution.py:2363
Sparse Core Ops, SparseCore 0:
  123.2 46.2 all-gather.2

commit v5 on v4

--- a/solution.py
+++ b/solution.py
@@ -936,7 +936,6 @@
             sends += gather_forward(gather, gather_sems, peers, count)
         else:
             sends += reduce_send_half(slot, part, send_back, recv_back, back_sems, peers)
-    sends += reduce_pass(send_back, recv_back, back_sems, peers)
     stores = fetch([(value, value_out)], store_sems, 1)
 
     def weights(i, carry):
@@ -950,13 +949,20 @@
             ).astype(low)
         return carry
 
-    lax.fori_loop(0, width // rows_up, weights, 0)
-    swapped = [(wgrad, other)]
-    swaps = swap_begin(swapped, core_sems)
-    sends += swaps
+    middle = width // rows_up // 2
+    early, late_part = pl.ds(0, middle), pl.ds(middle, middle)
+    lax.fori_loop(0, middle, weights, 0)
+    swapped = [(wgrad.at[:, early], other.at[early])]
+    swaps = swap_begin(swapped, core_sems.at[0])
+    sends += reduce_pass(send_back, recv_back, back_sems, peers)
+    lax.fori_loop(middle, 2 * middle, weights, 0)
+    swapped_late = [(wgrad.at[:, late_part], other.at[late_part])]
+    swaps_late = swap_begin(swapped_late, core_sems.at[1])
+    sends += swaps + swaps_late
+    swap_end(swaps, swapped)
     reduce_wait(send_back, recv_back, back_sems, peers)
     norm_back_parts(middle_grad_out, recv_back, grad, x, par[2:3, :], sums_out)
-    swap_end(swaps, swapped)
+    swap_end(swaps_late, swapped_late)
     stores += fetch([(wgrad.at[lax.axis_index("section")], half_out)], store_sems)
     for copy in sends:
         copy.wait_send()
@@ -1042,15 +1048,21 @@
             ).astype(low)
         return carry
 
-    lax.fori_loop(0, width // up_rows, weights, 0)
-    swapped = [(wgrad, other)]
-    swaps = swap_begin(swapped, core_sems)
-    sends += swaps
+    half_blocks = width // up_rows // 2
+    early, late_part = pl.ds(0, half_blocks), pl.ds(half_blocks, half_blocks)
+    lax.fori_loop(0, half_blocks, weights, 0)
+    swapped = [(wgrad.at[:, early], other.at[early])]
+    swaps = swap_begin(swapped, core_sems.at[0])
     sends += reduce_pass(send, recv, reduce_sems, peers)
-    swap_end(swaps, swapped)
-    stores = fetch([(wgrad.at[lax.axis_index("section")], half_out)], store_sems)
+    lax.fori_loop(half_blocks, 2 * half_blocks, weights, 0)
+    swapped_late = [(wgrad.at[:, late_part], other.at[late_part])]
+    swaps_late = swap_begin(swapped_late, core_sems.at[1])
+    sends += swaps + swaps_late
     plane_sum.end(summed)
     sends += plane_sum.sends
+    swap_end(swaps, swapped)
+    swap_end(swaps_late, swapped_late)
+    stores = fetch([(wgrad.at[lax.axis_index("section")], half_out)], store_sems)
     reduce_wait(send, recv, reduce_sems, peers)
     norm_back_parts(middle_grad_out, recv, grad, middle, par[2:3, :], sums_out)
     for copy in sends:
@@ -1499,7 +1511,7 @@
         + [vm(pack.shape, low), vm(pack.shape[1:], low)]
         + exchange_scratch(count, width)
         + semaphores(3, 2)
-        + [pltpu.SemaphoreType.DMA((2, 1))],
+        + [pltpu.SemaphoreType.DMA((2, 2, 1))],
         3 * 10**10,
     )
 
@@ -1531,7 +1543,7 @@
         + exchange_scratch(count, width)
         + semaphores(5, 1)
         + plane_sum_scratch(earlier)
-        + [pltpu.SemaphoreType.DMA((2, 1))],
+        + [pltpu.SemaphoreType.DMA((2, 2, 1))],
         2 * 10**10,
     )
 

time: 428 us -> 424 us (level)
  no operation moved by 1% of the time
where the time goes in v5:
time: 424 us; the launch traced here: 416 us
  Pallas kernels  402 us (95%)
  between operations  14.3 us (3%)
    pallas_call x7, Pallas kernels, run_kernel(): pl.pallas_call(kernel, out_shape=[jax.ShapeDtypeStruct(shape, kind) for s...  394 us
  transfers between devices with their start and end apart: 1, of which 1 were waited for; matrix products, arithmetic and copies ran while one was open for 0% of the time, Pallas kernels for 11%

profile of v5, /device:TPU:0, one launch (start us, length us, event | category | flops | bytes accessed | tf_op | source)
XLA Modules:
  0.0 416.2 jit_solution(10274195142071594583)
XLA Ops:
  7.2 0.0 all-gather.3.cloned.1.call-start
  7.2 115.8 %opening.1 = (bf16[2,4,256,512]{3,2,1,0:T(8,128)(2,1)}, bf16[2,4,512,512]{3,2,1,0:T(8,128)(2,1)}, bf16[1024,1024]{1,0:T(8,128)(2,1)}, f32[2,8,1024]{2,1,0:T(8,12...) custom-call(bf16[2,1,256,1024]{3,2,1,0:T(8,128)(2,1)} %x.3, ...), custom_call_target="tpu_custom_call" | custom-call | flops 10000000000 | bytes 33554432 | tf_op jit(solution)/shard_map/opening/pallas_call | solution.py:1339
  123.0 0.0 all-gather.3.cloned.1.call-update
  123.1 46.1 %mixer_forward.1 = (bf16[1024,1024]{1,0:T(8,128)(2,1)}, bf16[1024,768]{1,0:T(8,128)(2,1)}, bf16[1024,768]{1,0:T(8,128)(2,1)}, bf16[1024,256]{1,0:T(8,128)(2,1)},...) custom-call(f32[256,1024]{1,0:T(8,128)} %get-tuple-element.86.x.out0, ...), custom_call_target="tpu_custom_call" | custom-call | flops 10000000000 | bytes 33554432 | tf_op jit(solution)/shard_map/mixer_forward/pallas_call | solution.py:1339
  169.2 0.2 all-gather.3.cloned.1.call-done
  169.4 45.6 %ff_turn.1 = (bf16[4,512,512]{2,1,0:T(8,128)(2,1)}, bf16[1024,1024]{1,0:T(8,128)(2,1)}, f32[256,1024]{1,0:T(8,128)}, f32[2,1024]{1,0:T(2,128)}) custom-call(bf16[2,1,256,1024]{3,2,1,0:T(8,128)(2,1)} %cotangent.1, f32[256,1024]{1,0:T(8,128)} %get-tuple-element.91.x, f32[2,8,1024]{2,1,0:T(8,128)} %get-tuple-element.87.refs_0_.par_all, s32[1,2]{1,0:T(1,128)} %bitcast.28, ...), custom_call_target="tpu_custom_call" | custom-call | flops 30000001024 | bytes 33554432 | tf_op jit(solution)/shard_map/ff_turn/pallas_call | solution.py:1339
  215.1 49.0 %mixer_backward.2 = (bf16[4,256,512]{2,1,0:T(8,128)(2,1)}, f32[160,256]{1,0:T(8,128)}, f32[256,1024]{1,0:T(8,128)}, bf16[512,512]{1,0:T(8,128)(2,1)}) custom-call(f32[256,1024]{1,0:T(8,128)} %get-tuple-element.94.grad, f32[256,1024]{1,0:T(8,128)} %get-tuple-element.86.x.out0, f32[2,8,1024]{2,1,0:T(8,128)} %get-tuple-element.87.refs_0_.par_all, ...), custom_call_target="tpu_custom_call" | custom-call | flops 20000000000 | bytes 33554432 | tf_op jit(solution)/shard_map/mixer_backward/pallas_call | solution.py:1339
  264.1 42.8 %ff_backward.1 = (bf16[4,512,512]{2,1,0:T(8,128)(2,1)}, f32[256,1024]{1,0:T(8,128)}, f32[2,1024]{1,0:T(2,128)}, bf16[256,512]{1,0:T(8,128)(2,1)}) custom-call(f32[256,1024]{1,0:T(8,128)} %get-tuple-element.108.grad.grad1, f32[256,1024]{1,0:T(8,128)} %get-tuple-element.109.middle, f32[2,8,1024]{2,1,0:T(8,128)} %get-tuple-element.87.refs_0_.par_all, ...), custom_call_target="tpu_custom_call" | custom-call | flops 20000000000 | bytes 33554432 | tf_op jit(solution)/shard_map/ff_backward/pallas_call | solution.py:1339
  306.9 51.8 %mixer_backward.3 = (bf16[4,256,512]{2,1,0:T(8,128)(2,1)}, f32[160,256]{1,0:T(8,128)}, f32[256,1024]{1,0:T(8,128)}, bf16[512,512]{1,0:T(8,128)(2,1)}) custom-call(f32[256,1024]{1,0:T(8,128)} %get-tuple-element.115.grad, bf16[2,1,256,1024]{3,2,1,0:T(8,128)(2,1)} %x.3, f32[2,8,1024]{2,1,0:T(8,128)} %get-tuple-element.87.refs_0_.par_all, ...), custom_call_target="tpu_custom_call" | custom-call | flops 20000000000 | bytes 33554432 | tf_op jit(solution)/shard_map/mixer_backward/pallas_call | solution.py:1339
  358.7 42.9 %finish.1 = (f32[2,256,1024]{2,1,0:T(8,128)}, f32[2,256,1024]{2,1,0:T(8,128)}, bf16[2,4,64,384]{3,2,1,0:T(8,128)(2,1)}, bf16[2,256,128]{2,1,0:T(8,128)(2,1)}, bf...) custom-call(f32[160,256]{1,0:T(8,128)} %get-tuple-element.131.vec0, ...), custom_call_target="tpu_custom_call" | custom-call | flops 1000000000 | bytes 33554432 | tf_op jit(solution)/shard_map/finish/pallas_call | solution.py:1339
  401.6 7.6 %unpack.1 = (f32[2,256,1024]{2,1,0:T(8,128)}, f32[2,256,1024]{2,1,0:T(8,128)}, f32[64,3072]{1,0:T(8,128)}, f32[64,1024]{1,0:T(8,128)}, f32[64,4096]{1,0:T(8,128)...) custom-call(f32[2,256,1024]{2,1,0:T(8,128)} %get-tuple-element.139.b, ...), custom_call_target="tpu_custom_call" | custom-call | tf_op jit(solution)/shard_map/unpack/pallas_call | solution.py:2081
Async XLA Ops:
  7.2 162.3 %all-gather.3.cloned.1.call-start = ((), (), s32[]{:S(2)}) async-start(), calls=%async_computation | async-start | bytes 4718592 | tf_op jit(solution)/shard_map/all_gather | solution.py:2375
Sparse Core Ops, SparseCore 0:
  123.2 46.2 all-gather.2

commit v6 on v5

--- a/solution.py
+++ b/solution.py
@@ -1262,6 +1262,7 @@
             )
         return carry
 
+    sends += reduce_pass(send, recv, reduce_sems, peers)
     lax.fori_loop(0, width // depth, weights, 0)
     for h in range(2):
         value = t_mm(gated[...], gather[:, h * width // 2 : (h + 1) * width // 2]).astype(low)
@@ -1269,7 +1270,6 @@
     swapped = [(wgrad_in, other_in), (wgrad_out_part, other_out)]
     swaps = swap_begin(swapped, core_sems)
     sends += swaps
-    sends += reduce_pass(send, recv, reduce_sems, peers)
     taps_sum[...] = jnp.zeros(taps_sum.shape, f32)
 
     def tap_sums(i, carry):

time: 424 us -> 427 us (level)
  no operation moved by 1% of the time
where the time goes in v6:
time: 427 us; the launch traced here: 419 us
  Pallas kernels  405 us (95%)
  between operations  14.3 us (3%)
    pallas_call x7, Pallas kernels, run_kernel(): pl.pallas_call(kernel, out_shape=[jax.ShapeDtypeStruct(shape, kind) for s...  397 us
  transfers between devices with their start and end apart: 1, of which 1 were waited for; matrix products, arithmetic and copies ran while one was open for 0% of the time, Pallas kernels for 11%

profile of v6, /device:TPU:0, one launch (start us, length us, event | category | flops | bytes accessed | tf_op | source)
XLA Modules:
  0.0 419.3 jit_solution(11043840250866538693)
XLA Ops:
  7.2 0.0 all-gather.3.cloned.1.call-start
  7.2 115.8 %opening.1 = (bf16[2,4,256,512]{3,2,1,0:T(8,128)(2,1)}, bf16[2,4,512,512]{3,2,1,0:T(8,128)(2,1)}, bf16[1024,1024]{1,0:T(8,128)(2,1)}, f32[2,8,1024]{2,1,0:T(8,12...) custom-call(bf16[2,1,256,1024]{3,2,1,0:T(8,128)(2,1)} %x.3, ...), custom_call_target="tpu_custom_call" | custom-call | flops 10000000000 | bytes 33554432 | tf_op jit(solution)/shard_map/opening/pallas_call | solution.py:1339
  123.0 0.0 all-gather.3.cloned.1.call-update
  123.1 46.1 %mixer_forward.1 = (bf16[1024,1024]{1,0:T(8,128)(2,1)}, bf16[1024,768]{1,0:T(8,128)(2,1)}, bf16[1024,768]{1,0:T(8,128)(2,1)}, bf16[1024,256]{1,0:T(8,128)(2,1)},...) custom-call(f32[256,1024]{1,0:T(8,128)} %get-tuple-element.86.x.out0, ...), custom_call_target="tpu_custom_call" | custom-call | flops 10000000000 | bytes 33554432 | tf_op jit(solution)/shard_map/mixer_forward/pallas_call | solution.py:1339
  169.2 0.2 all-gather.3.cloned.1.call-done
  169.4 45.6 %ff_turn.1 = (bf16[4,512,512]{2,1,0:T(8,128)(2,1)}, bf16[1024,1024]{1,0:T(8,128)(2,1)}, f32[256,1024]{1,0:T(8,128)}, f32[2,1024]{1,0:T(2,128)}) custom-call(bf16[2,1,256,1024]{3,2,1,0:T(8,128)(2,1)} %cotangent.1, f32[256,1024]{1,0:T(8,128)} %get-tuple-element.91.x, f32[2,8,1024]{2,1,0:T(8,128)} %get-tuple-element.87.refs_0_.par_all, s32[1,2]{1,0:T(1,128)} %bitcast.28, ...), custom_call_target="tpu_custom_call" | custom-call | flops 30000001024 | bytes 33554432 | tf_op jit(solution)/shard_map/ff_turn/pallas_call | solution.py:1339
  215.1 51.0 %mixer_backward.2 = (bf16[4,256,512]{2,1,0:T(8,128)(2,1)}, f32[160,256]{1,0:T(8,128)}, f32[256,1024]{1,0:T(8,128)}, bf16[512,512]{1,0:T(8,128)(2,1)}) custom-call(f32[256,1024]{1,0:T(8,128)} %get-tuple-element.94.grad, f32[256,1024]{1,0:T(8,128)} %get-tuple-element.86.x.out0, f32[2,8,1024]{2,1,0:T(8,128)} %get-tuple-element.87.refs_0_.par_all, ...), custom_call_target="tpu_custom_call" | custom-call | flops 20000000000 | bytes 33554432 | tf_op jit(solution)/shard_map/mixer_backward/pallas_call | solution.py:1339
  266.0 42.8 %ff_backward.1 = (bf16[4,512,512]{2,1,0:T(8,128)(2,1)}, f32[256,1024]{1,0:T(8,128)}, f32[2,1024]{1,0:T(2,128)}, bf16[256,512]{1,0:T(8,128)(2,1)}) custom-call(f32[256,1024]{1,0:T(8,128)} %get-tuple-element.108.grad.grad1, f32[256,1024]{1,0:T(8,128)} %get-tuple-element.109.middle, f32[2,8,1024]{2,1,0:T(8,128)} %get-tuple-element.87.refs_0_.par_all, ...), custom_call_target="tpu_custom_call" | custom-call | flops 20000000000 | bytes 33554432 | tf_op jit(solution)/shard_map/ff_backward/pallas_call | solution.py:1339
  308.8 53.3 %mixer_backward.3 = (bf16[4,256,512]{2,1,0:T(8,128)(2,1)}, f32[160,256]{1,0:T(8,128)}, f32[256,1024]{1,0:T(8,128)}, bf16[512,512]{1,0:T(8,128)(2,1)}) custom-call(f32[256,1024]{1,0:T(8,128)} %get-tuple-element.115.grad, bf16[2,1,256,1024]{3,2,1,0:T(8,128)(2,1)} %x.3, f32[2,8,1024]{2,1,0:T(8,128)} %get-tuple-element.87.refs_0_.par_all, ...), custom_call_target="tpu_custom_call" | custom-call | flops 20000000000 | bytes 33554432 | tf_op jit(solution)/shard_map/mixer_backward/pallas_call | solution.py:1339
  362.1 42.6 %finish.1 = (f32[2,256,1024]{2,1,0:T(8,128)}, f32[2,256,1024]{2,1,0:T(8,128)}, bf16[2,4,64,384]{3,2,1,0:T(8,128)(2,1)}, bf16[2,256,128]{2,1,0:T(8,128)(2,1)}, bf...) custom-call(f32[160,256]{1,0:T(8,128)} %get-tuple-element.131.vec0, ...), custom_call_target="tpu_custom_call" | custom-call | flops 1000000000 | bytes 33554432 | tf_op jit(solution)/shard_map/finish/pallas_call | solution.py:1339
  404.6 7.6 %unpack.1 = (f32[2,256,1024]{2,1,0:T(8,128)}, f32[2,256,1024]{2,1,0:T(8,128)}, f32[64,3072]{1,0:T(8,128)}, f32[64,1024]{1,0:T(8,128)}, f32[64,4096]{1,0:T(8,128)...) custom-call(f32[2,256,1024]{2,1,0:T(8,128)} %get-tuple-element.139.b, ...), custom_call_target="tpu_custom_call" | custom-call | tf_op jit(solution)/shard_map/unpack/pallas_call | solution.py:2081
Async XLA Ops:
  7.2 162.3 %all-gather.3.cloned.1.call-start = ((), (), s32[]{:S(2)}) async-start(), calls=%async_computation | async-start | bytes 4718592 | tf_op jit(solution)/shard_map/all_gather | solution.py:2375
Sparse Core Ops, SparseCore 0:
  123.2 46.2 all-gather.2
